TPU v7x, 512 devices: a whole 4x4x16 slice. The times are simulated.
512 devices in a mesh: dp: 32 (over x, z_lo), tensor: 16 (over z_hi, y, core).
Axes of the slice: x: 4, y: 4, z: 16 (z_hi: 2, z_lo: 8; z = z_hi * 8 + z_lo), core: 2. Of those that a mesh axis runs over, the one named last changes fastest.
Arguments:
- tokens: bfloat16 [64, 256, 6144], P('dp', None, 'tensor'), may hold values from -6 to 6
- mix_weight: int32 [64], P('dp'), may hold values from 0 to 256
- partner_offset: int32 [64], P('dp'), may hold values from 0 to 1
- ln_gain: float32 [6144], replicated, may hold values from 0.25 to 1.75
- qkv_weight: bfloat16 [3, 6144, 4096], P(None, 'dp', 'tensor'), may hold values from -0.05103104 to 0.05103104
- qk_gain: float32 [2, 4096], P(None, 'tensor'), may hold values from 0.6 to 5
Outputs:
- attended: bfloat16 [64, 256, 4096], P('dp', None, 'tensor')
All inputs are finite; a program needn't handle non-finite values.
Results may differ from a plain program's by a relative error of at most 0.012.
The roundings to bfloat16 on the way count: a program that leaves them out, or rounds other values in their place, can miss the bound.
Values may be sent and summed in bfloat16 or wider, within the bound.
No kernel may reach another device: no remote copies, remote signals or barrier semaphores. Data moves between devices by JAX's collectives and lax.ppermute only.
A program may use at most 64 MiB of HBM per device.

v0:
```python
import jax
import jax.numpy as jnp
from jax import lax
from jax.sharding import PartitionSpec as P

HEAD = 128


def passed_along(value, axis, by):
    count = lax.axis_size(axis)
    return lax.ppermute(value, axis, [(i, (i + by) % count) for i in range(count)])


def norm_last(values, eps):
    mean = jnp.mean(values, axis=-1, keepdims=True)
    centred = values - mean
    var = jnp.mean(centred * centred, axis=-1, keepdims=True)
    return centred / jnp.sqrt(var + eps)


def per_device(tokens, mix_weight, partner_offset, ln_gain, qkv_weight, qk_gain):
    images = tokens.shape[0]
    partner_block = passed_along(tokens, "dp", -1)
    local_index = (jnp.arange(images, dtype=jnp.int32) + partner_offset) % images
    partner = jnp.take(partner_block, local_index, axis=0)
    lam = mix_weight.astype(jnp.float32) / 256.0
    mixed = lam[:, None, None] * tokens.astype(jnp.float32) + (1.0 - lam)[
        :, None, None
    ] * partner.astype(jnp.float32)
    mixed = mixed.astype(jnp.bfloat16)
    mixed_all = lax.all_gather(mixed, "tensor", axis=2, tiled=True)
    normed = (norm_last(mixed_all.astype(jnp.float32), 1e-06) * ln_gain).astype(jnp.bfloat16)
    width_dev = qkv_weight.shape[2]
    patches = normed.shape[1]
    projected = jnp.einsum(
        "ipd,cde->cipe",
        normed,
        lax.all_gather(qkv_weight, "dp", axis=1, tiled=True),
        preferred_element_type=jnp.float32,
    )
    qkv = projected.astype(jnp.bfloat16)
    heads_dev = width_dev // HEAD
    query = qkv[0].astype(jnp.float32).reshape(images, patches, heads_dev, HEAD)
    keys = qkv[1].astype(jnp.float32).reshape(images, patches, heads_dev, HEAD)
    values = qkv[2].reshape(images, patches, heads_dev, HEAD)
    q_norm = (
        norm_last(query, 1e-06) * qk_gain[0].reshape(heads_dev, HEAD) * HEAD ** (-0.5)
    ).astype(jnp.bfloat16)
    k_norm = (norm_last(keys, 1e-06) * qk_gain[1].reshape(heads_dev, HEAD)).astype(jnp.bfloat16)
    scores = jnp.einsum("iphe,iqhe->ihpq", q_norm, k_norm, preferred_element_type=jnp.float32)
    probs = jax.nn.softmax(scores, axis=-1).astype(jnp.bfloat16)
    output = jnp.einsum("ihpq,iqhe->iphe", probs, values, preferred_element_type=jnp.float32)
    return output.astype(jnp.bfloat16).reshape(images, patches, width_dev)


def solution(mesh):
    placed = (
        P("dp", None, "tensor"),
        P("dp"),
        P("dp"),
        P(),
        P(None, "dp", "tensor"),
        P(None, "tensor"),
    )
    return jax.shard_map(
        per_device, mesh=mesh, in_specs=placed, out_specs=P("dp", None, "tensor"), check_vma=False
    )
```

profile of v0, /device:TPU:16, one launch (start us, length us, event | category | flops | bytes accessed | tf_op | source)
XLA Modules:
  0.0 465.7 jit_solution(2682046418120455660)
XLA Ops:
  6.5 0.0 copy-start.1
  6.5 0.0 all-gather.3.cloned.1.call-start
  6.5 15.5 %collective-permute-start = (bf16[2,256,384]{2,1,0:T(8,128)(2,1)}, bf16[2,256,384]{2,1,0:T(8,128)(2,1)S(1)}, u32[]{:S(2)}, u32[]{:S(2)}) collective-permute-start(bf16[2,256,384]{2,1,0:T(8,128)(2,1)} %param.6), channel_id=1, source_target_pairs={{0,496},{16,0},{32,16},{48,32},{64,48},{80,64},{96,80},{112,96},{1... | collective-permute-start | bytes 1179656 | tf_op jit(solution)/shard_map/ppermute | solution.py:11
  22.0 0.7 compare_and_fusion
  22.7 0.7 convert_multiply_fusion
  23.4 7.3 %collective-permute-done = bf16[2,256,384]{2,1,0:T(8,128)(2,1)S(1)} collective-permute-done((bf16[2,256,384]{2,1,0:T(8,128)(2,1)}, bf16[2,256,384]{2,1,0:T(8,128)(2,1)S(1)}, u32[]{:S(2)}, u32[]{:S(2)}) %collective-permute-start) | collective-permute-done | bytes 393248 | tf_op jit(solution)/shard_map/ppermute | solution.py:11
  30.7 0.6 gather_fusion
  31.3 2.0 add_convert_fusion
  33.3 0.0 all-gather.3.cloned.1.call-update
  33.4 0.0 all-gather.5.cloned.1.call-start
  33.4 0.7 all-gather.5.cloned.1.call-update
  34.1 0.8 fusion.37
  34.9 149.1 %all-gather.3.cloned.1.call-done = bf16[2,256,6144]{2,1,0:T(8,128)(2,1)} async-done(((bf16[2,256,384]{2,1,0:T(8,128)(2,1)}), bf16[2,256,6144]{2,1,0:T(8,128)(2,1)}) %all-gather.3.cloned.1.call-update) | async-done | bytes 6291472 | tf_op jit(solution)/shard_map/all_gather | solution.py:31
  184.0 0.0 copy-start
  184.0 3.8 convert_reduce_fusion
  187.8 0.7 copy-done
  188.6 1.8 fusion.3
  190.4 252.0 %all-gather.5.cloned.1.call-done = bf16[3,6144,256]{2,1,0:T(8,128)(2,1)} async-done(((bf16[3,192,256]{2,1,0:T(8,128)(2,1)}), bf16[3,6144,256]{2,1,0:T(8,128)(2,1)}) %all-gather.5.cloned.1.call-update) | async-done | bytes 9437200 | tf_op jit(solution)/shard_map/all_gather | solution.py:38
  442.4 0.0 copy-done.1
  442.4 12.8 %fusion.20 = bf16[3,2,256,256]{2,3,0,1:T(8,128)(2,1)S(1)} fusion(bf16[3,6144,256]{2,1,0:T(8,128)(2,1)} %all-gather.5.cloned.1.call-done, bf16[2,256,6144]{2,1,0:T(8,128)(2,1)} %all-gather.3.cloned.1.call-done, f32[6144]{0:T(1024)S(1)} %copy-done.1, f32[2,256]{1,0:T(2,128)S(1)} %add_sqrt_fusion.2, f32[2,256]{1,0:T(2,128)S(1)} %broadcast_multiply_fusion.2), kind=kOutput, calls=%fused_computation.18 | convolution fusion | flops 4847960064 | bytes 16543744 | tf_op jit(solution)/shard_map/ipd,cde->cipe/dot_general | solution.py:35
  455.2 0.1 fusion.36
  455.2 0.1 copy.7
  455.4 0.1 convert_reduce_fusion.2
  455.4 0.1 copy.8
  455.6 0.1 convert_reduce_fusion.1
  455.6 0.4 multiply_reduce_fusion.1
  456.0 0.4 multiply_reduce_fusion
  456.4 1.0 fusion.25
  457.4 0.2 fusion.38
  457.7 0.4 convolution_convert_fusion
  458.1 0.8 copy.10
  (6 shorter events, 0.0 us)
Async XLA Ops:
  6.5 435.8 %copy-start.1 = (f32[6144]{0:T(1024)S(1)}, f32[6144]{0:T(1024)}, u32[]{:S(2)}) copy-start(f32[6144]{0:T(1024)} %param.9) | copy-start | bytes 73732
  6.5 177.5 %all-gather.3.cloned.1.call-start = ((), (), s32[]{:S(2)}) async-start(), calls=%async_computation | async-start | bytes 6684672 | tf_op jit(solution)/shard_map/all_gather | solution.py:31
  6.5 24.1 %collective-permute-start = (bf16[2,256,384]{2,1,0:T(8,128)(2,1)}, bf16[2,256,384]{2,1,0:T(8,128)(2,1)S(1)}, u32[]{:S(2)}, u32[]{:S(2)}) collective-permute-start(bf16[2,256,384]{2,1,0:T(8,128)(2,1)} %param.6), channel_id=1, source_target_pairs={{0,496},{16,0},{32,16},{48,32},{64,48},{80,64},{96,80},{112,96},{1... | collective-permute-start | bytes 1179656 | tf_op jit(solution)/shard_map/ppermute | solution.py:11
  33.4 409.0 %all-gather.5.cloned.1.call-start = ((), (), s32[]{:S(2)}) async-start(), calls=%async_computation.1 | async-start | bytes 9732096 | tf_op jit(solution)/shard_map/all_gather | solution.py:38
  184.0 4.6 copy-start
Sparse Core Ops, SparseCore 0:
  33.5 150.4 all-gather.2
  186.1 256.2 all-gather.4
where the time goes:
time: 466 us
  waiting for transfers between devices  409 us (88%)
  starting transfers between devices  15.5 us (3%)
  matrix products  14.1 us (3%)
  between operations  13.5 us (3%)
  other arithmetic  10.1 us (2%)
    all_gather x1, waiting for transfers between devices, per_device(): lax.all_gather(qkv_weight, 'dp', axis=1, tiled=True)  252 us
    all_gather x1, waiting for transfers between devices, per_device(): mixed_all = lax.all_gather(mixed, 'tensor', axis=2, tiled=True)  149 us
    ppermute x1, starting transfers between devices, passed_along(): lax.ppermute(value, axis, [(i, (i + by) % count) for i in range(count)])  15.5 us
    dot_general x1, matrix products, per_device(): jnp.einsum('ipd,cde->cipe', normed, lax.all_gather(qkv_weight, 'dp', axis...  12.8 us
  transfers between devices with their start and end apart: 3, of which 3 were waited for; matrix products, arithmetic and copies ran while one was open for 2% of the time, Pallas kernels for 0%

commit v1 on v0

v1 whole, which is shorter than its diff:
```python
import jax
import jax.numpy as jnp
from jax import lax
from jax.sharding import Mesh, PartitionSpec as P

HEAD = 128
AXES = ("x", "zl", "zh", "y", "c")
SIZES = (4, 8, 2, 4, 2)


def move(value, target):
    pairs = []
    for source in range(512):
        c = source % 2
        y = source // 2 % 4
        zh = source // 8 % 2
        zl = source // 16 % 8
        x = source // 128
        goal = target(x, zl, zh, y, c)
        if goal is None:
            continue
        gx, gzl, gzh, gy, gc = goal
        pairs.append((source, (((gx % 4 * 8 + gzl) * 2 + gzh) * 4 + gy % 4) * 2 + gc))
    return lax.ppermute(value, AXES, pairs)


def along_x(value, by):
    return move(value, lambda x, zl, zh, y, c: (x + by, zl, zh, y, c))


def along_y(value, by):
    return move(value, lambda x, zl, zh, y, c: (x, zl, zh, y + by, c))


def along_z(value, by):
    def target(x, zl, zh, y, c):
        z = (zh * 8 + zl + by) % 16
        return x, z % 8, z // 8, y, c

    return move(value, target)


def other_core(value):
    return move(value, lambda x, zl, zh, y, c: (x, zl, zh, y, 1 - c))


def previous_images(value):
    def target(x, zl, zh, y, c):
        dp = (x * 8 + zl - 1) % 32
        return dp // 8, dp % 8, zh, y, c

    return move(value, target)


def norm_last(values, eps):
    mean = jnp.mean(values, axis=-1, keepdims=True)
    centred = values - mean
    var = jnp.mean(centred * centred, axis=-1, keepdims=True)
    return centred / jnp.sqrt(var + eps)


def ring_of_four(value, shift, axis):
    size = value.shape[axis] // 2
    low, high = lax.slice_in_dim(value, 0, size, axis=axis), lax.slice_in_dim(value, size, 2 * size, axis=axis)
    from_left = shift(value, 1)
    from_right = shift(value, -1)
    low = shift(lax.slice_in_dim(from_left, 0, size, axis=axis), 1)
    high = shift(lax.slice_in_dim(from_right, size, 2 * size, axis=axis), -1)
    opposite = jnp.concatenate([low, high], axis=axis)
    return value, from_right, opposite, from_left


def gather_tokens(mixed):
    ahead = along_z(along_z(mixed[0], 4), 4)
    behind = along_z(along_z(mixed[1], -4), -4)
    other = jnp.stack([ahead, behind])
    zh, y, c = lax.axis_index("zh"), lax.axis_index("y"), lax.axis_index("c")
    both = jnp.where(zh == 0, jnp.stack([mixed, other]), jnp.stack([other, mixed]))
    column = jnp.stack(ring_of_four(both, along_y, 1))
    column = jnp.take(column, (jnp.arange(4) - y) % 4, axis=0)
    across = other_core(column)
    cores = jnp.where(c == 0, jnp.stack([column, across]), jnp.stack([across, column]))
    return cores.transpose(3, 4, 2, 1, 0, 5).reshape(2, 256, 6144)


def per_device(tokens, mix_weight, partner_offset, ln_gain, qkv_weight, qk_gain):
    images = tokens.shape[0]
    quarter = lax.all_gather(qkv_weight, "zl", axis=1, tiled=True)
    partner_block = previous_images(tokens)
    local_index = (jnp.arange(images, dtype=jnp.int32) + partner_offset) % images
    partner = jnp.take(partner_block, local_index, axis=0)
    lam = mix_weight.astype(jnp.float32) / 256.0
    mixed = lam[:, None, None] * tokens.astype(jnp.float32) + (1.0 - lam)[
        :, None, None
    ] * partner.astype(jnp.float32)
    mixed = mixed.astype(jnp.bfloat16)
    mixed_all = gather_tokens(mixed)
    normed = (norm_last(mixed_all.astype(jnp.float32), 1e-06) * ln_gain).astype(jnp.bfloat16)
    width_dev = qkv_weight.shape[2]
    patches = normed.shape[1]
    x = lax.axis_index("x")
    projected = 0.0
    for step, weight in enumerate(ring_of_four(quarter, along_x, 1)):
        rows = lax.dynamic_slice_in_dim(normed, (x + step) % 4 * 1536, 1536, axis=2)
        projected = projected + jnp.einsum(
            "ipd,cde->cipe", rows, weight, preferred_element_type=jnp.float32
        )
    qkv = projected.astype(jnp.bfloat16)
    heads_dev = width_dev // HEAD
    query = qkv[0].astype(jnp.float32).reshape(images, patches, heads_dev, HEAD)
    keys = qkv[1].astype(jnp.float32).reshape(images, patches, heads_dev, HEAD)
    values = qkv[2].reshape(images, patches, heads_dev, HEAD)
    q_norm = (
        norm_last(query, 1e-06) * qk_gain[0].reshape(heads_dev, HEAD) * HEAD ** (-0.5)
    ).astype(jnp.bfloat16)
    k_norm = (norm_last(keys, 1e-06) * qk_gain[1].reshape(heads_dev, HEAD)).astype(jnp.bfloat16)
    scores = jnp.einsum("iphe,iqhe->ihpq", q_norm, k_norm, preferred_element_type=jnp.float32)
    probs = jax.nn.softmax(scores, axis=-1).astype(jnp.bfloat16)
    output = jnp.einsum("ihpq,iqhe->iphe", probs, values, preferred_element_type=jnp.float32)
    return output.astype(jnp.bfloat16).reshape(images, patches, width_dev)


def solution(mesh):
    grid = Mesh(mesh.devices.reshape(SIZES), AXES)
    dp, tensor = ("x", "zl"), ("zh", "y", "c")
    placed = (
        P(dp, None, tensor),
        P(dp),
        P(dp),
        P(),
        P(None, dp, tensor),
        P(None, tensor),
    )
    return jax.shard_map(
        per_device, mesh=grid, in_specs=placed, out_specs=P(dp, None, tensor), check_vma=False
    )
```

time: 466 us -> 256 us (0.55)
  the two profiles are of different devices: /device:TPU:16 before, /device:TPU:6 now
where the time goes in v1:
time: 256 us; the launch traced here: 255 us
  waiting for transfers between devices  86.5 us (34%)
  starting transfers between devices  62 us (24%)
  local copies, waits for them, and re-layouts  44.2 us (17%)
  other arithmetic  34.2 us (13%)
  matrix products  14 us (5%)
  between operations  13.9 us (5%)
    ppermute x14, starting transfers between devices, move(): return lax.ppermute(value, AXES, pairs)  62 us
    ppermute x14, waiting for transfers between devices, move(): return lax.ppermute(value, AXES, pairs)  60 us
    convert_element_type x2, local copies, waits for them, and re-layouts, per_device(): mixed_all.astype(jnp.float32)  35.8 us
    all_gather x1, waiting for transfers between devices, per_device(): quarter = lax.all_gather(qkv_weight, 'zl', axis=1, tiled=True)  26.5 us
    dot_general x4, matrix products, per_device(): jnp.einsum('ipd,cde->cipe', rows, weight, preferred_element_type=jnp.floa...  12.6 us
    convert_element_type x1, other arithmetic, per_device(): (norm_last(mixed_all.astype(jnp.float32), 1e-06) * ln_gain).astype(jnp.bf...  9.82 us
    reduce_sum x3, other arithmetic, norm_last(): var = jnp.mean(centred * centred, axis=-1, keepdims=True)  5.75 us
  transfers between devices with their start and end apart: 15, of which 10 were waited for; matrix products, arithmetic and copies ran while one was open for 31% of the time, Pallas kernels for 0%

profile of v1, /device:TPU:6, one launch (start us, length us, event | category | flops | bytes accessed | tf_op | source)
XLA Modules:
  0.0 254.7 jit_solution(8668506422307529328)
XLA Ops:
  6.5 13.4 %collective-permute-start = (bf16[2,256,384]{2,1,0:T(8,128)(2,1)}, bf16[2,256,384]{2,1,0:T(8,128)(2,1)S(1)}, u32[]{:S(2)}, u32[]{:S(2)}) collective-permute-start(bf16[2,256,384]{2,1,0:T(8,128)(2,1)} %param.6), channel_id=1, source_target_pairs={{0,496},{1,497},{2,498},{3,499},{4,500},{5,501},{6,502},{7,503},{8... | collective-permute-start | bytes 1179656 | tf_op jit(solution)/shard_map/ppermute | solution.py:24
  20.0 0.7 compare_and_fusion
  20.6 0.7 convert_multiply_fusion
  21.3 7.3 %collective-permute-done = bf16[2,256,384]{2,1,0:T(8,128)(2,1)S(1)} collective-permute-done((bf16[2,256,384]{2,1,0:T(8,128)(2,1)}, bf16[2,256,384]{2,1,0:T(8,128)(2,1)S(1)}, u32[]{:S(2)}, u32[]{:S(2)}) %collective-permute-start) | collective-permute-done | bytes 393248 | tf_op jit(solution)/shard_map/ppermute | solution.py:24
  28.6 0.6 gather_fusion
  29.3 1.2 add_convert_fusion
  30.6 1.9 collective-permute-start.1
  32.5 7.8 %collective-permute-start.3 = (bf16[256,384]{1,0:T(8,128)(2,1)S(1)}, bf16[256,384]{1,0:T(8,128)(2,1)S(1)}, u32[]{:S(2)}, u32[]{:S(2)}) collective-permute-start(bf16[256,384]{1,0:T(8,128)(2,1)S(1)} %get-tuple-element.13), channel_id=1, source_target_pairs={{0,72},{1,73},{2,74},{3,75},{4,76},{5,77},{6,78},{7,79},{8,64},{9,... | collective-permute-start | bytes 589832 | tf_op jit(solution)/shard_map/ppermute | solution.py:24
  40.3 9.1 %collective-permute-done.1 = bf16[256,384]{1,0:T(8,128)(2,1)S(1)} collective-permute-done((bf16[256,384]{1,0:T(8,128)(2,1)S(1)}, bf16[256,384]{1,0:T(8,128)(2,1)S(1)}, u32[]{:S(2)}, u32[]{:S(2)}) %collective-permute-start.1) | collective-permute-done | bytes 196640 | tf_op jit(solution)/shard_map/ppermute | solution.py:24
  49.4 6.7 %collective-permute-start.2 = (bf16[256,384]{1,0:T(8,128)(2,1)S(1)}, bf16[256,384]{1,0:T(8,128)(2,1)S(1)}, u32[]{:S(2)}, u32[]{:S(2)}) collective-permute-start(bf16[256,384]{1,0:T(8,128)(2,1)S(1)} %collective-permute-done.1), channel_id=1, source_target_pairs={{0,64},{1,65},{2,66},{3,67},{4,68},{5,69},{6,70},{7,71},{8,72},{9,... | collective-permute-start | bytes 589832 | tf_op jit(solution)/shard_map/ppermute | solution.py:24
  56.2 3.0 %collective-permute-start.4 = (bf16[256,384]{1,0:T(8,128)(2,1)S(1)}, bf16[256,384]{1,0:T(8,128)(2,1)S(1)}, u32[]{:S(2)}, u32[]{:S(2)}) collective-permute-start(bf16[256,384]{1,0:T(8,128)(2,1)S(1)} %collective-permute-done.3), channel_id=1, source_target_pairs={{0,72},{1,73},{2,74},{3,75},{4,76},{5,77},{6,78},{7,79},{8,64},{9,... | collective-permute-start | bytes 589832 | tf_op jit(solution)/shard_map/ppermute | solution.py:24
  59.2 14.2 %collective-permute-done.2 = bf16[256,384]{1,0:T(8,128)(2,1)S(1)} collective-permute-done((bf16[256,384]{1,0:T(8,128)(2,1)S(1)}, bf16[256,384]{1,0:T(8,128)(2,1)S(1)}, u32[]{:S(2)}, u32[]{:S(2)}) %collective-permute-start.2) | collective-permute-done | bytes 196640 | tf_op jit(solution)/shard_map/ppermute | solution.py:24
  73.4 1.0 collective-permute-done.4
  74.4 0.1 fusion.35
  74.5 0.1 maximum_select_fusion.2
  74.6 3.5 %collective-permute-start.6 = (bf16[2,2,256,384]{3,2,1,0:T(8,128)(2,1)S(1)}, bf16[2,2,256,384]{3,2,1,0:T(8,128)(2,1)S(1)}, u32[]{:S(2)}, u32[]{:S(2)}) collective-permute-start(bf16[2,2,256,384]{3,2,1,0:T(8,128)(2,1)S(1)} %maximum_select_fusion.2), channel_id=1, source_target_pairs={{0,2},{1,3},{2,4},{3,5},{4,6},{5,7},{6,0},{7,1},{8,10},{9,11},{10,... | collective-permute-start | bytes 2359304 | tf_op jit(solution)/shard_map/ppermute | solution.py:24
  78.1 3.6 %collective-permute-start.5 = (bf16[2,2,256,384]{3,2,1,0:T(8,128)(2,1)S(1)}, bf16[2,2,256,384]{3,2,1,0:T(8,128)(2,1)S(1)}, u32[]{:S(2)}, u32[]{:S(2)}) collective-permute-start(bf16[2,2,256,384]{3,2,1,0:T(8,128)(2,1)S(1)} %maximum_select_fusion.2), channel_id=1, source_target_pairs={{0,6},{1,7},{2,0},{3,1},{4,2},{5,3},{6,4},{7,5},{8,14},{9,15},{10,... | collective-permute-start | bytes 2359304 | tf_op jit(solution)/shard_map/ppermute | solution.py:24
  81.7 0.0 all-gather.2.cloned.1.call-update
  81.7 15.5 %collective-permute-done.6 = bf16[2,2,256,384]{3,2,1,0:T(8,128)(2,1)S(1)} collective-permute-done((bf16[2,2,256,384]{3,2,1,0:T(8,128)(2,1)S(1)}, bf16[2,2,256,384]{3,2,1,0:T(8,128)(2,1)S(1)}, u32[]{:S(2)}, u32[]{:S(2)}) %collective-permute-start.6) | collective-permute-done | bytes 786464 | tf_op jit(solution)/shard_map/ppermute | solution.py:24
  97.3 2.2 collective-permute-start.7
  99.6 4.8 %collective-permute-start.8 = (bf16[2,1,256,384]{3,2,1,0:T(8,128)(2,1)S(1)}, bf16[2,1,256,384]{3,2,1,0:T(8,128)(2,1)S(1)}, u32[]{:S(2)}, u32[]{:S(2)}) collective-permute-start(bf16[2,1,256,384]{3,2,1,0:T(8,128)(2,1)S(1)} %slice.51), channel_id=1, source_target_pairs={{0,6},{1,7},{2,0},{3,1},{4,2},{5,3},{6,4},{7,5},{8,14},{9,15},{10,... | collective-permute-start | bytes 1179656 | tf_op jit(solution)/shard_map/ppermute | solution.py:24
  104.5 0.1 maximum_select_fusion.1
  104.6 6.0 %collective-permute-done.7 = bf16[2,1,256,384]{3,2,1,0:T(8,128)(2,1)S(1)} collective-permute-done((bf16[2,1,256,384]{3,2,1,0:T(8,128)(2,1)S(1)}, bf16[2,1,256,384]{3,2,1,0:T(8,128)(2,1)S(1)}, u32[]{:S(2)}, u32[]{:S(2)}) %collective-permute-start.7) | collective-permute-done | bytes 393248 | tf_op jit(solution)/shard_map/ppermute | solution.py:24
  110.7 1.2 collective-permute-done.8
  111.9 0.1 maximum_bitcast_fusion.2
  112.0 1.9 pad_maximum_fusion
  113.9 3.2 %gather_fusion.1 = bf16[4,2,2,256,384]{4,3,2,1,0:T(8,128)(2,1)S(1)} fusion(bf16[4,2,2,256,384]{4,3,2,1,0:T(8,128)(2,1)} %pad_maximum_fusion, s32[1024]{0:T(1024)S(1)} %pad_clamp_fusion), kind=kCustom, calls=%fused_computation.1 | custom fusion | bytes 6291472 | tf_op jit(solution)/shard_map/jit(_take)/gather | solution.py:80
  117.1 0.0 copy-start.3
  117.1 2.3 broadcast_select_fusion
  119.4 0.3 copy-done
  119.8 1.9 collective-permute-start.9
  121.8 2.3 bitcast_select_fusion
  124.1 26.5 %all-gather.2.cloned.1.call-done = bf16[3,1536,256]{2,1,0:T(8,128)(2,1)} async-done(((bf16[3,192,256]{2,1,0:T(8,128)(2,1)}), bf16[3,1536,256]{2,1,0:T(8,128)(2,1)}) %all-gather.2.cloned.1.call-update) | async-done | bytes 2359312 | tf_op jit(solution)/shard_map/all_gather | solution.py:88
  150.6 2.7 %collective-permute-start.10 = (bf16[3,1536,256]{2,1,0:T(8,128)(2,1)}, bf16[3,1536,256]{2,1,0:T(8,128)(2,1)}, u32[]{:S(2)}, u32[]{:S(2)}) collective-permute-start(bf16[3,1536,256]{2,1,0:T(8,128)(2,1)} %all-gather.2.cloned.1.call-done), channel_id=1, source_target_pairs={{0,384},{1,385},{2,386},{3,387},{4,388},{5,389},{6,390},{7,391},{8... | collective-permute-start | bytes 7077896 | tf_op jit(solution)/shard_map/ppermute | solution.py:24
  153.3 4.3 %collective-permute-start.11 = (bf16[3,1536,256]{2,1,0:T(8,128)(2,1)}, bf16[3,1536,256]{2,1,0:T(8,128)(2,1)}, u32[]{:S(2)}, u32[]{:S(2)}) collective-permute-start(bf16[3,1536,256]{2,1,0:T(8,128)(2,1)} %all-gather.2.cloned.1.call-done), channel_id=1, source_target_pairs={{0,128},{1,129},{2,130},{3,131},{4,132},{5,133},{6,134},{7,135},{8... | collective-permute-start | bytes 7077896 | tf_op jit(solution)/shard_map/ppermute | solution.py:24
  157.6 4.2 %convert_bitcast_fusion = f32[2,256,2,4,2,384]{5,1,0,2,3,4:T(8,128)S(1)} fusion(bf16[1,4,2,2,256,384]{5,4,3,2,1,0:T(8,128)(2,1)S(1)} %bitcast_select_fusion, bf16[1,4,2,2,256,384]{5,4,3,2,1,0:T(8,128)(2,1)} %bitcast.13, pred[]{:T(512)S(6)} %eq.15), kind=kLoop, calls=%fused_computation.3 | loop fusion | flops 12582912 | bytes 18874368 | tf_op jit(solution)/shard_map/convert_element_type | solution.py:98
  161.9 19.6 %copy.7 = f32[2,256,2,4,2,384]{5,4,3,2,1,0:T(2,128)} copy(f32[2,256,2,4,2,384]{5,1,0,2,3,4:T(8,128)S(1)} %convert_bitcast_fusion) | data formatting | bytes 25165824 | tf_op jit(solution)/shard_map/convert_element_type | solution.py:98
  181.5 16.2 %reshape.191 = f32[2,256,6144]{2,1,0:T(8,128)} reshape(f32[2,256,2,4,2,384]{5,4,3,2,1,0:T(2,128)} %copy.7) | data formatting | bytes 25165824 | tf_op jit(solution)/shard_map/convert_element_type | solution.py:98
  197.7 4.4 %fusion.1 = f32[2,256]{1,0:T(2,128)S(1)} fusion(bf16[1,4,2,2,256,384]{5,4,3,2,1,0:T(8,128)(2,1)S(1)} %bitcast_select_fusion, bf16[1,4,2,2,256,384]{5,4,3,2,1,0:T(8,128)(2,1)} %bitcast.13, pred[]{:T(512)S(6)} %eq.15), kind=kLoop, calls=%fused_computation.6 | loop fusion | flops 15728128 | bytes 6293505 | tf_op jit(solution)/shard_map/reduce_sum | solution.py:56
  202.1 5.0 %multiply_reduce_fusion = f32[2,256]{1,0:T(2,128)S(1)} fusion(f32[2,256]{1,0:T(2,128)S(1)} %broadcast_multiply_fusion.2, bf16[1,4,2,2,256,384]{5,4,3,2,1,0:T(8,128)(2,1)S(1)} %bitcast_select_fusion, bf16[1,4,2,2,256,384]{5,4,3,2,1,0:T(8,128)(2,1)} %bitcast.13, pred[]{:T(512)S(6)} %eq.15), kind=kLoop, calls=%fused_computation.5 | loop fusion | flops 22019584 | bytes 6295553 | tf_op jit(solution)/shard_map/reduce_sum | solution.py:58
  207.1 0.0 copy-start.2
  207.1 1.4 slice.52
  208.5 2.8 %collective-permute-start.12 = (bf16[3,768,256]{2,1,0:T(8,128)(2,1)S(1)}, bf16[3,768,256]{2,1,0:T(8,128)(2,1)S(1)}, u32[]{:S(2)}, u32[]{:S(2)}) collective-permute-start(bf16[3,768,256]{2,1,0:T(8,128)(2,1)S(1)} %slice.52), channel_id=1, source_target_pairs={{0,128},{1,129},{2,130},{3,131},{4,132},{5,133},{6,134},{7,135},{8... | collective-permute-start | bytes 3538952 | tf_op jit(solution)/shard_map/ppermute | solution.py:24
  211.3 1.4 slice.53
  212.7 3.2 %collective-permute-start.13 = (bf16[3,768,256]{2,1,0:T(8,128)(2,1)S(1)}, bf16[3,768,256]{2,1,0:T(8,128)(2,1)}, u32[]{:S(2)}, u32[]{:S(2)}) collective-permute-start(bf16[3,768,256]{2,1,0:T(8,128)(2,1)S(1)} %slice.53), channel_id=1, source_target_pairs={{0,384},{1,385},{2,386},{3,387},{4,388},{5,389},{6,390},{7,391},{8... | collective-permute-start | bytes 3538952 | tf_op jit(solution)/shard_map/ppermute | solution.py:24
  215.9 9.8 %multiply_convert_fusion = bf16[2,256,6144]{2,1,0:T(8,128)(2,1)} fusion(f32[2,256,6144]{2,1,0:T(8,128)} %reshape.191, f32[6144]{0:T(1024)S(1)} %copy-done.2, f32[2,256]{1,0:T(2,128)S(1)} %add_sqrt_fusion.2, f32[2,256]{1,0:T(2,128)S(1)} %broadcast_multiply_fusion.2), kind=kLoop, calls=%fused_computation.4 | loop fusion | flops 12582912 | bytes 18903040 | tf_op jit(solution)/shard_map/convert_element_type | solution.py:98
  225.7 3.7 %fusion.9 = f32[2,256,3,256]{1,3,2,0:T(8,128)S(1)} fusion(bf16[3,1536,256]{2,1,0:T(8,128)(2,1)} %all-gather.2.cloned.1.call-done, bf16[2,256,6144]{2,1,0:T(8,128)(2,1)} %multiply_convert_fusion, s32[]{:T(128)S(6)} %select_n.135), kind=kOutput, calls=%fused_computation.19 | convolution fusion | flops 1207959552 | bytes 5505028 | tf_op jit(solution)/shard_map/ipd,cde->cipe/dot_general | solution.py:105
  229.4 0.2 copy-done.1
  229.7 3.1 %fusion.7 = f32[2,256,3,256]{1,3,2,0:T(8,128)S(1)} fusion(bf16[3,1536,256]{2,1,0:T(8,128)(2,1)} %collective-permute-done.10, bf16[2,256,6144]{2,1,0:T(8,128)(2,1)S(1)} %copy-done.1, s32[]{:T(128)S(6)} %select_n.137), kind=kOutput, calls=%fused_computation.17 | convolution fusion | flops 1207959552 | bytes 5505028 | tf_op jit(solution)/shard_map/ipd,cde->cipe/dot_general | solution.py:105
  232.8 0.9 collective-permute-done.12
  233.7 4.6 %collective-permute-done.13 = bf16[3,768,256]{2,1,0:T(8,128)(2,1)} collective-permute-done((bf16[3,768,256]{2,1,0:T(8,128)(2,1)S(1)}, bf16[3,768,256]{2,1,0:T(8,128)(2,1)}, u32[]{:S(2)}, u32[]{:S(2)}) %collective-permute-start.13) | collective-permute-done | bytes 1179680 | tf_op jit(solution)/shard_map/ppermute | solution.py:24
  238.3 2.7 %fusion.2 = f32[3,256,2,256]{3,1,0,2:T(8,128)S(1)} fusion(bf16[3,768,256]{2,1,0:T(8,128)(2,1)} %collective-permute-done.13, bf16[3,768,256]{2,1,0:T(8,128)(2,1)S(1)} %collective-permute-done.12, bf16[2,256,6144]{2,1,0:T(8,128)(2,1)S(1)} %copy-done.1, s32[]{:T(128)S(6)} %select_n.139), kind=kOutput, calls=%fused_computation.12 | convolution fusion | flops 1212678144 | bytes 5505028 | tf_op jit(solution)/shard_map/ipd,cde->cipe/dot_general | solution.py:105
  241.0 3.1 %fusion.15 = bf16[3,2,256,256]{2,3,0,1:T(8,128)(2,1)S(1)} fusion(f32[3,256,2,256]{3,1,0,2:T(8,128)S(1)} %fusion.2, f32[2,256,3,256]{1,3,2,0:T(8,128)S(1)} %fusion.9, f32[2,256,3,256]{1,3,2,0:T(8,128)S(1)} %fusion.7, bf16[3,1536,256]{2,1,0:T(8,128)(2,1)} %collective-permute-done.11, bf16[2,256,6144]{2,1,0:T(8,128)(2,1)S(1)} %copy-done.1, s32[]{:T(128)S(6)} %select_n.141), kind=kOutput, calls=%fused_computation.26 | convolution fusion | flops 1209532416 | bytes 9437188 | tf_op jit(solution)/shard_map/ipd,cde->cipe/dot_general | solution.py:105
  244.2 0.1 fusion.47
  244.2 0.1 copy.12
  244.4 0.1 convert_reduce_fusion.1
  244.4 0.1 copy.13
  244.6 0.1 convert_reduce_fusion
  244.6 0.4 multiply_reduce_fusion.2
  245.0 0.4 multiply_reduce_fusion.1
  245.4 1.0 fusion.26
  246.4 0.2 fusion.49
  246.6 0.4 convolution_convert_fusion
  247.1 0.8 copy.15
  (23 shorter events, 0.2 us)
Async XLA Ops:
  6.5 144.0 %all-gather.2.cloned.1.call-start = ((), (), s32[]{:S(2)}) async-start(), calls=%async_computation | async-start | bytes 2654208 | tf_op jit(solution)/shard_map/all_gather | solution.py:88
  6.5 22.1 %collective-permute-start = (bf16[2,256,384]{2,1,0:T(8,128)(2,1)}, bf16[2,256,384]{2,1,0:T(8,128)(2,1)S(1)}, u32[]{:S(2)}, u32[]{:S(2)}) collective-permute-start(bf16[2,256,384]{2,1,0:T(8,128)(2,1)} %param.6), channel_id=1, source_target_pairs={{0,496},{1,497},{2,498},{3,499},{4,500},{5,501},{6,502},{7,503},{8... | collective-permute-start | bytes 1179656 | tf_op jit(solution)/shard_map/ppermute | solution.py:24
  30.6 18.9 %collective-permute-start.1 = (bf16[256,384]{1,0:T(8,128)(2,1)S(1)}, bf16[256,384]{1,0:T(8,128)(2,1)S(1)}, u32[]{:S(2)}, u32[]{:S(2)}) collective-permute-start(bf16[256,384]{1,0:T(8,128)(2,1)S(1)} %get-tuple-element.12), channel_id=1, source_target_pairs={{0,64},{1,65},{2,66},{3,67},{4,68},{5,69},{6,70},{7,71},{8,72},{9,... | collective-permute-start | bytes 589832 | tf_op jit(solution)/shard_map/ppermute | solution.py:24
  32.5 23.7 %collective-permute-start.3 = (bf16[256,384]{1,0:T(8,128)(2,1)S(1)}, bf16[256,384]{1,0:T(8,128)(2,1)S(1)}, u32[]{:S(2)}, u32[]{:S(2)}) collective-permute-start(bf16[256,384]{1,0:T(8,128)(2,1)S(1)} %get-tuple-element.13), channel_id=1, source_target_pairs={{0,72},{1,73},{2,74},{3,75},{4,76},{5,77},{6,78},{7,79},{8,64},{9,... | collective-permute-start | bytes 589832 | tf_op jit(solution)/shard_map/ppermute | solution.py:24
  49.4 24.0 %collective-permute-start.2 = (bf16[256,384]{1,0:T(8,128)(2,1)S(1)}, bf16[256,384]{1,0:T(8,128)(2,1)S(1)}, u32[]{:S(2)}, u32[]{:S(2)}) collective-permute-start(bf16[256,384]{1,0:T(8,128)(2,1)S(1)} %collective-permute-done.1), channel_id=1, source_target_pairs={{0,64},{1,65},{2,66},{3,67},{4,68},{5,69},{6,70},{7,71},{8,72},{9,... | collective-permute-start | bytes 589832 | tf_op jit(solution)/shard_map/ppermute | solution.py:24
  56.2 18.2 %collective-permute-start.4 = (bf16[256,384]{1,0:T(8,128)(2,1)S(1)}, bf16[256,384]{1,0:T(8,128)(2,1)S(1)}, u32[]{:S(2)}, u32[]{:S(2)}) collective-permute-start(bf16[256,384]{1,0:T(8,128)(2,1)S(1)} %collective-permute-done.3), channel_id=1, source_target_pairs={{0,72},{1,73},{2,74},{3,75},{4,76},{5,77},{6,78},{7,79},{8,64},{9,... | collective-permute-start | bytes 589832 | tf_op jit(solution)/shard_map/ppermute | solution.py:24
  74.6 22.6 %collective-permute-start.6 = (bf16[2,2,256,384]{3,2,1,0:T(8,128)(2,1)S(1)}, bf16[2,2,256,384]{3,2,1,0:T(8,128)(2,1)S(1)}, u32[]{:S(2)}, u32[]{:S(2)}) collective-permute-start(bf16[2,2,256,384]{3,2,1,0:T(8,128)(2,1)S(1)} %maximum_select_fusion.2), channel_id=1, source_target_pairs={{0,2},{1,3},{2,4},{3,5},{4,6},{5,7},{6,0},{7,1},{8,10},{9,11},{10,... | collective-permute-start | bytes 2359304 | tf_op jit(solution)/shard_map/ppermute | solution.py:24
  78.1 21.4 %collective-permute-start.5 = (bf16[2,2,256,384]{3,2,1,0:T(8,128)(2,1)S(1)}, bf16[2,2,256,384]{3,2,1,0:T(8,128)(2,1)S(1)}, u32[]{:S(2)}, u32[]{:S(2)}) collective-permute-start(bf16[2,2,256,384]{3,2,1,0:T(8,128)(2,1)S(1)} %maximum_select_fusion.2), channel_id=1, source_target_pairs={{0,6},{1,7},{2,0},{3,1},{4,2},{5,3},{6,4},{7,5},{8,14},{9,15},{10,... | collective-permute-start | bytes 2359304 | tf_op jit(solution)/shard_map/ppermute | solution.py:24
  97.3 13.4 %collective-permute-start.7 = (bf16[2,1,256,384]{3,2,1,0:T(8,128)(2,1)S(1)}, bf16[2,1,256,384]{3,2,1,0:T(8,128)(2,1)S(1)}, u32[]{:S(2)}, u32[]{:S(2)}) collective-permute-start(bf16[2,1,256,384]{3,2,1,0:T(8,128)(2,1)S(1)} %slice.50), channel_id=1, source_target_pairs={{0,2},{1,3},{2,4},{3,5},{4,6},{5,7},{6,0},{7,1},{8,10},{9,11},{10,... | collective-permute-start | bytes 1179656 | tf_op jit(solution)/shard_map/ppermute | solution.py:24
  99.6 12.3 %collective-permute-start.8 = (bf16[2,1,256,384]{3,2,1,0:T(8,128)(2,1)S(1)}, bf16[2,1,256,384]{3,2,1,0:T(8,128)(2,1)S(1)}, u32[]{:S(2)}, u32[]{:S(2)}) collective-permute-start(bf16[2,1,256,384]{3,2,1,0:T(8,128)(2,1)S(1)} %slice.51), channel_id=1, source_target_pairs={{0,6},{1,7},{2,0},{3,1},{4,2},{5,3},{6,4},{7,5},{8,14},{9,15},{10,... | collective-permute-start | bytes 1179656 | tf_op jit(solution)/shard_map/ppermute | solution.py:24
  117.1 2.7 %copy-start = (bf16[4,2,2,256,384]{4,3,2,1,0:T(8,128)(2,1)}, bf16[4,2,2,256,384]{4,3,2,1,0:T(8,128)(2,1)S(1)}, u32[]{:S(2)}) copy-start(bf16[4,2,2,256,384]{4,3,2,1,0:T(8,128)(2,1)S(1)} %gather_fusion.1) | copy-start | bytes 9437188
  117.1 4.7 %copy-start.3 = (f32[2,256]{1,0:T(2,128)S(1)}, f32[2,256]{1,0:T(2,128)}, u32[]{:S(2)}) copy-start(f32[2,256]{1,0:T(2,128)} %param.11) | copy-start | bytes 6148
  119.8 37.9 %collective-permute-start.9 = (bf16[4,2,2,256,384]{4,3,2,1,0:T(8,128)(2,1)}, bf16[4,2,2,256,384]{4,3,2,1,0:T(8,128)(2,1)}, u32[]{:S(2)}, u32[]{:S(2)}) collective-permute-start(bf16[4,2,2,256,384]{4,3,2,1,0:T(8,128)(2,1)} %broadcast_select_fusion), channel_id=1, source_target_pairs={{0,1},{1,0},{2,3},{3,2},{4,5},{5,4},{6,7},{7,6},{8,9},{9,8},{10,11... | collective-permute-start | bytes 9437192 | tf_op jit(solution)/shard_map/ppermute | solution.py:24
  150.6 60.7 %collective-permute-start.10 = (bf16[3,1536,256]{2,1,0:T(8,128)(2,1)}, bf16[3,1536,256]{2,1,0:T(8,128)(2,1)}, u32[]{:S(2)}, u32[]{:S(2)}) collective-permute-start(bf16[3,1536,256]{2,1,0:T(8,128)(2,1)} %all-gather.2.cloned.1.call-done), channel_id=1, source_target_pairs={{0,384},{1,385},{2,386},{3,387},{4,388},{5,389},{6,390},{7,391},{8... | collective-permute-start | bytes 7077896 | tf_op jit(solution)/shard_map/ppermute | solution.py:24
  153.3 53.8 %collective-permute-start.11 = (bf16[3,1536,256]{2,1,0:T(8,128)(2,1)}, bf16[3,1536,256]{2,1,0:T(8,128)(2,1)}, u32[]{:S(2)}, u32[]{:S(2)}) collective-permute-start(bf16[3,1536,256]{2,1,0:T(8,128)(2,1)} %all-gather.2.cloned.1.call-done), channel_id=1, source_target_pairs={{0,128},{1,129},{2,130},{3,131},{4,132},{5,133},{6,134},{7,135},{8... | collective-permute-start | bytes 7077896 | tf_op jit(solution)/shard_map/ppermute | solution.py:24
  207.1 8.8 %copy-start.2 = (f32[6144]{0:T(1024)S(1)}, f32[6144]{0:T(1024)}, u32[]{:S(2)}) copy-start(f32[6144]{0:T(1024)} %param.9) | copy-start | bytes 73732
  208.5 25.2 %collective-permute-start.12 = (bf16[3,768,256]{2,1,0:T(8,128)(2,1)S(1)}, bf16[3,768,256]{2,1,0:T(8,128)(2,1)S(1)}, u32[]{:S(2)}, u32[]{:S(2)}) collective-permute-start(bf16[3,768,256]{2,1,0:T(8,128)(2,1)S(1)} %slice.52), channel_id=1, source_target_pairs={{0,128},{1,129},{2,130},{3,131},{4,132},{5,133},{6,134},{7,135},{8... | collective-permute-start | bytes 3538952 | tf_op jit(solution)/shard_map/ppermute | solution.py:24
  212.7 25.7 %collective-permute-start.13 = (bf16[3,768,256]{2,1,0:T(8,128)(2,1)S(1)}, bf16[3,768,256]{2,1,0:T(8,128)(2,1)}, u32[]{:S(2)}, u32[]{:S(2)}) collective-permute-start(bf16[3,768,256]{2,1,0:T(8,128)(2,1)S(1)} %slice.53), channel_id=1, source_target_pairs={{0,384},{1,385},{2,386},{3,387},{4,388},{5,389},{6,390},{7,391},{8... | collective-permute-start | bytes 3538952 | tf_op jit(solution)/shard_map/ppermute | solution.py:24
  225.7 4.0 %copy-start.1 = (bf16[2,256,6144]{2,1,0:T(8,128)(2,1)S(1)}, bf16[2,256,6144]{2,1,0:T(8,128)(2,1)}, u32[]{:S(2)}) copy-start(bf16[2,256,6144]{2,1,0:T(8,128)(2,1)} %multiply_convert_fusion) | copy-start | bytes 18874372
Sparse Core Ops, SparseCore 0:
  81.9 68.6 all-gather.1

commit v2 on v1

v2 whole, which is shorter than its diff:
```python
import functools

import jax
import jax.numpy as jnp
import numpy as np
from jax import lax
from jax.experimental import pallas as pl
from jax.experimental.pallas import tpu as pltpu
from jax.sharding import Mesh, PartitionSpec as P

HEAD = 128
AXES = ("x", "zl", "zh", "y", "c")
SIZES = (4, 8, 2, 4, 2)
VMEM_LIMIT = 56 * 1024 * 1024

SLOT_SOURCES = np.array(
    [
        [0, 2, 1, 3, 4, 5, 6, 7],
        [1, 0, 2, 4, 3, 5, 6, 7],
        [2, 1, 3, 0, 4, 6, 7, 5],
        [3, 2, 4, 1, 5, 7, 6, 0],
        [4, 3, 5, 2, 6, 0, 1, 7],
        [5, 4, 6, 3, 7, 1, 0, 2],
        [6, 5, 7, 4, 3, 2, 1, 0],
        [7, 6, 5, 3, 4, 2, 1, 0],
    ],
    dtype=np.int32,
)


def move(value, target):
    pairs = []
    for source in range(512):
        c = source % 2
        y = source // 2 % 4
        zh = source // 8 % 2
        zl = source // 16 % 8
        x = source // 128
        goal = target(x, zl, zh, y, c)
        if goal is None:
            continue
        gx, gzl, gzh, gy, gc = goal
        pairs.append((source, (((gx % 4 * 8 + gzl) * 2 + gzh) * 4 + gy % 4) * 2 + gc))
    return lax.ppermute(value, AXES, pairs)


def along_x(value, by):
    return move(value, lambda x, zl, zh, y, c: (x + by, zl, zh, y, c))


def along_z(value, by):
    def target(x, zl, zh, y, c):
        z = (zh * 8 + zl + by) % 16
        return x, z % 8, z // 8, y, c

    return move(value, target)


def along_line(value, up=(), down=()):
    def target(x, zl, zh, y, c):
        if zl in up:
            return x, zl + 1, zh, y, c
        if zl in down:
            return x, zl - 1, zh, y, c
        return None

    return move(value, target)


def previous_images(value):
    def target(x, zl, zh, y, c):
        dp = (x * 8 + zl - 1) % 32
        return dp // 8, dp % 8, zh, y, c

    return move(value, target)


def norm_last(values, eps):
    mean = jnp.mean(values, axis=-1, keepdims=True)
    centred = values - mean
    var = jnp.mean(centred * centred, axis=-1, keepdims=True)
    return centred / jnp.sqrt(var + eps)


def norm_kernel(own_ref, other_ref, gain_ref, out_ref):
    parts = [ref[j].astype(jnp.float32) for ref in (own_ref, other_ref) for j in range(8)]
    count = 16 * parts[0].shape[1]
    total = functools.reduce(jnp.add, parts)
    mean = jnp.sum(total, axis=-1, keepdims=True) / count
    parts = [part - mean for part in parts]
    total = functools.reduce(jnp.add, [part * part for part in parts])
    scale = 1.0 / jnp.sqrt(jnp.sum(total, axis=-1, keepdims=True) / count + 1e-06)
    for block, part in enumerate(parts):
        normed = (part * scale * gain_ref[block : block + 1, :]).astype(jnp.bfloat16)
        out_ref[block] = normed[:, :192]
        out_ref[16 + block] = normed[:, 192:]


def norm_tokens(own, other, gain):
    rows = 64
    return pl.pallas_call(
        norm_kernel,
        out_shape=jax.ShapeDtypeStruct((32, 512, 192), jnp.bfloat16),
        grid=(512 // rows,),
        in_specs=[
            pl.BlockSpec((8, rows, 384), lambda i: (0, i, 0)),
            pl.BlockSpec((8, rows, 384), lambda i: (0, i, 0)),
            pl.BlockSpec((16, 384), lambda i: (0, 0)),
        ],
        out_specs=pl.BlockSpec((32, rows, 192), lambda i: (0, i, 0)),
        compiler_params=pltpu.CompilerParams(vmem_limit_bytes=VMEM_LIMIT),
        cost_estimate=pl.CostEstimate(
            flops=512 * 6144 * 8, bytes_accessed=14 * 2**20, transcendentals=0
        ),
    )(own, other, gain)


def add_products(blocks, index_ref, normed_ref, piece_refs, acc_ref):
    for which, (left, right) in blocks:
        rows = normed_ref[index_ref[which]]
        for c in range(3):
            weight = jnp.concatenate(
                [piece_refs[left[0]][left[1], c], piece_refs[right[0]][right[1], c]], axis=-1
            )
            acc_ref[c] += jnp.dot(rows, weight, preferred_element_type=jnp.float32)


def first_kernel(blocks, index_ref, normed_ref, *refs):
    pieces, acc_ref = refs[:-1], refs[-1]
    acc_ref[...] = jnp.zeros_like(acc_ref)
    add_products(blocks, index_ref, normed_ref, pieces, acc_ref)


def next_kernel(blocks, index_ref, normed_ref, held_ref, *refs):
    pieces, acc_ref = refs[:-1], refs[-1]
    acc_ref[...] = held_ref[...]
    add_products(blocks, index_ref, normed_ref, pieces, acc_ref)


def attend(acc_ref, gain_ref, out_ref):
    for head in range(2):
        columns = slice(head * HEAD, (head + 1) * HEAD)
        for image in range(2):
            rows = slice(image * 256, (image + 1) * 256)
            query, keys, values = (
                acc_ref[c, rows, columns].astype(jnp.bfloat16) for c in range(3)
            )
            q_norm = (
                norm_last(query.astype(jnp.float32), 1e-06)
                * gain_ref[0:1, columns]
                * HEAD ** (-0.5)
            ).astype(jnp.bfloat16)
            k_norm = (
                norm_last(keys.astype(jnp.float32), 1e-06) * gain_ref[1:2, columns]
            ).astype(jnp.bfloat16)
            scores = lax.dot_general(
                q_norm, k_norm, (((1,), (1,)), ((), ())), preferred_element_type=jnp.float32
            )
            raised = jnp.exp(scores - jnp.max(scores, axis=-1, keepdims=True))
            probs = (raised / jnp.sum(raised, axis=-1, keepdims=True)).astype(jnp.bfloat16)
            out_ref[rows, columns] = jnp.dot(
                probs, values, preferred_element_type=jnp.float32
            ).astype(jnp.bfloat16)


def last_kernel(blocks, index_ref, normed_ref, held_ref, gain_ref, *refs):
    pieces, out_ref, acc_ref = refs[:-2], refs[-2], refs[-1]
    acc_ref[...] = held_ref[...]
    add_products(blocks, index_ref, normed_ref, pieces, acc_ref)
    attend(acc_ref, gain_ref, out_ref)


def project(kernel, blocks, index, normed, extra, pieces, out_shape, scratch=()):
    whole = pl.BlockSpec(memory_space=pltpu.VMEM)
    return pl.pallas_call(
        functools.partial(kernel, blocks),
        out_shape=out_shape,
        in_specs=[pl.BlockSpec(memory_space=pltpu.SMEM)] + [whole] * (1 + len(extra) + len(pieces)),
        out_specs=whole,
        scratch_shapes=list(scratch),
        compiler_params=pltpu.CompilerParams(vmem_limit_bytes=VMEM_LIMIT),
        cost_estimate=pl.CostEstimate(
            flops=len(blocks) * 512 * 192 * 768 * 2,
            bytes_accessed=8 * 2**20 + len(blocks) * 294912,
            transcendentals=0,
        ),
    )(index, normed, *extra, *pieces)


def weight_slots(own, zl):
    a1 = along_line(own, up=range(0, 7))
    b1 = along_line(own, down=range(1, 8))
    a2 = along_line(a1, up=range(1, 7))
    b2 = along_line(b1, down=range(1, 7))
    a3 = along_line(a2, up=range(2, 7))
    b3 = along_line(b2, down=range(1, 6))
    a4 = along_line(a3, up=range(3, 7))
    b4 = along_line(b3, down=range(1, 5))
    m4 = jnp.where(zl >= 4, a4, b4)
    m5 = along_line(m4, up=range(4, 7), down=range(1, 4))
    m6 = along_line(m5, up=range(5, 7), down=range(1, 3))
    m7 = along_line(m6, up=(6,), down=(1,))
    end = (zl == 0) | (zl == 7)
    second = (zl == 1) | (zl == 6)
    return [
        own,
        jnp.where(zl == 0, b2, a1),
        jnp.where(zl == 7, a2, b1),
        jnp.where(zl <= 1, b3, jnp.where(zl == 7, m4, a2)),
        jnp.where(zl == 0, m4, jnp.where(zl <= 5, b2, a3)),
        jnp.where(end, m5, m4),
        jnp.where(end, m6, jnp.where(zl == 3, b3, jnp.where(zl == 4, a3, m5))),
        jnp.where(
            end, m7, jnp.where(second, m6, jnp.where((zl == 2) | (zl == 4), b3, a3))
        ),
    ]


def per_device(tokens, mix_weight, partner_offset, ln_gain, qkv_weight, qk_gain):
    x, zl, zh = lax.axis_index("x"), lax.axis_index("zl"), lax.axis_index("zh")

    partner_block = previous_images(tokens)
    lam = (mix_weight.astype(jnp.float32) / 256.0)[:, None, None]
    first = ((jnp.arange(2, dtype=jnp.int32) + partner_offset) % 2 == 0)[:, None, None]
    partner = jnp.where(first, partner_block[0], partner_block[1])
    mixed = lam * tokens.astype(jnp.float32) + (1.0 - lam) * partner.astype(jnp.float32)
    mixed = mixed.astype(jnp.bfloat16)

    ahead = along_z(along_z(mixed[0], 4), 4)
    behind = along_z(along_z(mixed[1], -4), -4)
    own_features = lax.all_gather(mixed.reshape(512, 384), ("y", "c"))
    other_features = lax.all_gather(jnp.concatenate([ahead, behind]), ("y", "c"))

    halves = jnp.stack([qkv_weight[:, :, :HEAD], qkv_weight[:, :, HEAD:]])
    slots = weight_slots(halves, zl)
    own, left, right = [], [], []
    for group in ((0,), (1, 2), (3, 4), (5, 6), (7,)):
        block = jnp.concatenate([slots[slot] for slot in group])
        to_right, to_left = [block], [block]
        if left:
            full = left[-1].shape[0] // 2 * 2 if len(left) == 1 else 4
            for start in range(0, full, 2):
                to_right.append(left[-1][start : start + 1])
                to_left.append(right[-1][start + 1 : start + 2])
        own.append(block)
        left.append(along_x(jnp.concatenate(to_right), 1))
        right.append(along_x(jnp.concatenate(to_left), -1))
    last_left = along_x(left[-1][0:1], 1)
    last_right = along_x(right[-1][1:2], -1)

    sources = jnp.asarray(SLOT_SOURCES)[zl]
    block_of = ((x + jnp.arange(4, dtype=jnp.int32)) % 4 * 8)[:, None] + sources[None, :]
    feature = block_of // 2
    index = block_of % 2 * 16 + (feature // 8 + zh) % 2 * 8 + feature % 8
    index = index.reshape(32).astype(jnp.int32)

    gain = ln_gain.reshape(2, 8, 384)
    gain = jnp.where(zh == 0, gain, gain[::-1]).reshape(16, 384)
    normed = norm_tokens(own_features, other_features, gain)

    def three(slot, place):
        return [
            (slot, ((0, 2 * place), (0, 2 * place + 1))),
            (8 + slot, ((2, 2 * place), (2, 2 * place + 1))),
            (24 + slot, ((1, 2 * place), (1, 2 * place + 1))),
        ]

    def at(blocks, base):
        return [
            (which, ((a[0] + base, a[1]), (b[0] + base, b[1]))) for which, (a, b) in blocks
        ]

    first_blocks, pieces = [], []
    for group, (slots_in, opposite) in enumerate(
        [((0,), ()), ((1, 2), (0,)), ((3, 4), (1, 2)), ((5, 6), (3, 4))]
    ):
        blocks = []
        for place, slot in enumerate(slots_in):
            blocks += three(slot, place)
        for place, slot in enumerate(opposite):
            tail = 2 * len(slots_in) + place
            blocks.append((16 + slot, ((1, tail), (2, tail))))
        first_blocks += at(blocks, 3 * group)
        pieces += [own[group], left[group], right[group]]
    acc_shape = jax.ShapeDtypeStruct((3, 512, 256), jnp.float32)
    acc = project(first_kernel, first_blocks, index, normed, [], pieces, acc_shape)
    blocks = three(7, 0) + [(16 + 5, ((1, 2), (2, 2))), (16 + 6, ((1, 3), (2, 3)))]
    acc = project(
        next_kernel, blocks, index, normed, [acc], [own[4], left[4], right[4]], acc_shape
    )
    out = project(
        last_kernel,
        [(16 + 7, ((0, 0), (1, 0)))],
        index,
        normed,
        [acc, qk_gain],
        [last_left, last_right],
        jax.ShapeDtypeStruct((512, 256), jnp.bfloat16),
        [pltpu.VMEM((3, 512, 256), jnp.float32)],
    )
    return out.reshape(2, 256, 256)


def solution(mesh):
    grid = Mesh(mesh.devices.reshape(SIZES), AXES)
    dp, tensor = ("x", "zl"), ("zh", "y", "c")
    placed = (
        P(dp, None, tensor),
        P(dp),
        P(dp),
        P(),
        P(None, dp, tensor),
        P(None, tensor),
    )
    return jax.shard_map(
        per_device, mesh=grid, in_specs=placed, out_specs=P(dp, None, tensor), check_vma=False
    )
```

time: 256 us -> 281 us (1.098)
  the two profiles are of different devices: /device:TPU:6 before, /device:TPU:80 now
where the time goes in v2:
time: 281 us; the launch traced here: 280 us
  waiting for transfers between devices  116 us (41%)
  starting transfers between devices  93.6 us (33%)
  Pallas kernels  35.1 us (12%)
  between operations  14 us (5%)
  other arithmetic  11.9 us (4%)
  local copies, waits for them, and re-layouts  8.83 us (3%)
    ppermute x28, waiting for transfers between devices, move(): return lax.ppermute(value, AXES, pairs)  116 us
    ppermute x28, starting transfers between devices, move(): return lax.ppermute(value, AXES, pairs)  93.6 us
    pallas_call x3, Pallas kernels, project(): pl.pallas_call(functools.partial(kernel, blocks), out_shape=out_shape, in...  25 us
    pallas_call x1, Pallas kernels, norm_tokens(): pl.pallas_call(norm_kernel, out_shape=jax.ShapeDtypeStruct((32, 512, 192)...  10.1 us
  transfers between devices with their start and end apart: 30, of which 17 were waited for; matrix products, arithmetic and copies ran while one was open for 5% of the time, Pallas kernels for 10%

profile of v2, /device:TPU:80, one launch (start us, length us, event | category | flops | bytes accessed | tf_op | source)
XLA Modules:
  0.0 279.8 jit_solution(3661795908465834115)
XLA Ops:
  6.5 2.0 collective-permute-start
  8.6 0.7 fusion.8
  9.9 9.8 %collective-permute-done = bf16[2,256,384]{2,1,0:T(8,128)(2,1)S(1)} collective-permute-done((bf16[2,256,384]{2,1,0:T(8,128)(2,1)}, bf16[2,256,384]{2,1,0:T(8,128)(2,1)S(1)}, u32[]{:S(2)}, u32[]{:S(2)}) %collective-permute-start) | collective-permute-done | bytes 393248 | tf_op jit(solution)/shard_map/ppermute | solution.py:44
  19.7 2.0 add_convert_fusion
  21.8 1.0 slice_bitcast_fusion.5
  22.9 5.0 %collective-permute-start.9 = (bf16[2,3,192,128]{3,2,1,0:T(8,128)(2,1)S(1)}, bf16[2,3,192,128]{3,2,1,0:T(8,128)(2,1)S(1)}, u32[]{:S(2)}, u32[]{:S(2)}) collective-permute-start(bf16[2,3,192,128]{3,2,1,0:T(8,128)(2,1)S(1)} %pad_maximum_fusion.15.refs_0_), channel_id=1, source_target_pairs={{0,16},{1,17},{2,18},{3,19},{4,20},{5,21},{6,22},{7,23},{8,24},{9,... | collective-permute-start | bytes 884744 | tf_op jit(solution)/shard_map/ppermute | solution.py:44
  28.0 1.9 collective-permute-start.7
  29.9 7.0 %collective-permute-done.9 = bf16[2,3,192,128]{3,2,1,0:T(8,128)(2,1)S(1)} collective-permute-done((bf16[2,3,192,128]{3,2,1,0:T(8,128)(2,1)S(1)}, bf16[2,3,192,128]{3,2,1,0:T(8,128)(2,1)S(1)}, u32[]{:S(2)}, u32[]{:S(2)}) %collective-permute-start.9) | collective-permute-done | bytes 294944 | tf_op jit(solution)/shard_map/ppermute | solution.py:44
  36.9 3.5 %collective-permute-start.10 = (bf16[2,3,192,128]{3,2,1,0:T(8,128)(2,1)S(1)}, bf16[2,3,192,128]{3,2,1,0:T(8,128)(2,1)S(1)}, u32[]{:S(2)}, u32[]{:S(2)}) collective-permute-start(bf16[2,3,192,128]{3,2,1,0:T(8,128)(2,1)S(1)} %collective-permute-done.9), channel_id=1, source_target_pairs={{16,32},{17,33},{18,34},{19,35},{20,36},{21,37},{22,38},{23,39},{2... | collective-permute-start | bytes 884744 | tf_op jit(solution)/shard_map/ppermute | solution.py:44
  40.4 4.3 %collective-permute-start.8 = (bf16[2,3,192,128]{3,2,1,0:T(8,128)(2,1)S(1)}, bf16[2,3,192,128]{3,2,1,0:T(8,128)(2,1)S(1)}, u32[]{:S(2)}, u32[]{:S(2)}) collective-permute-start(bf16[2,3,192,128]{3,2,1,0:T(8,128)(2,1)S(1)} %collective-permute-done.7), channel_id=1, source_target_pairs={{16,0},{17,1},{18,2},{19,3},{20,4},{21,5},{22,6},{23,7},{24,8},{25... | collective-permute-start | bytes 884744 | tf_op jit(solution)/shard_map/ppermute | solution.py:44
  44.7 3.5 %collective-permute-done.10 = bf16[2,3,192,128]{3,2,1,0:T(8,128)(2,1)S(1)} collective-permute-done((bf16[2,3,192,128]{3,2,1,0:T(8,128)(2,1)S(1)}, bf16[2,3,192,128]{3,2,1,0:T(8,128)(2,1)S(1)}, u32[]{:S(2)}, u32[]{:S(2)}) %collective-permute-start.10) | collective-permute-done | bytes 294944 | tf_op jit(solution)/shard_map/ppermute | solution.py:44
  48.2 3.2 %collective-permute-start.14 = (bf16[2,3,192,128]{3,2,1,0:T(8,128)(2,1)S(1)}, bf16[2,3,192,128]{3,2,1,0:T(8,128)(2,1)S(1)}, u32[]{:S(2)}, u32[]{:S(2)}) collective-permute-start(bf16[2,3,192,128]{3,2,1,0:T(8,128)(2,1)S(1)} %collective-permute-done.10), channel_id=1, source_target_pairs={{32,48},{33,49},{34,50},{35,51},{36,52},{37,53},{38,54},{39,55},{4... | collective-permute-start | bytes 884744 | tf_op jit(solution)/shard_map/ppermute | solution.py:44
  51.9 1.9 collective-permute-start.13
  53.8 3.1 %collective-permute-done.14 = bf16[2,3,192,128]{3,2,1,0:T(8,128)(2,1)S(1)} collective-permute-done((bf16[2,3,192,128]{3,2,1,0:T(8,128)(2,1)S(1)}, bf16[2,3,192,128]{3,2,1,0:T(8,128)(2,1)S(1)}, u32[]{:S(2)}, u32[]{:S(2)}) %collective-permute-start.14) | collective-permute-done | bytes 294944 | tf_op jit(solution)/shard_map/ppermute | solution.py:44
  57.6 5.4 %collective-permute-done.13 = bf16[2,3,192,128]{3,2,1,0:T(8,128)(2,1)S(1)} collective-permute-done((bf16[2,3,192,128]{3,2,1,0:T(8,128)(2,1)S(1)}, bf16[2,3,192,128]{3,2,1,0:T(8,128)(2,1)S(1)}, u32[]{:S(2)}, u32[]{:S(2)}) %collective-permute-start.13) | collective-permute-done | bytes 294944 | tf_op jit(solution)/shard_map/ppermute | solution.py:44
  63.0 1.9 collective-permute-start.16
  65.0 8.3 %collective-permute-done.16 = bf16[2,3,192,128]{3,2,1,0:T(8,128)(2,1)S(1)} collective-permute-done((bf16[2,3,192,128]{3,2,1,0:T(8,128)(2,1)S(1)}, bf16[2,3,192,128]{3,2,1,0:T(8,128)(2,1)S(1)}, u32[]{:S(2)}, u32[]{:S(2)}) %collective-permute-start.16) | collective-permute-done | bytes 294944 | tf_op jit(solution)/shard_map/ppermute | solution.py:44
  73.4 1.9 collective-permute-start.19
  75.3 7.0 %collective-permute-done.19 = bf16[2,3,192,128]{3,2,1,0:T(8,128)(2,1)S(1)} collective-permute-done((bf16[2,3,192,128]{3,2,1,0:T(8,128)(2,1)S(1)}, bf16[2,3,192,128]{3,2,1,0:T(8,128)(2,1)S(1)}, u32[]{:S(2)}, u32[]{:S(2)}) %collective-permute-start.19) | collective-permute-done | bytes 294944 | tf_op jit(solution)/shard_map/ppermute | solution.py:44
  82.3 1.6 collective-permute-start.20
  84.0 6.2 %collective-permute-start.3 = (bf16[256,384]{1,0:T(8,128)(2,1)S(1)}, bf16[256,384]{1,0:T(8,128)(2,1)S(1)}, u32[]{:S(2)}, u32[]{:S(2)}) collective-permute-start(bf16[256,384]{1,0:T(8,128)(2,1)S(1)} %get-tuple-element.28), channel_id=1, source_target_pairs={{0,72},{1,73},{2,74},{3,75},{4,76},{5,77},{6,78},{7,79},{8,64},{9,... | collective-permute-start | bytes 589832 | tf_op jit(solution)/shard_map/ppermute | solution.py:44
  90.2 3.6 %collective-permute-start.1 = (bf16[256,384]{1,0:T(8,128)(2,1)S(1)}, bf16[256,384]{1,0:T(8,128)(2,1)S(1)}, u32[]{:S(2)}, u32[]{:S(2)}) collective-permute-start(bf16[256,384]{1,0:T(8,128)(2,1)S(1)} %get-tuple-element.27), channel_id=1, source_target_pairs={{0,64},{1,65},{2,66},{3,67},{4,68},{5,69},{6,70},{7,71},{8,72},{9,... | collective-permute-start | bytes 589832 | tf_op jit(solution)/shard_map/ppermute | solution.py:44
  93.8 6.3 %collective-permute-start.6 = (bf16[2,3,192,128]{3,2,1,0:T(8,128)(2,1)S(1)}, bf16[2,3,192,128]{3,2,1,0:T(8,128)(2,1)S(1)}, u32[]{:S(2)}, u32[]{:S(2)}) collective-permute-start(bf16[2,3,192,128]{3,2,1,0:T(8,128)(2,1)S(1)} %pad_maximum_fusion.15.refs_0_), channel_id=1, source_target_pairs={{0,384},{1,385},{2,386},{3,387},{4,388},{5,389},{6,390},{7,391},{8... | collective-permute-start | bytes 884744 | tf_op jit(solution)/shard_map/ppermute | solution.py:44
  100.1 1.9 collective-permute-start.5
  102.0 10.2 %collective-permute-done.3 = bf16[256,384]{1,0:T(8,128)(2,1)S(1)} collective-permute-done((bf16[256,384]{1,0:T(8,128)(2,1)S(1)}, bf16[256,384]{1,0:T(8,128)(2,1)S(1)}, u32[]{:S(2)}, u32[]{:S(2)}) %collective-permute-start.3) | collective-permute-done | bytes 196640 | tf_op jit(solution)/shard_map/ppermute | solution.py:44
  112.2 8.3 %collective-permute-start.4 = (bf16[256,384]{1,0:T(8,128)(2,1)S(1)}, bf16[256,384]{1,0:T(8,128)(2,1)S(1)}, u32[]{:S(2)}, u32[]{:S(2)}) collective-permute-start(bf16[256,384]{1,0:T(8,128)(2,1)S(1)} %collective-permute-done.3), channel_id=1, source_target_pairs={{0,72},{1,73},{2,74},{3,75},{4,76},{5,77},{6,78},{7,79},{8,64},{9,... | collective-permute-start | bytes 589832 | tf_op jit(solution)/shard_map/ppermute | solution.py:44
  120.5 1.9 collective-permute-start.2
  122.4 1.4 collective-permute-start.23
  123.8 0.7 slice.93
  124.5 7.9 %collective-permute-done.2 = bf16[256,384]{1,0:T(8,128)(2,1)S(1)} collective-permute-done((bf16[256,384]{1,0:T(8,128)(2,1)S(1)}, bf16[256,384]{1,0:T(8,128)(2,1)S(1)}, u32[]{:S(2)}, u32[]{:S(2)}) %collective-permute-start.2) | collective-permute-done | bytes 196640 | tf_op jit(solution)/shard_map/ppermute | solution.py:44
  132.4 0.8 pad_maximum_fusion.14
  133.3 1.5 select_select_fusion
  135.0 8.2 %collective-permute-start.12 = (bf16[5,3,192,128]{3,2,1,0:T(8,128)(2,1)S(1)}, bf16[5,3,192,128]{3,2,1,0:T(8,128)(2,1)S(1)}, u32[]{:S(2)}, u32[]{:S(2)}) collective-permute-start(bf16[5,3,192,128]{3,2,1,0:T(8,128)(2,1)S(1)} %get-tuple-element.25), channel_id=1, source_target_pairs={{0,384},{1,385},{2,386},{3,387},{4,388},{5,389},{6,390},{7,391},{8... | collective-permute-start | bytes 2211848 | tf_op jit(solution)/shard_map/ppermute | solution.py:44
  143.2 1.9 collective-permute-start.11
  145.1 11.9 %collective-permute-done.12.refs_5_ = bf16[5,3,192,128]{3,2,1,0:T(8,128)(2,1)S(1)} collective-permute-done((bf16[5,3,192,128]{3,2,1,0:T(8,128)(2,1)S(1)}, bf16[5,3,192,128]{3,2,1,0:T(8,128)(2,1)S(1)}, u32[]{:S(2)}, u32[]{:S(2)}) %collective-permute-start.12) | collective-permute-done | bytes 737312 | tf_op jit(solution)/shard_map/ppermute | solution.py:44
  157.0 0.9 copy-done.4
  157.9 5.0 %collective-permute-done.11.refs_4_ = bf16[5,3,192,128]{3,2,1,0:T(8,128)(2,1)S(1)} collective-permute-done((bf16[5,3,192,128]{3,2,1,0:T(8,128)(2,1)S(1)}, bf16[5,3,192,128]{3,2,1,0:T(8,128)(2,1)S(1)}, u32[]{:S(2)}, u32[]{:S(2)}) %collective-permute-start.11) | collective-permute-done | bytes 737312 | tf_op jit(solution)/shard_map/ppermute | solution.py:44
  162.9 0.9 copy-done.5
  164.0 1.9 collective-permute-start.18
  165.9 3.9 %collective-permute-start.17 = (bf16[6,3,192,128]{3,2,1,0:T(8,128)(2,1)S(1)}, bf16[6,3,192,128]{3,2,1,0:T(8,128)(2,1)S(1)}, u32[]{:S(2)}, u32[]{:S(2)}) collective-permute-start(bf16[6,3,192,128]{3,2,1,0:T(8,128)(2,1)S(1)} %get-tuple-element.24), channel_id=1, source_target_pairs={{0,128},{1,129},{2,130},{3,131},{4,132},{5,133},{6,134},{7,135},{8... | collective-permute-start | bytes 2654216 | tf_op jit(solution)/shard_map/ppermute | solution.py:44
  169.8 13.8 %collective-permute-done.18.refs_8_ = bf16[6,3,192,128]{3,2,1,0:T(8,128)(2,1)S(1)} collective-permute-done((bf16[6,3,192,128]{3,2,1,0:T(8,128)(2,1)S(1)}, bf16[6,3,192,128]{3,2,1,0:T(8,128)(2,1)S(1)}, u32[]{:S(2)}, u32[]{:S(2)}) %collective-permute-start.18) | collective-permute-done | bytes 884768 | tf_op jit(solution)/shard_map/ppermute | solution.py:44
  183.6 3.1 %collective-permute-done.17.refs_7_ = bf16[6,3,192,128]{3,2,1,0:T(8,128)(2,1)S(1)} collective-permute-done((bf16[6,3,192,128]{3,2,1,0:T(8,128)(2,1)S(1)}, bf16[6,3,192,128]{3,2,1,0:T(8,128)(2,1)S(1)}, u32[]{:S(2)}, u32[]{:S(2)}) %collective-permute-start.17) | collective-permute-done | bytes 884768 | tf_op jit(solution)/shard_map/ppermute | solution.py:44
  186.8 1.0 copy-done.3
  187.7 1.4 pad_maximum_fusion.5
  189.1 1.9 collective-permute-start.22
  191.1 3.9 %collective-permute-start.21 = (bf16[6,3,192,128]{3,2,1,0:T(8,128)(2,1)}, bf16[6,3,192,128]{3,2,1,0:T(8,128)(2,1)}, u32[]{:S(2)}, u32[]{:S(2)}) collective-permute-start(bf16[6,3,192,128]{3,2,1,0:T(8,128)(2,1)} %get-tuple-element.22), channel_id=1, source_target_pairs={{0,128},{1,129},{2,130},{3,131},{4,132},{5,133},{6,134},{7,135},{8... | collective-permute-start | bytes 2654216 | tf_op jit(solution)/shard_map/ppermute | solution.py:44
  195.0 0.7 dynamic-slice_bitcast_fusion
  195.9 12.0 %collective-permute-done.22.refs_11_ = bf16[6,3,192,128]{3,2,1,0:T(8,128)(2,1)} collective-permute-done((bf16[6,3,192,128]{3,2,1,0:T(8,128)(2,1)}, bf16[6,3,192,128]{3,2,1,0:T(8,128)(2,1)}, u32[]{:S(2)}, u32[]{:S(2)}) %collective-permute-start.22) | collective-permute-done | bytes 884768 | tf_op jit(solution)/shard_map/ppermute | solution.py:44
  207.8 1.0 fusion.12
  208.9 5.0 %collective-permute-done.21.refs_10_ = bf16[6,3,192,128]{3,2,1,0:T(8,128)(2,1)} collective-permute-done((bf16[6,3,192,128]{3,2,1,0:T(8,128)(2,1)}, bf16[6,3,192,128]{3,2,1,0:T(8,128)(2,1)}, u32[]{:S(2)}, u32[]{:S(2)}) %collective-permute-start.21) | collective-permute-done | bytes 884768 | tf_op jit(solution)/shard_map/ppermute | solution.py:44
  213.9 1.0 fusion.13
  214.9 1.2 fusion.1
  216.0 2.7 collective-permute-start.24
  218.7 4.3 %collective-permute-start.25 = (bf16[4,3,192,128]{3,2,1,0:T(8,128)(2,1)}, bf16[4,3,192,128]{3,2,1,0:T(8,128)(2,1)S(1)}, u32[]{:S(2)}, u32[]{:S(2)}) collective-permute-start(bf16[4,3,192,128]{3,2,1,0:T(8,128)(2,1)} %get-tuple-element.34), channel_id=1, source_target_pairs={{0,384},{1,385},{2,386},{3,387},{4,388},{5,389},{6,390},{7,391},{8... | collective-permute-start | bytes 1769480 | tf_op jit(solution)/shard_map/ppermute | solution.py:44
  224.2 0.9 pad_maximum_fusion.13.refs_9_
  225.1 1.2 pad_maximum_fusion.11
  226.3 2.9 %collective-permute-done.24.refs_1_ = bf16[4,3,192,128]{3,2,1,0:T(8,128)(2,1)S(1)} collective-permute-done((bf16[4,3,192,128]{3,2,1,0:T(8,128)(2,1)}, bf16[4,3,192,128]{3,2,1,0:T(8,128)(2,1)S(1)}, u32[]{:S(2)}, u32[]{:S(2)}) %collective-permute-start.24) | collective-permute-done | bytes 589856 | tf_op jit(solution)/shard_map/ppermute | solution.py:44
  229.2 1.9 collective-permute-start.26
  231.2 5.3 %collective-permute-start.27 = (bf16[1,3,192,128]{3,2,1,0:T(8,128)(2,1)S(1)}, bf16[1,3,192,128]{3,2,1,0:T(8,128)(2,1)S(1)}, u32[]{:S(2)}, u32[]{:S(2)}) collective-permute-start(bf16[1,3,192,128]{3,2,1,0:T(8,128)(2,1)S(1)} %slice.107), channel_id=1, source_target_pairs={{0,384},{1,385},{2,386},{3,387},{4,388},{5,389},{6,390},{7,391},{8... | collective-permute-start | bytes 442376 | tf_op jit(solution)/shard_map/ppermute | solution.py:44
  236.6 10.1 %shard_map.73.normed_ref = bf16[32,512,192]{2,1,0:T(8,128)(2,1)} custom-call(bf16[8,512,384]{2,1,0:T(8,128)(2,1)} %all-gather.4.cloned.1.call-done.own_ref, bf16[8,512,384]{2,1,0:T(8,128)(2,1)} %bitcast.20, f32[16,384]{1,0:T(8,128)} %fusion.2.gain_ref), custom_call_target="tpu_custom_call" | custom-call | flops 25165824 | bytes 14680064 | tf_op jit(solution)/shard_map/pallas_call | solution.py:101
  246.7 12.2 %shard_map.74.held_ref = f32[3,512,256]{2,1,0:T(8,128)} custom-call(s32[32]{0:T(128)} %fusion.3.index_ref, bf16[32,512,192]{2,1,0:T(8,128)(2,1)} %shard_map.73.normed_ref, bf16[2,3,192,128]{3,2,1,0:T(8,128)(2,1)} %copy-done.6, bf16[2,3,192,128]{3,2,1,0:T(8,128)(2,1)} %copy-done.10, bf16[2,3,192,128]{3,2,1,0:T(8,128)(2,1)} %copy-done.9, ...), custom_call_target="tpu_custom_call" | custom-call | flops 3925868544 | bytes 16056320 | tf_op jit(solution)/shard_map/pallas_call | solution.py:175
  258.9 6.6 %shard_map.75.held_ref = f32[3,512,256]{2,1,0:T(8,128)} custom-call(s32[32]{0:T(128)} %fusion.3.index_ref, bf16[32,512,192]{2,1,0:T(8,128)(2,1)} %shard_map.73.normed_ref, f32[3,512,256]{2,1,0:T(8,128)} %shard_map.74.held_ref, bf16[2,3,192,128]{3,2,1,0:T(8,128)(2,1)} %copy-done.1, bf16[4,3,192,128]{3,2,1,0:T(8,128)(2,1)} %copy-done.7, ...), custom_call_target="tpu_custom_call" | custom-call | flops 754974720 | bytes 9863168 | tf_op jit(solution)/shard_map/pallas_call | solution.py:175
  266.2 0.7 copy-done.18
  266.8 6.2 %shard_map.76 = bf16[512,256]{1,0:T(8,128)(2,1)} custom-call(s32[32]{0:T(128)} %fusion.3.index_ref, bf16[32,512,192]{2,1,0:T(8,128)(2,1)} %shard_map.73.normed_ref, f32[3,512,256]{2,1,0:T(8,128)} %shard_map.75.held_ref, f32[2,256]{1,0:T(2,128)} %gain_ref.1, bf16[1,3,192,128]{3,2,1,0:T(8,128)(2,1)} %copy-done.17, bf16[1,3,192,128]{3,2,1,0:T(8,128)(2,1)} %copy-done.18), custom_call_target="tpu_custom_call" | custom-call | flops 150994944 | bytes 8683520 | tf_op jit(solution)/shard_map/pallas_call | solution.py:175
  (76 shorter events, 4.6 us)
Async XLA Ops:
  6.5 230.0 %all-gather.4.cloned.1.call-start = ((), (), s32[]{:S(2)}) async-start(), calls=%async_computation | async-start | bytes 3538944 | tf_op jit(solution)/shard_map/all_gather | solution.py:231
  6.5 13.1 %collective-permute-start = (bf16[2,256,384]{2,1,0:T(8,128)(2,1)}, bf16[2,256,384]{2,1,0:T(8,128)(2,1)S(1)}, u32[]{:S(2)}, u32[]{:S(2)}) collective-permute-start(bf16[2,256,384]{2,1,0:T(8,128)(2,1)} %param.7), channel_id=1, source_target_pairs={{0,496},{1,497},{2,498},{3,499},{4,500},{5,501},{6,502},{7,503},{8... | collective-permute-start | bytes 1179656 | tf_op jit(solution)/shard_map/ppermute | solution.py:44
  21.8 62.2 %copy-start = (bf16[2,256,384]{2,1,0:T(8,128)(2,1)S(1)}, bf16[2,256,384]{2,1,0:T(8,128)(2,1)}, u32[]{:S(2)}) copy-start(bf16[2,256,384]{2,1,0:T(8,128)(2,1)} %add_convert_fusion) | copy-start | bytes 1179652
  21.8 214.8 %all-gather.6.cloned.1.call-start = ((), (), s32[]{:S(2)}) async-start(), calls=%async_computation.1 | async-start | bytes 3538944 | tf_op jit(solution)/shard_map/all_gather | solution.py:232
  22.9 111.9 %copy-start.6 = (bf16[2,3,192,128]{3,2,1,0:T(8,128)(2,1)}, bf16[2,3,192,128]{3,2,1,0:T(8,128)(2,1)S(1)}, u32[]{:S(2)}) copy-start(bf16[2,3,192,128]{3,2,1,0:T(8,128)(2,1)S(1)} %pad_maximum_fusion.15.refs_0_) | copy-start | bytes 884740
  22.9 14.0 %collective-permute-start.9 = (bf16[2,3,192,128]{3,2,1,0:T(8,128)(2,1)S(1)}, bf16[2,3,192,128]{3,2,1,0:T(8,128)(2,1)S(1)}, u32[]{:S(2)}, u32[]{:S(2)}) collective-permute-start(bf16[2,3,192,128]{3,2,1,0:T(8,128)(2,1)S(1)} %pad_maximum_fusion.15.refs_0_), channel_id=1, source_target_pairs={{0,16},{1,17},{2,18},{3,19},{4,20},{5,21},{6,22},{7,23},{8,24},{9,... | collective-permute-start | bytes 884744 | tf_op jit(solution)/shard_map/ppermute | solution.py:44
  28.0 12.4 %collective-permute-start.7 = (bf16[2,3,192,128]{3,2,1,0:T(8,128)(2,1)S(1)}, bf16[2,3,192,128]{3,2,1,0:T(8,128)(2,1)S(1)}, u32[]{:S(2)}, u32[]{:S(2)}) collective-permute-start(bf16[2,3,192,128]{3,2,1,0:T(8,128)(2,1)S(1)} %pad_maximum_fusion.15.refs_0_), channel_id=1, source_target_pairs={{16,0},{17,1},{18,2},{19,3},{20,4},{21,5},{22,6},{23,7},{24,8},{25... | collective-permute-start | bytes 884744 | tf_op jit(solution)/shard_map/ppermute | solution.py:44
  36.9 28.1 %copy-start.12 = (bf16[2,3,192,128]{3,2,1,0:T(8,128)(2,1)}, bf16[2,3,192,128]{3,2,1,0:T(8,128)(2,1)S(1)}, u32[]{:S(2)}) copy-start(bf16[2,3,192,128]{3,2,1,0:T(8,128)(2,1)S(1)} %collective-permute-done.9) | copy-start | bytes 884740
  36.9 11.4 %collective-permute-start.10 = (bf16[2,3,192,128]{3,2,1,0:T(8,128)(2,1)S(1)}, bf16[2,3,192,128]{3,2,1,0:T(8,128)(2,1)S(1)}, u32[]{:S(2)}, u32[]{:S(2)}) collective-permute-start(bf16[2,3,192,128]{3,2,1,0:T(8,128)(2,1)S(1)} %collective-permute-done.9), channel_id=1, source_target_pairs={{16,32},{17,33},{18,34},{19,35},{20,36},{21,37},{22,38},{23,39},{2... | collective-permute-start | bytes 884744 | tf_op jit(solution)/shard_map/ppermute | solution.py:44
  40.4 11.5 %collective-permute-start.8 = (bf16[2,3,192,128]{3,2,1,0:T(8,128)(2,1)S(1)}, bf16[2,3,192,128]{3,2,1,0:T(8,128)(2,1)S(1)}, u32[]{:S(2)}, u32[]{:S(2)}) collective-permute-start(bf16[2,3,192,128]{3,2,1,0:T(8,128)(2,1)S(1)} %collective-permute-done.7), channel_id=1, source_target_pairs={{16,0},{17,1},{18,2},{19,3},{20,4},{21,5},{22,6},{23,7},{24,8},{25... | collective-permute-start | bytes 884744 | tf_op jit(solution)/shard_map/ppermute | solution.py:44
  48.2 8.7 %collective-permute-start.14 = (bf16[2,3,192,128]{3,2,1,0:T(8,128)(2,1)S(1)}, bf16[2,3,192,128]{3,2,1,0:T(8,128)(2,1)S(1)}, u32[]{:S(2)}, u32[]{:S(2)}) collective-permute-start(bf16[2,3,192,128]{3,2,1,0:T(8,128)(2,1)S(1)} %collective-permute-done.10), channel_id=1, source_target_pairs={{32,48},{33,49},{34,50},{35,51},{36,52},{37,53},{38,54},{39,55},{4... | collective-permute-start | bytes 884744 | tf_op jit(solution)/shard_map/ppermute | solution.py:44
  51.9 13.1 %copy-start.13 = (bf16[2,3,192,128]{3,2,1,0:T(8,128)(2,1)}, bf16[2,3,192,128]{3,2,1,0:T(8,128)(2,1)S(1)}, u32[]{:S(2)}) copy-start(bf16[2,3,192,128]{3,2,1,0:T(8,128)(2,1)S(1)} %collective-permute-done.8) | copy-start | bytes 884740
  51.9 11.2 %collective-permute-start.13 = (bf16[2,3,192,128]{3,2,1,0:T(8,128)(2,1)S(1)}, bf16[2,3,192,128]{3,2,1,0:T(8,128)(2,1)S(1)}, u32[]{:S(2)}, u32[]{:S(2)}) collective-permute-start(bf16[2,3,192,128]{3,2,1,0:T(8,128)(2,1)S(1)} %collective-permute-done.8), channel_id=1, source_target_pairs={{16,0},{17,1},{18,2},{19,3},{20,4},{21,5},{22,6},{23,7},{24,8},{25... | collective-permute-start | bytes 884744 | tf_op jit(solution)/shard_map/ppermute | solution.py:44
  57.0 33.2 %copy-start.14 = (bf16[2,3,192,128]{3,2,1,0:T(8,128)(2,1)}, bf16[2,3,192,128]{3,2,1,0:T(8,128)(2,1)S(1)}, u32[]{:S(2)}) copy-start(bf16[2,3,192,128]{3,2,1,0:T(8,128)(2,1)S(1)} %collective-permute-done.14) | copy-start | bytes 884740
  57.0 8.0 %collective-permute-start.15 = (bf16[2,3,192,128]{3,2,1,0:T(8,128)(2,1)S(1)}, bf16[2,3,192,128]{3,2,1,0:T(8,128)(2,1)S(1)}, u32[]{:S(2)}, u32[]{:S(2)}) collective-permute-start(bf16[2,3,192,128]{3,2,1,0:T(8,128)(2,1)S(1)} %collective-permute-done.14), channel_id=1, source_target_pairs={{48,64},{49,65},{50,66},{51,67},{52,68},{53,69},{54,70},{55,71},{5... | collective-permute-start | bytes 884744 | tf_op jit(solution)/shard_map/ppermute | solution.py:44
  63.0 10.2 %collective-permute-start.16 = (bf16[2,3,192,128]{3,2,1,0:T(8,128)(2,1)S(1)}, bf16[2,3,192,128]{3,2,1,0:T(8,128)(2,1)S(1)}, u32[]{:S(2)}, u32[]{:S(2)}) collective-permute-start(bf16[2,3,192,128]{3,2,1,0:T(8,128)(2,1)S(1)} %collective-permute-done.13), channel_id=1, source_target_pairs={{16,0},{17,1},{18,2},{19,3},{20,4},{21,5},{22,6},{23,7},{24,8},{25... | collective-permute-start | bytes 884744 | tf_op jit(solution)/shard_map/ppermute | solution.py:44
  73.4 8.9 %collective-permute-start.19 = (bf16[2,3,192,128]{3,2,1,0:T(8,128)(2,1)S(1)}, bf16[2,3,192,128]{3,2,1,0:T(8,128)(2,1)S(1)}, u32[]{:S(2)}, u32[]{:S(2)}) collective-permute-start(bf16[2,3,192,128]{3,2,1,0:T(8,128)(2,1)S(1)} %get-tuple-element.6), channel_id=1, source_target_pairs={{16,0},{17,1},{18,2},{19,3},{20,4},{21,5},{22,6},{23,7},{24,8},{25... | collective-permute-start | bytes 884744 | tf_op jit(solution)/shard_map/ppermute | solution.py:44
  82.3 50.9 %copy-start.15 = (bf16[2,3,192,128]{3,2,1,0:T(8,128)(2,1)}, bf16[2,3,192,128]{3,2,1,0:T(8,128)(2,1)S(1)}, u32[]{:S(2)}) copy-start(bf16[2,3,192,128]{3,2,1,0:T(8,128)(2,1)S(1)} %collective-permute-done.19) | copy-start | bytes 884740
  82.3 40.1 %collective-permute-start.20 = (bf16[2,3,192,128]{3,2,1,0:T(8,128)(2,1)S(1)}, bf16[2,3,192,128]{3,2,1,0:T(8,128)(2,1)S(1)}, u32[]{:S(2)}, u32[]{:S(2)}) collective-permute-start(bf16[2,3,192,128]{3,2,1,0:T(8,128)(2,1)S(1)} %collective-permute-done.19), channel_id=1, source_target_pairs={{16,0},{17,1},{18,2},{19,3},{20,4},{21,5},{22,6},{23,7},{24,8},{25... | collective-permute-start | bytes 884744 | tf_op jit(solution)/shard_map/ppermute | solution.py:44
  84.0 28.2 %collective-permute-start.3 = (bf16[256,384]{1,0:T(8,128)(2,1)S(1)}, bf16[256,384]{1,0:T(8,128)(2,1)S(1)}, u32[]{:S(2)}, u32[]{:S(2)}) collective-permute-start(bf16[256,384]{1,0:T(8,128)(2,1)S(1)} %get-tuple-element.28), channel_id=1, source_target_pairs={{0,72},{1,73},{2,74},{3,75},{4,76},{5,77},{6,78},{7,79},{8,64},{9,... | collective-permute-start | bytes 589832 | tf_op jit(solution)/shard_map/ppermute | solution.py:44
  90.2 30.3 %collective-permute-start.1 = (bf16[256,384]{1,0:T(8,128)(2,1)S(1)}, bf16[256,384]{1,0:T(8,128)(2,1)S(1)}, u32[]{:S(2)}, u32[]{:S(2)}) collective-permute-start(bf16[256,384]{1,0:T(8,128)(2,1)S(1)} %get-tuple-element.27), channel_id=1, source_target_pairs={{0,64},{1,65},{2,66},{3,67},{4,68},{5,69},{6,70},{7,71},{8,72},{9,... | collective-permute-start | bytes 589832 | tf_op jit(solution)/shard_map/ppermute | solution.py:44
  93.8 30.1 %collective-permute-start.6 = (bf16[2,3,192,128]{3,2,1,0:T(8,128)(2,1)S(1)}, bf16[2,3,192,128]{3,2,1,0:T(8,128)(2,1)S(1)}, u32[]{:S(2)}, u32[]{:S(2)}) collective-permute-start(bf16[2,3,192,128]{3,2,1,0:T(8,128)(2,1)S(1)} %pad_maximum_fusion.15.refs_0_), channel_id=1, source_target_pairs={{0,384},{1,385},{2,386},{3,387},{4,388},{5,389},{6,390},{7,391},{8... | collective-permute-start | bytes 884744 | tf_op jit(solution)/shard_map/ppermute | solution.py:44
  100.1 24.5 %collective-permute-start.5 = (bf16[2,3,192,128]{3,2,1,0:T(8,128)(2,1)S(1)}, bf16[2,3,192,128]{3,2,1,0:T(8,128)(2,1)S(1)}, u32[]{:S(2)}, u32[]{:S(2)}) collective-permute-start(bf16[2,3,192,128]{3,2,1,0:T(8,128)(2,1)S(1)} %pad_maximum_fusion.15.refs_0_), channel_id=1, source_target_pairs={{0,128},{1,129},{2,130},{3,131},{4,132},{5,133},{6,134},{7,135},{8... | collective-permute-start | bytes 884744 | tf_op jit(solution)/shard_map/ppermute | solution.py:44
  112.2 12.4 %collective-permute-start.4 = (bf16[256,384]{1,0:T(8,128)(2,1)S(1)}, bf16[256,384]{1,0:T(8,128)(2,1)S(1)}, u32[]{:S(2)}, u32[]{:S(2)}) collective-permute-start(bf16[256,384]{1,0:T(8,128)(2,1)S(1)} %collective-permute-done.3), channel_id=1, source_target_pairs={{0,72},{1,73},{2,74},{3,75},{4,76},{5,77},{6,78},{7,79},{8,64},{9,... | collective-permute-start | bytes 589832 | tf_op jit(solution)/shard_map/ppermute | solution.py:44
  120.5 11.9 %collective-permute-start.2 = (bf16[256,384]{1,0:T(8,128)(2,1)S(1)}, bf16[256,384]{1,0:T(8,128)(2,1)S(1)}, u32[]{:S(2)}, u32[]{:S(2)}) collective-permute-start(bf16[256,384]{1,0:T(8,128)(2,1)S(1)} %collective-permute-done.1), channel_id=1, source_target_pairs={{0,64},{1,65},{2,66},{3,67},{4,68},{5,69},{6,70},{7,71},{8,72},{9,... | collective-permute-start | bytes 589832 | tf_op jit(solution)/shard_map/ppermute | solution.py:44
  122.4 10.8 %copy-start.16 = (bf16[2,3,192,128]{3,2,1,0:T(8,128)(2,1)}, bf16[2,3,192,128]{3,2,1,0:T(8,128)(2,1)S(1)}, u32[]{:S(2)}) copy-start(bf16[2,3,192,128]{3,2,1,0:T(8,128)(2,1)S(1)} %collective-permute-done.20) | copy-start | bytes 884740
  122.4 10.8 %collective-permute-start.23 = (bf16[2,3,192,128]{3,2,1,0:T(8,128)(2,1)S(1)}, bf16[2,3,192,128]{3,2,1,0:T(8,128)(2,1)}, u32[]{:S(2)}, u32[]{:S(2)}) collective-permute-start(bf16[2,3,192,128]{3,2,1,0:T(8,128)(2,1)S(1)} %collective-permute-done.20), channel_id=1, source_target_pairs={{16,0},{17,1},{18,2},{19,3},{20,4},{21,5},{22,6},{23,7},{24,8},{25... | collective-permute-start | bytes 884744 | tf_op jit(solution)/shard_map/ppermute | solution.py:44
  123.8 11.2 %copy-start.9 = (bf16[2,3,192,128]{3,2,1,0:T(8,128)(2,1)}, bf16[2,3,192,128]{3,2,1,0:T(8,128)(2,1)S(1)}, u32[]{:S(2)}) copy-start(bf16[2,3,192,128]{3,2,1,0:T(8,128)(2,1)S(1)} %collective-permute-done.6.refs_2_) | copy-start | bytes 884740
  124.5 8.7 %copy-start.10 = (bf16[2,3,192,128]{3,2,1,0:T(8,128)(2,1)}, bf16[2,3,192,128]{3,2,1,0:T(8,128)(2,1)S(1)}, u32[]{:S(2)}) copy-start(bf16[2,3,192,128]{3,2,1,0:T(8,128)(2,1)S(1)} %collective-permute-done.5.refs_1_) | copy-start | bytes 884740
  133.3 1.6 copy-start.11
  133.3 1.6 slice-start
  134.8 80.0 %copy-start.1 = (bf16[2,3,192,128]{3,2,1,0:T(8,128)(2,1)}, bf16[2,3,192,128]{3,2,1,0:T(8,128)(2,1)S(1)}, u32[]{:S(2)}) copy-start(bf16[2,3,192,128]{3,2,1,0:T(8,128)(2,1)S(1)} %get-tuple-element.11.refs_0_) | copy-start | bytes 884740
  135.0 22.0 %collective-permute-start.12 = (bf16[5,3,192,128]{3,2,1,0:T(8,128)(2,1)S(1)}, bf16[5,3,192,128]{3,2,1,0:T(8,128)(2,1)S(1)}, u32[]{:S(2)}, u32[]{:S(2)}) collective-permute-start(bf16[5,3,192,128]{3,2,1,0:T(8,128)(2,1)S(1)} %get-tuple-element.25), channel_id=1, source_target_pairs={{0,384},{1,385},{2,386},{3,387},{4,388},{5,389},{6,390},{7,391},{8... | collective-permute-start | bytes 2211848 | tf_op jit(solution)/shard_map/ppermute | solution.py:44
  143.2 19.7 %collective-permute-start.11 = (bf16[5,3,192,128]{3,2,1,0:T(8,128)(2,1)S(1)}, bf16[5,3,192,128]{3,2,1,0:T(8,128)(2,1)S(1)}, u32[]{:S(2)}, u32[]{:S(2)}) collective-permute-start(bf16[5,3,192,128]{3,2,1,0:T(8,128)(2,1)S(1)} %get-tuple-element.26), channel_id=1, source_target_pairs={{0,128},{1,129},{2,130},{3,131},{4,132},{5,133},{6,134},{7,135},{8... | collective-permute-start | bytes 2211848 | tf_op jit(solution)/shard_map/ppermute | solution.py:44
  157.0 0.9 copy-start.4
  162.9 0.9 copy-start.5
  164.0 19.6 %collective-permute-start.18 = (bf16[6,3,192,128]{3,2,1,0:T(8,128)(2,1)S(1)}, bf16[6,3,192,128]{3,2,1,0:T(8,128)(2,1)S(1)}, u32[]{:S(2)}, u32[]{:S(2)}) collective-permute-start(bf16[6,3,192,128]{3,2,1,0:T(8,128)(2,1)S(1)} %get-tuple-element.23), channel_id=1, source_target_pairs={{0,384},{1,385},{2,386},{3,387},{4,388},{5,389},{6,390},{7,391},{8... | collective-permute-start | bytes 2654216 | tf_op jit(solution)/shard_map/ppermute | solution.py:44
  165.9 20.8 %collective-permute-start.17 = (bf16[6,3,192,128]{3,2,1,0:T(8,128)(2,1)S(1)}, bf16[6,3,192,128]{3,2,1,0:T(8,128)(2,1)S(1)}, u32[]{:S(2)}, u32[]{:S(2)}) collective-permute-start(bf16[6,3,192,128]{3,2,1,0:T(8,128)(2,1)S(1)} %get-tuple-element.24), channel_id=1, source_target_pairs={{0,128},{1,129},{2,130},{3,131},{4,132},{5,133},{6,134},{7,135},{8... | collective-permute-start | bytes 2654216 | tf_op jit(solution)/shard_map/ppermute | solution.py:44
  183.6 32.4 %copy-start.2 = (bf16[6,3,192,128]{3,2,1,0:T(8,128)(2,1)}, bf16[6,3,192,128]{3,2,1,0:T(8,128)(2,1)S(1)}, u32[]{:S(2)}) copy-start(bf16[6,3,192,128]{3,2,1,0:T(8,128)(2,1)S(1)} %collective-permute-done.18.refs_8_) | copy-start | bytes 2654212
  186.8 1.0 copy-start.3
  187.7 35.9 %copy-start.19 = (f32[6144]{0:T(1024)S(1)}, f32[6144]{0:T(1024)}, u32[]{:S(2)}) copy-start(f32[6144]{0:T(1024)} %param.10) | copy-start | bytes 73732
  189.1 18.7 %collective-permute-start.22 = (bf16[6,3,192,128]{3,2,1,0:T(8,128)(2,1)}, bf16[6,3,192,128]{3,2,1,0:T(8,128)(2,1)}, u32[]{:S(2)}, u32[]{:S(2)}) collective-permute-start(bf16[6,3,192,128]{3,2,1,0:T(8,128)(2,1)} %get-tuple-element.21), channel_id=1, source_target_pairs={{0,384},{1,385},{2,386},{3,387},{4,388},{5,389},{6,390},{7,391},{8... | collective-permute-start | bytes 2654216 | tf_op jit(solution)/shard_map/ppermute | solution.py:44
  191.1 22.8 %collective-permute-start.21 = (bf16[6,3,192,128]{3,2,1,0:T(8,128)(2,1)}, bf16[6,3,192,128]{3,2,1,0:T(8,128)(2,1)}, u32[]{:S(2)}, u32[]{:S(2)}) collective-permute-start(bf16[6,3,192,128]{3,2,1,0:T(8,128)(2,1)} %get-tuple-element.22), channel_id=1, source_target_pairs={{0,128},{1,129},{2,130},{3,131},{4,132},{5,133},{6,134},{7,135},{8... | collective-permute-start | bytes 2654216 | tf_op jit(solution)/shard_map/ppermute | solution.py:44
  216.0 13.2 %collective-permute-start.24 = (bf16[4,3,192,128]{3,2,1,0:T(8,128)(2,1)}, bf16[4,3,192,128]{3,2,1,0:T(8,128)(2,1)S(1)}, u32[]{:S(2)}, u32[]{:S(2)}) collective-permute-start(bf16[4,3,192,128]{3,2,1,0:T(8,128)(2,1)} %get-tuple-element.35), channel_id=1, source_target_pairs={{0,128},{1,129},{2,130},{3,131},{4,132},{5,133},{6,134},{7,135},{8... | collective-permute-start | bytes 1769480 | tf_op jit(solution)/shard_map/ppermute | solution.py:44
  218.7 12.4 %collective-permute-start.25 = (bf16[4,3,192,128]{3,2,1,0:T(8,128)(2,1)}, bf16[4,3,192,128]{3,2,1,0:T(8,128)(2,1)S(1)}, u32[]{:S(2)}, u32[]{:S(2)}) collective-permute-start(bf16[4,3,192,128]{3,2,1,0:T(8,128)(2,1)} %get-tuple-element.34), channel_id=1, source_target_pairs={{0,384},{1,385},{2,386},{3,387},{4,388},{5,389},{6,390},{7,391},{8... | collective-permute-start | bytes 1769480 | tf_op jit(solution)/shard_map/ppermute | solution.py:44
  229.2 17.5 %copy-start.7 = (bf16[4,3,192,128]{3,2,1,0:T(8,128)(2,1)}, bf16[4,3,192,128]{3,2,1,0:T(8,128)(2,1)S(1)}, u32[]{:S(2)}) copy-start(bf16[4,3,192,128]{3,2,1,0:T(8,128)(2,1)S(1)} %collective-permute-done.24.refs_1_) | copy-start | bytes 1769476
  229.2 36.3 %collective-permute-start.26 = (bf16[1,3,192,128]{3,2,1,0:T(8,128)(2,1)S(1)}, bf16[1,3,192,128]{3,2,1,0:T(8,128)(2,1)S(1)}, u32[]{:S(2)}, u32[]{:S(2)}) collective-permute-start(bf16[1,3,192,128]{3,2,1,0:T(8,128)(2,1)S(1)} %slice.106), channel_id=1, source_target_pairs={{0,128},{1,129},{2,130},{3,131},{4,132},{5,133},{6,134},{7,135},{8... | collective-permute-start | bytes 442376 | tf_op jit(solution)/shard_map/ppermute | solution.py:44
  231.2 15.5 %copy-start.8 = (bf16[4,3,192,128]{3,2,1,0:T(8,128)(2,1)}, bf16[4,3,192,128]{3,2,1,0:T(8,128)(2,1)S(1)}, u32[]{:S(2)}) copy-start(bf16[4,3,192,128]{3,2,1,0:T(8,128)(2,1)S(1)} %collective-permute-done.25.refs_2_) | copy-start | bytes 1769476
  231.2 34.3 %collective-permute-start.27 = (bf16[1,3,192,128]{3,2,1,0:T(8,128)(2,1)S(1)}, bf16[1,3,192,128]{3,2,1,0:T(8,128)(2,1)S(1)}, u32[]{:S(2)}, u32[]{:S(2)}) collective-permute-start(bf16[1,3,192,128]{3,2,1,0:T(8,128)(2,1)S(1)} %slice.107), channel_id=1, source_target_pairs={{0,384},{1,385},{2,386},{3,387},{4,388},{5,389},{6,390},{7,391},{8... | collective-permute-start | bytes 442376 | tf_op jit(solution)/shard_map/ppermute | solution.py:44
  265.5 0.7 copy-start.17
  266.2 0.7 copy-start.18
Sparse Core Ops, SparseCore 0:
  21.9 43.8 all-gather.3
  133.4 34.4 all-gather.5

commit v3 on v2

--- a/solution.py
+++ b/solution.py
@@ -11,7 +11,7 @@
 HEAD = 128
 AXES = ("x", "zl", "zh", "y", "c")
 SIZES = (4, 8, 2, 4, 2)
-VMEM_LIMIT = 56 * 1024 * 1024
+VMEM_LIMIT = 32 * 1024 * 1024
 
 SLOT_SOURCES = np.array(
     [
@@ -187,33 +187,84 @@
     )(index, normed, *extra, *pieces)
 
 
-def weight_slots(own, zl):
+def relay_kernel(slots, forward, zl_ref, *refs):
+    *sources, left_ref, right_ref, to_right, to_left = refs
+    zl = zl_ref[0]
+    for place, choices in enumerate(slots):
+        for source, rows in choices:
+            chosen = functools.reduce(jnp.logical_or, [zl == row for row in rows])
+
+            @pl.when(chosen)
+            def _(source=source, place=place):
+                block = sources[source][...]
+                to_right[2 * place : 2 * place + 2] = block
+                to_left[2 * place : 2 * place + 2] = block
+
+    for place in range(forward):
+        to_right[2 * len(slots) + place] = left_ref[2 * place]
+        to_left[2 * len(slots) + place] = right_ref[2 * place + 1]
+
+
+def relay(zl, slots, arrays, left, right, forward):
+    whole = pl.BlockSpec(memory_space=pltpu.VMEM)
+    message = jax.ShapeDtypeStruct((2 * len(slots) + forward, 3, 192, HEAD), jnp.bfloat16)
+    return pl.pallas_call(
+        functools.partial(relay_kernel, slots, forward),
+        out_shape=(message, message),
+        in_specs=[pl.BlockSpec(memory_space=pltpu.SMEM)] + [whole] * (len(arrays) + 2),
+        out_specs=(whole, whole),
+        compiler_params=pltpu.CompilerParams(vmem_limit_bytes=16 * 2**20),
+        cost_estimate=pl.CostEstimate(flops=0, bytes_accessed=4 * 2**20, transcendentals=0),
+    )(zl, *arrays, left, right)
+
+
+def gather_weights(own, zl):
+    row = zl.reshape(1)
+    left, right, sent = [along_x(own, 1)], [along_x(own, -1)], [(own, own)]
+
+    def group(slots, arrays):
+        forward = left[-1].shape[0] // 2 if len(left) == 1 else 2
+        to_right, to_left = relay(row, slots, arrays, left[-1], right[-1], forward)
+        sent.append((to_right, to_left))
+        left.append(along_x(to_right, 1))
+        right.append(along_x(to_left, -1))
+
     a1 = along_line(own, up=range(0, 7))
     b1 = along_line(own, down=range(1, 8))
     a2 = along_line(a1, up=range(1, 7))
     b2 = along_line(b1, down=range(1, 7))
+    group(
+        [[(0, range(1, 8)), (3, (0,))], [(1, range(0, 7)), (2, (7,))]],
+        [a1, b1, a2, b2],
+    )
     a3 = along_line(a2, up=range(2, 7))
     b3 = along_line(b2, down=range(1, 6))
     a4 = along_line(a3, up=range(3, 7))
     b4 = along_line(b3, down=range(1, 5))
     m4 = jnp.where(zl >= 4, a4, b4)
+    group(
+        [
+            [(0, range(2, 7)), (3, (0, 1)), (4, (7,))],
+            [(1, range(1, 6)), (2, (6, 7)), (4, (0,))],
+        ],
+        [a2, b2, a3, b3, m4],
+    )
     m5 = along_line(m4, up=range(4, 7), down=range(1, 4))
     m6 = along_line(m5, up=range(5, 7), down=range(1, 3))
+    group(
+        [
+            [(0, range(1, 7)), (1, (0, 7))],
+            [(1, (1, 2, 5, 6)), (2, (0, 7)), (3, (4,)), (4, (3,))],
+        ],
+        [m4, m5, m6, a3, b3],
+    )
     m7 = along_line(m6, up=(6,), down=(1,))
-    end = (zl == 0) | (zl == 7)
-    second = (zl == 1) | (zl == 6)
-    return [
-        own,
-        jnp.where(zl == 0, b2, a1),
-        jnp.where(zl == 7, a2, b1),
-        jnp.where(zl <= 1, b3, jnp.where(zl == 7, m4, a2)),
-        jnp.where(zl == 0, m4, jnp.where(zl <= 5, b2, a3)),
-        jnp.where(end, m5, m4),
-        jnp.where(end, m6, jnp.where(zl == 3, b3, jnp.where(zl == 4, a3, m5))),
-        jnp.where(
-            end, m7, jnp.where(second, m6, jnp.where((zl == 2) | (zl == 4), b3, a3))
-        ),
-    ]
+    group(
+        [[(0, (0, 7)), (1, (1, 6)), (2, (3, 5)), (3, (2, 4))]],
+        [m7, m6, a3, b3],
+    )
+    last = along_x(left[-1][0:1], 1), along_x(right[-1][1:2], -1)
+    return sent, left, right, last
 
 
 def per_device(tokens, mix_weight, partner_offset, ln_gain, qkv_weight, qk_gain):
@@ -232,21 +283,7 @@
     other_features = lax.all_gather(jnp.concatenate([ahead, behind]), ("y", "c"))
 
     halves = jnp.stack([qkv_weight[:, :, :HEAD], qkv_weight[:, :, HEAD:]])
-    slots = weight_slots(halves, zl)
-    own, left, right = [], [], []
-    for group in ((0,), (1, 2), (3, 4), (5, 6), (7,)):
-        block = jnp.concatenate([slots[slot] for slot in group])
-        to_right, to_left = [block], [block]
-        if left:
-            full = left[-1].shape[0] // 2 * 2 if len(left) == 1 else 4
-            for start in range(0, full, 2):
-                to_right.append(left[-1][start : start + 1])
-                to_left.append(right[-1][start + 1 : start + 2])
-        own.append(block)
-        left.append(along_x(jnp.concatenate(to_right), 1))
-        right.append(along_x(jnp.concatenate(to_left), -1))
-    last_left = along_x(left[-1][0:1], 1)
-    last_right = along_x(right[-1][1:2], -1)
+    sent, left, right, (last_left, last_right) = gather_weights(halves, zl)
 
     sources = jnp.asarray(SLOT_SOURCES)[zl]
     block_of = ((x + jnp.arange(4, dtype=jnp.int32)) % 4 * 8)[:, None] + sources[None, :]
@@ -281,12 +318,12 @@
             tail = 2 * len(slots_in) + place
             blocks.append((16 + slot, ((1, tail), (2, tail))))
         first_blocks += at(blocks, 3 * group)
-        pieces += [own[group], left[group], right[group]]
+        pieces += [sent[group][0], left[group], right[group]]
     acc_shape = jax.ShapeDtypeStruct((3, 512, 256), jnp.float32)
     acc = project(first_kernel, first_blocks, index, normed, [], pieces, acc_shape)
     blocks = three(7, 0) + [(16 + 5, ((1, 2), (2, 2))), (16 + 6, ((1, 3), (2, 3)))]
     acc = project(
-        next_kernel, blocks, index, normed, [acc], [own[4], left[4], right[4]], acc_shape
+        next_kernel, blocks, index, normed, [acc], [sent[4][0], left[4], right[4]], acc_shape
     )
     out = project(
         last_kernel,

time: 281 us -> 243 us (0.86)
  the two profiles are of different devices: /device:TPU:80 before, /device:TPU:6 now
where the time goes in v3:
time: 243 us; the launch traced here: 241 us
  starting transfers between devices  96.5 us (40%)
  waiting for transfers between devices  84 us (35%)
  Pallas kernels  24.9 us (10%)
  local copies, waits for them, and re-layouts  14.8 us (6%)
  between operations  14 us (6%)
  other arithmetic  6.7 us (3%)
    ppermute x28, starting transfers between devices, move(): return lax.ppermute(value, AXES, pairs)  96.5 us
    ppermute x28, waiting for transfers between devices, move(): return lax.ppermute(value, AXES, pairs)  83.9 us
    pallas_call x3, Pallas kernels, project(): pl.pallas_call(functools.partial(kernel, blocks), out_shape=out_shape, in...  12.6 us
    unnamed x48, local copies, waits for them, and re-layouts  8.37 us
    pallas_call x1, Pallas kernels, norm_tokens(): pl.pallas_call(norm_kernel, out_shape=jax.ShapeDtypeStruct((32, 512, 192)...  6.42 us
    pallas_call x4, Pallas kernels, relay(): pl.pallas_call(functools.partial(relay_kernel, slots, forward), out_shape...  5.91 us
  transfers between devices with their start and end apart: 30, of which 17 were waited for; matrix products, arithmetic and copies ran while one was open for 5% of the time, Pallas kernels for 9%

profile of v3, /device:TPU:6, one launch (start us, length us, event | category | flops | bytes accessed | tf_op | source)
XLA Modules:
  0.0 240.9 jit_solution(1005141659207465253)
XLA Ops:
  6.5 13.5 %collective-permute-start = (bf16[2,256,384]{2,1,0:T(8,128)(2,1)}, bf16[2,256,384]{2,1,0:T(8,128)(2,1)S(1)}, u32[]{:S(2)}, u32[]{:S(2)}) collective-permute-start(bf16[2,256,384]{2,1,0:T(8,128)(2,1)} %param.7), channel_id=1, source_target_pairs={{0,496},{1,497},{2,498},{3,499},{4,500},{5,501},{6,502},{7,503},{8... | collective-permute-start | bytes 1179656 | tf_op jit(solution)/shard_map/ppermute | solution.py:44
  21.4 7.3 %collective-permute-done = bf16[2,256,384]{2,1,0:T(8,128)(2,1)S(1)} collective-permute-done((bf16[2,256,384]{2,1,0:T(8,128)(2,1)}, bf16[2,256,384]{2,1,0:T(8,128)(2,1)S(1)}, u32[]{:S(2)}, u32[]{:S(2)}) %collective-permute-start) | collective-permute-done | bytes 393248 | tf_op jit(solution)/shard_map/ppermute | solution.py:44
  28.8 2.0 add_convert_fusion
  30.9 1.1 slice_bitcast_fusion.1
  32.0 3.6 %collective-permute-start.3 = (bf16[256,384]{1,0:T(8,128)(2,1)S(1)}, bf16[256,384]{1,0:T(8,128)(2,1)S(1)}, u32[]{:S(2)}, u32[]{:S(2)}) collective-permute-start(bf16[256,384]{1,0:T(8,128)(2,1)S(1)} %get-tuple-element.22), channel_id=1, source_target_pairs={{0,72},{1,73},{2,74},{3,75},{4,76},{5,77},{6,78},{7,79},{8,64},{9,... | collective-permute-start | bytes 589832 | tf_op jit(solution)/shard_map/ppermute | solution.py:44
  35.6 6.2 %collective-permute-start.1 = (bf16[256,384]{1,0:T(8,128)(2,1)S(1)}, bf16[256,384]{1,0:T(8,128)(2,1)S(1)}, u32[]{:S(2)}, u32[]{:S(2)}) collective-permute-start(bf16[256,384]{1,0:T(8,128)(2,1)S(1)} %get-tuple-element.21), channel_id=1, source_target_pairs={{0,64},{1,65},{2,66},{3,67},{4,68},{5,69},{6,70},{7,71},{8,72},{9,... | collective-permute-start | bytes 589832 | tf_op jit(solution)/shard_map/ppermute | solution.py:44
  41.7 4.6 %collective-permute-done.3 = bf16[256,384]{1,0:T(8,128)(2,1)S(1)} collective-permute-done((bf16[256,384]{1,0:T(8,128)(2,1)S(1)}, bf16[256,384]{1,0:T(8,128)(2,1)S(1)}, u32[]{:S(2)}, u32[]{:S(2)}) %collective-permute-start.3) | collective-permute-done | bytes 196640 | tf_op jit(solution)/shard_map/ppermute | solution.py:44
  46.3 6.9 %collective-permute-start.4 = (bf16[256,384]{1,0:T(8,128)(2,1)S(1)}, bf16[256,384]{1,0:T(8,128)(2,1)S(1)}, u32[]{:S(2)}, u32[]{:S(2)}) collective-permute-start(bf16[256,384]{1,0:T(8,128)(2,1)S(1)} %collective-permute-done.3), channel_id=1, source_target_pairs={{0,72},{1,73},{2,74},{3,75},{4,76},{5,77},{6,78},{7,79},{8,64},{9,... | collective-permute-start | bytes 589832 | tf_op jit(solution)/shard_map/ppermute | solution.py:44
  53.3 1.4 collective-permute-done.1
  54.7 7.0 %collective-permute-start.2 = (bf16[256,384]{1,0:T(8,128)(2,1)S(1)}, bf16[256,384]{1,0:T(8,128)(2,1)S(1)}, u32[]{:S(2)}, u32[]{:S(2)}) collective-permute-start(bf16[256,384]{1,0:T(8,128)(2,1)S(1)} %collective-permute-done.1), channel_id=1, source_target_pairs={{0,64},{1,65},{2,66},{3,67},{4,68},{5,69},{6,70},{7,71},{8,72},{9,... | collective-permute-start | bytes 589832 | tf_op jit(solution)/shard_map/ppermute | solution.py:44
  61.7 3.1 %collective-permute-done.4 = bf16[256,384]{1,0:T(8,128)(2,1)S(1)} collective-permute-done((bf16[256,384]{1,0:T(8,128)(2,1)S(1)}, bf16[256,384]{1,0:T(8,128)(2,1)S(1)}, u32[]{:S(2)}, u32[]{:S(2)}) %collective-permute-start.4) | collective-permute-done | bytes 196640 | tf_op jit(solution)/shard_map/ppermute | solution.py:44
  64.8 8.2 %collective-permute-done.2 = bf16[256,384]{1,0:T(8,128)(2,1)S(1)} collective-permute-done((bf16[256,384]{1,0:T(8,128)(2,1)S(1)}, bf16[256,384]{1,0:T(8,128)(2,1)S(1)}, u32[]{:S(2)}, u32[]{:S(2)}) %collective-permute-start.2) | collective-permute-done | bytes 196640 | tf_op jit(solution)/shard_map/ppermute | solution.py:44
  73.0 0.8 pad_maximum_fusion
  73.9 6.1 %collective-permute-start.7 = (bf16[2,3,192,128]{3,2,1,0:T(8,128)(2,1)S(1)}, bf16[2,3,192,128]{3,2,1,0:T(8,128)(2,1)S(1)}, u32[]{:S(2)}, u32[]{:S(2)}) collective-permute-start(bf16[2,3,192,128]{3,2,1,0:T(8,128)(2,1)S(1)} %pad_maximum_fusion.1.refs_0_), channel_id=1, source_target_pairs={{0,16},{1,17},{2,18},{3,19},{4,20},{5,21},{6,22},{7,23},{8,24},{9,... | collective-permute-start | bytes 884744 | tf_op jit(solution)/shard_map/ppermute | solution.py:44
  80.0 1.3 collective-permute-start.8
  81.3 3.9 %collective-permute-done.7.refs_0_ = bf16[2,3,192,128]{3,2,1,0:T(8,128)(2,1)S(1)} collective-permute-done((bf16[2,3,192,128]{3,2,1,0:T(8,128)(2,1)S(1)}, bf16[2,3,192,128]{3,2,1,0:T(8,128)(2,1)S(1)}, u32[]{:S(2)}, u32[]{:S(2)}) %collective-permute-start.7) | collective-permute-done | bytes 294944 | tf_op jit(solution)/shard_map/ppermute | solution.py:44
  85.9 3.3 %collective-permute-done.8.refs_1_ = bf16[2,3,192,128]{3,2,1,0:T(8,128)(2,1)S(1)} collective-permute-done((bf16[2,3,192,128]{3,2,1,0:T(8,128)(2,1)S(1)}, bf16[2,3,192,128]{3,2,1,0:T(8,128)(2,1)S(1)}, u32[]{:S(2)}, u32[]{:S(2)}) %collective-permute-start.8) | collective-permute-done | bytes 294944 | tf_op jit(solution)/shard_map/ppermute | solution.py:44
  89.2 1.3 collective-permute-start.10
  90.5 8.8 %collective-permute-start.5 = (bf16[2,3,192,128]{3,2,1,0:T(8,128)(2,1)S(1)}, bf16[2,3,192,128]{3,2,1,0:T(8,128)(2,1)S(1)}, u32[]{:S(2)}, u32[]{:S(2)}) collective-permute-start(bf16[2,3,192,128]{3,2,1,0:T(8,128)(2,1)S(1)} %pad_maximum_fusion.1.refs_0_), channel_id=1, source_target_pairs={{0,128},{1,129},{2,130},{3,131},{4,132},{5,133},{6,134},{7,135},{8... | collective-permute-start | bytes 884744 | tf_op jit(solution)/shard_map/ppermute | solution.py:44
  99.3 1.9 collective-permute-start.6
  101.9 2.2 collective-permute-done.10.refs_3_.refs_1_
  104.1 1.3 collective-permute-start.14
  105.4 3.7 %collective-permute-done.6.refs_5_.refs_2_ = bf16[2,3,192,128]{3,2,1,0:T(8,128)(2,1)S(1)} collective-permute-done((bf16[2,3,192,128]{3,2,1,0:T(8,128)(2,1)S(1)}, bf16[2,3,192,128]{3,2,1,0:T(8,128)(2,1)S(1)}, u32[]{:S(2)}, u32[]{:S(2)}) %collective-permute-start.6) | collective-permute-done | bytes 294944 | tf_op jit(solution)/shard_map/ppermute | solution.py:44
  109.1 1.0 shard_map.74
  110.2 1.9 collective-permute-start.11
  112.1 3.9 %collective-permute-start.12 = (bf16[5,3,192,128]{3,2,1,0:T(8,128)(2,1)}, bf16[5,3,192,128]{3,2,1,0:T(8,128)(2,1)S(1)}, u32[]{:S(2)}, u32[]{:S(2)}) collective-permute-start(bf16[5,3,192,128]{3,2,1,0:T(8,128)(2,1)} %get-tuple-element.14), channel_id=1, source_target_pairs={{0,384},{1,385},{2,386},{3,387},{4,388},{5,389},{6,390},{7,391},{8... | collective-permute-start | bytes 2211848 | tf_op jit(solution)/shard_map/ppermute | solution.py:44
  116.1 1.4 collective-permute-start.15
  117.5 1.3 collective-permute-start.16
  118.8 8.7 %collective-permute-done.16 = bf16[2,3,192,128]{3,2,1,0:T(8,128)(2,1)} collective-permute-done((bf16[2,3,192,128]{3,2,1,0:T(8,128)(2,1)S(1)}, bf16[2,3,192,128]{3,2,1,0:T(8,128)(2,1)}, u32[]{:S(2)}, u32[]{:S(2)}) %collective-permute-start.16) | collective-permute-done | bytes 294944 | tf_op jit(solution)/shard_map/ppermute | solution.py:44
  127.5 1.0 broadcast_select_fusion.refs_4_.refs_0_
  128.9 3.0 %collective-permute-start.17 = (bf16[6,3,192,128]{3,2,1,0:T(8,128)(2,1)S(1)}, bf16[6,3,192,128]{3,2,1,0:T(8,128)(2,1)S(1)}, u32[]{:S(2)}, u32[]{:S(2)}) collective-permute-start(bf16[6,3,192,128]{3,2,1,0:T(8,128)(2,1)S(1)} %get-tuple-element.15.refs_6_), channel_id=1, source_target_pairs={{0,128},{1,129},{2,130},{3,131},{4,132},{5,133},{6,134},{7,135},{8... | collective-permute-start | bytes 2654216 | tf_op jit(solution)/shard_map/ppermute | solution.py:44
  131.9 0.9 copy-done.17
  132.8 2.8 %collective-permute-start.18 = (bf16[6,3,192,128]{3,2,1,0:T(8,128)(2,1)S(1)}, bf16[6,3,192,128]{3,2,1,0:T(8,128)(2,1)S(1)}, u32[]{:S(2)}, u32[]{:S(2)}) collective-permute-start(bf16[6,3,192,128]{3,2,1,0:T(8,128)(2,1)S(1)} %get-tuple-element.16), channel_id=1, source_target_pairs={{0,384},{1,385},{2,386},{3,387},{4,388},{5,389},{6,390},{7,391},{8... | collective-permute-start | bytes 2654216 | tf_op jit(solution)/shard_map/ppermute | solution.py:44
  135.7 1.3 collective-permute-start.19
  137.0 9.4 %collective-permute-done.19.refs_1_ = bf16[2,3,192,128]{3,2,1,0:T(8,128)(2,1)S(1)} collective-permute-done((bf16[2,3,192,128]{3,2,1,0:T(8,128)(2,1)S(1)}, bf16[2,3,192,128]{3,2,1,0:T(8,128)(2,1)S(1)}, u32[]{:S(2)}, u32[]{:S(2)}) %collective-permute-start.19) | collective-permute-done | bytes 294944 | tf_op jit(solution)/shard_map/ppermute | solution.py:44
  146.4 1.3 collective-permute-start.20
  147.7 8.0 %collective-permute-done.20.refs_2_.refs_1_ = bf16[2,3,192,128]{3,2,1,0:T(8,128)(2,1)} collective-permute-done((bf16[2,3,192,128]{3,2,1,0:T(8,128)(2,1)S(1)}, bf16[2,3,192,128]{3,2,1,0:T(8,128)(2,1)}, u32[]{:S(2)}, u32[]{:S(2)}) %collective-permute-start.20) | collective-permute-done | bytes 294944 | tf_op jit(solution)/shard_map/ppermute | solution.py:44
  155.7 1.0 copy-done.9
  156.7 2.5 %shard_map.76 = (bf16[6,3,192,128]{3,2,1,0:T(8,128)(2,1)}, bf16[6,3,192,128]{3,2,1,0:T(8,128)(2,1)}) custom-call(s32[1]{0:T(128)} %bitcast.10.zl_ref, bf16[2,3,192,128]{3,2,1,0:T(8,128)(2,1)S(1)} %broadcast_select_fusion.refs_4_.refs_0_, bf16[2,3,192,128]{3,2,1,0:T(8,128)(2,1)S(1)} %collective-permute-done.19.refs_1_, ...), custom_call_target="tpu_custom_call" | custom-call | bytes 4194304 | tf_op jit(solution)/shard_map/pallas_call | solution.py:211
  159.2 5.3 %collective-permute-start.21 = (bf16[6,3,192,128]{3,2,1,0:T(8,128)(2,1)}, bf16[6,3,192,128]{3,2,1,0:T(8,128)(2,1)S(1)}, u32[]{:S(2)}, u32[]{:S(2)}) collective-permute-start(bf16[6,3,192,128]{3,2,1,0:T(8,128)(2,1)} %get-tuple-element.17.refs_9_), channel_id=1, source_target_pairs={{0,128},{1,129},{2,130},{3,131},{4,132},{5,133},{6,134},{7,135},{8... | collective-permute-start | bytes 2654216 | tf_op jit(solution)/shard_map/ppermute | solution.py:44
  164.5 1.9 collective-permute-start.22
  166.4 1.3 collective-permute-start.23
  168.4 6.9 %collective-permute-done.23.refs_0_ = bf16[2,3,192,128]{3,2,1,0:T(8,128)(2,1)} collective-permute-done((bf16[2,3,192,128]{3,2,1,0:T(8,128)(2,1)}, bf16[2,3,192,128]{3,2,1,0:T(8,128)(2,1)}, u32[]{:S(2)}, u32[]{:S(2)}) %collective-permute-start.23) | collective-permute-done | bytes 294944 | tf_op jit(solution)/shard_map/ppermute | solution.py:44
  175.3 2.8 %collective-permute-done.21.refs_10_.refs_4_ = bf16[6,3,192,128]{3,2,1,0:T(8,128)(2,1)S(1)} collective-permute-done((bf16[6,3,192,128]{3,2,1,0:T(8,128)(2,1)}, bf16[6,3,192,128]{3,2,1,0:T(8,128)(2,1)S(1)}, u32[]{:S(2)}, u32[]{:S(2)}) %collective-permute-start.21) | collective-permute-done | bytes 884768 | tf_op jit(solution)/shard_map/ppermute | solution.py:44
  178.1 5.2 %collective-permute-done.22.refs_11_.refs_5_ = bf16[6,3,192,128]{3,2,1,0:T(8,128)(2,1)S(1)} collective-permute-done((bf16[6,3,192,128]{3,2,1,0:T(8,128)(2,1)}, bf16[6,3,192,128]{3,2,1,0:T(8,128)(2,1)S(1)}, u32[]{:S(2)}, u32[]{:S(2)}) %collective-permute-start.22) | collective-permute-done | bytes 884768 | tf_op jit(solution)/shard_map/ppermute | solution.py:44
  183.4 1.0 copy-done.7
  184.3 1.0 copy-done.10
  185.3 2.2 shard_map.78
  187.5 1.9 collective-permute-start.24
  189.4 3.9 %collective-permute-start.25 = (bf16[4,3,192,128]{3,2,1,0:T(8,128)(2,1)}, bf16[4,3,192,128]{3,2,1,0:T(8,128)(2,1)}, u32[]{:S(2)}, u32[]{:S(2)}) collective-permute-start(bf16[4,3,192,128]{3,2,1,0:T(8,128)(2,1)} %get-tuple-element.20), channel_id=1, source_target_pairs={{0,384},{1,385},{2,386},{3,387},{4,388},{5,389},{6,390},{7,391},{8... | collective-permute-start | bytes 1769480 | tf_op jit(solution)/shard_map/ppermute | solution.py:44
  193.5 1.4 reshape.36
  194.9 1.4 fusion.gain_ref
  196.3 4.8 %collective-permute-done.24.refs_1_ = bf16[4,3,192,128]{3,2,1,0:T(8,128)(2,1)} collective-permute-done((bf16[4,3,192,128]{3,2,1,0:T(8,128)(2,1)}, bf16[4,3,192,128]{3,2,1,0:T(8,128)(2,1)}, u32[]{:S(2)}, u32[]{:S(2)}) %collective-permute-start.24) | collective-permute-done | bytes 589856 | tf_op jit(solution)/shard_map/ppermute | solution.py:44
  201.1 1.6 slice.36
  202.7 1.9 collective-permute-start.26
  204.7 1.6 slice.37
  206.2 4.1 %collective-permute-start.27 = (bf16[1,3,192,128]{3,2,1,0:T(8,128)(2,1)}, bf16[1,3,192,128]{3,2,1,0:T(8,128)(2,1)}, u32[]{:S(2)}, u32[]{:S(2)}) collective-permute-start(bf16[1,3,192,128]{3,2,1,0:T(8,128)(2,1)} %slice.37), channel_id=1, source_target_pairs={{0,384},{1,385},{2,386},{3,387},{4,388},{5,389},{6,390},{7,391},{8... | collective-permute-start | bytes 442376 | tf_op jit(solution)/shard_map/ppermute | solution.py:44
  210.4 1.9 copy-done
  212.3 1.9 copy-done.1
  214.2 0.7 copy-done.21
  215.0 6.4 %shard_map.73.normed_ref = bf16[32,512,192]{2,1,0:T(8,128)(2,1)S(1)} custom-call(bf16[8,512,384]{2,1,0:T(8,128)(2,1)S(1)} %copy-done, bf16[8,512,384]{2,1,0:T(8,128)(2,1)S(1)} %bitcast.20, f32[16,384]{1,0:T(8,128)S(1)} %copy-done.21), custom_call_target="tpu_custom_call" | custom-call | flops 25165824 | bytes 14680064 | tf_op jit(solution)/shard_map/pallas_call | solution.py:101
  221.5 6.7 %shard_map.77.held_ref = f32[3,512,256]{2,1,0:T(8,128)S(1)} custom-call(s32[32]{0:T(128)S(1)} %fusion.1.index_ref, bf16[32,512,192]{2,1,0:T(8,128)(2,1)S(1)} %shard_map.73.normed_ref, bf16[2,3,192,128]{3,2,1,0:T(8,128)(2,1)S(1)} %copy-done.12, bf16[2,3,192,128]{3,2,1,0:T(8,128)(2,1)S(1)} %copy-done.14, bf16[2,3,192,128]{3,2,1,0:T(8,128)(2,1)S(1)} %copy-done.16, ...), custom_call_target="tpu_custom_call" | custom-call | flops 3925868544 | bytes 16056320 | tf_op jit(solution)/shard_map/pallas_call | solution.py:175
  228.2 2.6 %shard_map.79.held_ref = f32[3,512,256]{2,1,0:T(8,128)S(1)} custom-call(s32[32]{0:T(128)S(1)} %fusion.1.index_ref, bf16[32,512,192]{2,1,0:T(8,128)(2,1)S(1)} %shard_map.73.normed_ref, f32[3,512,256]{2,1,0:T(8,128)S(1)} %shard_map.77.held_ref, bf16[4,3,192,128]{3,2,1,0:T(8,128)(2,1)} %get-tuple-element.19.refs_0_, ...), custom_call_target="tpu_custom_call" | custom-call | flops 754974720 | bytes 9863168 | tf_op jit(solution)/shard_map/pallas_call | solution.py:175
  230.8 3.3 %shard_map.80 = bf16[512,256]{1,0:T(8,128)(2,1)} custom-call(s32[32]{0:T(128)S(1)} %fusion.1.index_ref, bf16[32,512,192]{2,1,0:T(8,128)(2,1)S(1)} %shard_map.73.normed_ref, f32[3,512,256]{2,1,0:T(8,128)S(1)} %shard_map.79.held_ref, f32[2,256]{1,0:T(2,128)S(1)} %copy-done.22, bf16[1,3,192,128]{3,2,1,0:T(8,128)(2,1)} %collective-permute-done.26.refs_0_, ...), custom_call_target="tpu_custom_call" | custom-call | flops 150994944 | bytes 8683520 | tf_op jit(solution)/shard_map/pallas_call | solution.py:175
  (72 shorter events, 4.3 us)
Async XLA Ops:
  6.5 67.2 %copy-start.23 = (bf16[3,192,256]{2,1,0:T(8,128)(2,1)S(1)}, bf16[3,192,256]{2,1,0:T(8,128)(2,1)}, u32[]{:S(2)}) copy-start(bf16[3,192,256]{2,1,0:T(8,128)(2,1)} %param.11) | copy-start | bytes 884740
  6.5 203.8 %all-gather.4.cloned.1.call-start = ((), (), s32[]{:S(2)}) async-start(), calls=%async_computation | async-start | bytes 3538944 | tf_op jit(solution)/shard_map/all_gather | solution.py:282
  6.5 22.2 %collective-permute-start = (bf16[2,256,384]{2,1,0:T(8,128)(2,1)}, bf16[2,256,384]{2,1,0:T(8,128)(2,1)S(1)}, u32[]{:S(2)}, u32[]{:S(2)}) collective-permute-start(bf16[2,256,384]{2,1,0:T(8,128)(2,1)} %param.7), channel_id=1, source_target_pairs={{0,496},{1,497},{2,498},{3,499},{4,500},{5,501},{6,502},{7,503},{8... | collective-permute-start | bytes 1179656 | tf_op jit(solution)/shard_map/ppermute | solution.py:44
  30.9 179.5 %all-gather.6.cloned.1.call-start = ((), (), s32[]{:S(2)}) async-start(), calls=%async_computation.1 | async-start | bytes 3538944 | tf_op jit(solution)/shard_map/all_gather | solution.py:283
  32.0 14.4 %collective-permute-start.3 = (bf16[256,384]{1,0:T(8,128)(2,1)S(1)}, bf16[256,384]{1,0:T(8,128)(2,1)S(1)}, u32[]{:S(2)}, u32[]{:S(2)}) collective-permute-start(bf16[256,384]{1,0:T(8,128)(2,1)S(1)} %get-tuple-element.22), channel_id=1, source_target_pairs={{0,72},{1,73},{2,74},{3,75},{4,76},{5,77},{6,78},{7,79},{8,64},{9,... | collective-permute-start | bytes 589832 | tf_op jit(solution)/shard_map/ppermute | solution.py:44
  35.6 19.1 %collective-permute-start.1 = (bf16[256,384]{1,0:T(8,128)(2,1)S(1)}, bf16[256,384]{1,0:T(8,128)(2,1)S(1)}, u32[]{:S(2)}, u32[]{:S(2)}) collective-permute-start(bf16[256,384]{1,0:T(8,128)(2,1)S(1)} %get-tuple-element.21), channel_id=1, source_target_pairs={{0,64},{1,65},{2,66},{3,67},{4,68},{5,69},{6,70},{7,71},{8,72},{9,... | collective-permute-start | bytes 589832 | tf_op jit(solution)/shard_map/ppermute | solution.py:44
  46.3 18.5 %collective-permute-start.4 = (bf16[256,384]{1,0:T(8,128)(2,1)S(1)}, bf16[256,384]{1,0:T(8,128)(2,1)S(1)}, u32[]{:S(2)}, u32[]{:S(2)}) collective-permute-start(bf16[256,384]{1,0:T(8,128)(2,1)S(1)} %collective-permute-done.3), channel_id=1, source_target_pairs={{0,72},{1,73},{2,74},{3,75},{4,76},{5,77},{6,78},{7,79},{8,64},{9,... | collective-permute-start | bytes 589832 | tf_op jit(solution)/shard_map/ppermute | solution.py:44
  54.7 18.3 %collective-permute-start.2 = (bf16[256,384]{1,0:T(8,128)(2,1)S(1)}, bf16[256,384]{1,0:T(8,128)(2,1)S(1)}, u32[]{:S(2)}, u32[]{:S(2)}) collective-permute-start(bf16[256,384]{1,0:T(8,128)(2,1)S(1)} %collective-permute-done.1), channel_id=1, source_target_pairs={{0,64},{1,65},{2,66},{3,67},{4,68},{5,69},{6,70},{7,71},{8,72},{9,... | collective-permute-start | bytes 589832 | tf_op jit(solution)/shard_map/ppermute | solution.py:44
  73.9 36.3 %copy-start.11 = (bf16[2,3,192,128]{3,2,1,0:T(8,128)(2,1)}, bf16[2,3,192,128]{3,2,1,0:T(8,128)(2,1)S(1)}, u32[]{:S(2)}) copy-start(bf16[2,3,192,128]{3,2,1,0:T(8,128)(2,1)S(1)} %pad_maximum_fusion.1.refs_0_) | copy-start | bytes 884740
  73.9 11.4 %collective-permute-start.7 = (bf16[2,3,192,128]{3,2,1,0:T(8,128)(2,1)S(1)}, bf16[2,3,192,128]{3,2,1,0:T(8,128)(2,1)S(1)}, u32[]{:S(2)}, u32[]{:S(2)}) collective-permute-start(bf16[2,3,192,128]{3,2,1,0:T(8,128)(2,1)S(1)} %pad_maximum_fusion.1.refs_0_), channel_id=1, source_target_pairs={{0,16},{1,17},{2,18},{3,19},{4,20},{5,21},{6,22},{7,23},{8,24},{9,... | collective-permute-start | bytes 884744 | tf_op jit(solution)/shard_map/ppermute | solution.py:44
  80.0 9.2 %collective-permute-start.8 = (bf16[2,3,192,128]{3,2,1,0:T(8,128)(2,1)S(1)}, bf16[2,3,192,128]{3,2,1,0:T(8,128)(2,1)S(1)}, u32[]{:S(2)}, u32[]{:S(2)}) collective-permute-start(bf16[2,3,192,128]{3,2,1,0:T(8,128)(2,1)S(1)} %pad_maximum_fusion.1.refs_0_), channel_id=1, source_target_pairs={{16,0},{17,1},{18,2},{19,3},{20,4},{21,5},{22,6},{23,7},{24,8},{25... | collective-permute-start | bytes 884744 | tf_op jit(solution)/shard_map/ppermute | solution.py:44
  85.3 16.0 %collective-permute-start.9 = (bf16[2,3,192,128]{3,2,1,0:T(8,128)(2,1)S(1)}, bf16[2,3,192,128]{3,2,1,0:T(8,128)(2,1)S(1)}, u32[]{:S(2)}, u32[]{:S(2)}) collective-permute-start(bf16[2,3,192,128]{3,2,1,0:T(8,128)(2,1)S(1)} %collective-permute-done.7.refs_0_), channel_id=1, source_target_pairs={{16,32},{17,33},{18,34},{19,35},{20,36},{21,37},{22,38},{23,39},{2... | collective-permute-start | bytes 884744 | tf_op jit(solution)/shard_map/ppermute | solution.py:44
  89.2 14.9 %collective-permute-start.10 = (bf16[2,3,192,128]{3,2,1,0:T(8,128)(2,1)S(1)}, bf16[2,3,192,128]{3,2,1,0:T(8,128)(2,1)S(1)}, u32[]{:S(2)}, u32[]{:S(2)}) collective-permute-start(bf16[2,3,192,128]{3,2,1,0:T(8,128)(2,1)S(1)} %collective-permute-done.8.refs_1_), channel_id=1, source_target_pairs={{16,0},{17,1},{18,2},{19,3},{20,4},{21,5},{22,6},{23,7},{24,8},{25... | collective-permute-start | bytes 884744 | tf_op jit(solution)/shard_map/ppermute | solution.py:44
  90.5 14.9 %collective-permute-start.5 = (bf16[2,3,192,128]{3,2,1,0:T(8,128)(2,1)S(1)}, bf16[2,3,192,128]{3,2,1,0:T(8,128)(2,1)S(1)}, u32[]{:S(2)}, u32[]{:S(2)}) collective-permute-start(bf16[2,3,192,128]{3,2,1,0:T(8,128)(2,1)S(1)} %pad_maximum_fusion.1.refs_0_), channel_id=1, source_target_pairs={{0,128},{1,129},{2,130},{3,131},{4,132},{5,133},{6,134},{7,135},{8... | collective-permute-start | bytes 884744 | tf_op jit(solution)/shard_map/ppermute | solution.py:44
  99.3 9.8 %collective-permute-start.6 = (bf16[2,3,192,128]{3,2,1,0:T(8,128)(2,1)S(1)}, bf16[2,3,192,128]{3,2,1,0:T(8,128)(2,1)S(1)}, u32[]{:S(2)}, u32[]{:S(2)}) collective-permute-start(bf16[2,3,192,128]{3,2,1,0:T(8,128)(2,1)S(1)} %pad_maximum_fusion.1.refs_0_), channel_id=1, source_target_pairs={{0,384},{1,385},{2,386},{3,387},{4,388},{5,389},{6,390},{7,391},{8... | collective-permute-start | bytes 884744 | tf_op jit(solution)/shard_map/ppermute | solution.py:44
  101.2 14.8 %collective-permute-start.13 = (bf16[2,3,192,128]{3,2,1,0:T(8,128)(2,1)S(1)}, bf16[2,3,192,128]{3,2,1,0:T(8,128)(2,1)S(1)}, u32[]{:S(2)}, u32[]{:S(2)}) collective-permute-start(bf16[2,3,192,128]{3,2,1,0:T(8,128)(2,1)S(1)} %collective-permute-done.9.refs_2_.refs_0_), channel_id=1, source_target_pairs={{32,48},{33,49},{34,50},{35,51},{36,52},{37,53},{38,54},{39,55},{4... | collective-permute-start | bytes 884744 | tf_op jit(solution)/shard_map/ppermute | solution.py:44
  104.1 13.4 %collective-permute-start.14 = (bf16[2,3,192,128]{3,2,1,0:T(8,128)(2,1)S(1)}, bf16[2,3,192,128]{3,2,1,0:T(8,128)(2,1)S(1)}, u32[]{:S(2)}, u32[]{:S(2)}) collective-permute-start(bf16[2,3,192,128]{3,2,1,0:T(8,128)(2,1)S(1)} %collective-permute-done.10.refs_3_.refs_1_), channel_id=1, source_target_pairs={{16,0},{17,1},{18,2},{19,3},{20,4},{21,5},{22,6},{23,7},{24,8},{25... | collective-permute-start | bytes 884744 | tf_op jit(solution)/shard_map/ppermute | solution.py:44
  105.4 4.8 %copy-start.13 = (bf16[2,3,192,128]{3,2,1,0:T(8,128)(2,1)}, bf16[2,3,192,128]{3,2,1,0:T(8,128)(2,1)S(1)}, u32[]{:S(2)}) copy-start(bf16[2,3,192,128]{3,2,1,0:T(8,128)(2,1)S(1)} %collective-permute-done.5.refs_4_.refs_1_) | copy-start | bytes 884740
  109.1 1.1 copy-start.15
  110.2 21.7 %copy-start.19 = (bf16[5,3,192,128]{3,2,1,0:T(8,128)(2,1)}, bf16[5,3,192,128]{3,2,1,0:T(8,128)(2,1)S(1)}, u32[]{:S(2)}) copy-start(bf16[5,3,192,128]{3,2,1,0:T(8,128)(2,1)S(1)} %get-tuple-element.13.refs_3_) | copy-start | bytes 2211844
  110.2 18.3 %collective-permute-start.11 = (bf16[5,3,192,128]{3,2,1,0:T(8,128)(2,1)S(1)}, bf16[5,3,192,128]{3,2,1,0:T(8,128)(2,1)S(1)}, u32[]{:S(2)}, u32[]{:S(2)}) collective-permute-start(bf16[5,3,192,128]{3,2,1,0:T(8,128)(2,1)S(1)} %get-tuple-element.13.refs_3_), channel_id=1, source_target_pairs={{0,128},{1,129},{2,130},{3,131},{4,132},{5,133},{6,134},{7,135},{8... | collective-permute-start | bytes 2211848 | tf_op jit(solution)/shard_map/ppermute | solution.py:44
  112.1 16.6 %collective-permute-start.12 = (bf16[5,3,192,128]{3,2,1,0:T(8,128)(2,1)}, bf16[5,3,192,128]{3,2,1,0:T(8,128)(2,1)S(1)}, u32[]{:S(2)}, u32[]{:S(2)}) collective-permute-start(bf16[5,3,192,128]{3,2,1,0:T(8,128)(2,1)} %get-tuple-element.14), channel_id=1, source_target_pairs={{0,384},{1,385},{2,386},{3,387},{4,388},{5,389},{6,390},{7,391},{8... | collective-permute-start | bytes 2211848 | tf_op jit(solution)/shard_map/ppermute | solution.py:44
  116.0 43.1 %copy-start.6 = (bf16[2,3,192,128]{3,2,1,0:T(8,128)(2,1)}, bf16[2,3,192,128]{3,2,1,0:T(8,128)(2,1)S(1)}, u32[]{:S(2)}) copy-start(bf16[2,3,192,128]{3,2,1,0:T(8,128)(2,1)S(1)} %collective-permute-done.13.refs_2_.refs_3_) | copy-start | bytes 884740
  116.1 2.7 %collective-permute-start.15 = (bf16[2,3,192,128]{3,2,1,0:T(8,128)(2,1)S(1)}, bf16[2,3,192,128]{3,2,1,0:T(8,128)(2,1)}, u32[]{:S(2)}, u32[]{:S(2)}) collective-permute-start(bf16[2,3,192,128]{3,2,1,0:T(8,128)(2,1)S(1)} %collective-permute-done.13.refs_2_.refs_3_), channel_id=1, source_target_pairs={{48,64},{49,65},{50,66},{51,67},{52,68},{53,69},{54,70},{55,71},{5... | collective-permute-start | bytes 884744 | tf_op jit(solution)/shard_map/ppermute | solution.py:44
  117.5 11.4 %copy-start.8 = (bf16[2,3,192,128]{3,2,1,0:T(8,128)(2,1)}, bf16[2,3,192,128]{3,2,1,0:T(8,128)(2,1)S(1)}, u32[]{:S(2)}) copy-start(bf16[2,3,192,128]{3,2,1,0:T(8,128)(2,1)S(1)} %collective-permute-done.14.refs_3_.refs_4_) | copy-start | bytes 884740
  117.5 10.0 %collective-permute-start.16 = (bf16[2,3,192,128]{3,2,1,0:T(8,128)(2,1)S(1)}, bf16[2,3,192,128]{3,2,1,0:T(8,128)(2,1)}, u32[]{:S(2)}, u32[]{:S(2)}) collective-permute-start(bf16[2,3,192,128]{3,2,1,0:T(8,128)(2,1)S(1)} %collective-permute-done.14.refs_3_.refs_4_), channel_id=1, source_target_pairs={{16,0},{17,1},{18,2},{19,3},{20,4},{21,5},{22,6},{23,7},{24,8},{25... | collective-permute-start | bytes 884744 | tf_op jit(solution)/shard_map/ppermute | solution.py:44
  128.5 30.7 %copy-start.2 = (bf16[5,3,192,128]{3,2,1,0:T(8,128)(2,1)}, bf16[5,3,192,128]{3,2,1,0:T(8,128)(2,1)S(1)}, u32[]{:S(2)}) copy-start(bf16[5,3,192,128]{3,2,1,0:T(8,128)(2,1)S(1)} %collective-permute-done.11.refs_5_.refs_4_) | copy-start | bytes 2211844
  128.7 30.5 %copy-start.4 = (bf16[5,3,192,128]{3,2,1,0:T(8,128)(2,1)}, bf16[5,3,192,128]{3,2,1,0:T(8,128)(2,1)S(1)}, u32[]{:S(2)}) copy-start(bf16[5,3,192,128]{3,2,1,0:T(8,128)(2,1)S(1)} %collective-permute-done.12.refs_6_.refs_5_) | copy-start | bytes 2211844
  128.9 26.9 %collective-permute-start.17 = (bf16[6,3,192,128]{3,2,1,0:T(8,128)(2,1)S(1)}, bf16[6,3,192,128]{3,2,1,0:T(8,128)(2,1)S(1)}, u32[]{:S(2)}, u32[]{:S(2)}) collective-permute-start(bf16[6,3,192,128]{3,2,1,0:T(8,128)(2,1)S(1)} %get-tuple-element.15.refs_6_), channel_id=1, source_target_pairs={{0,128},{1,129},{2,130},{3,131},{4,132},{5,133},{6,134},{7,135},{8... | collective-permute-start | bytes 2654216 | tf_op jit(solution)/shard_map/ppermute | solution.py:44
  131.9 0.9 copy-start.17
  132.8 22.9 %collective-permute-start.18 = (bf16[6,3,192,128]{3,2,1,0:T(8,128)(2,1)S(1)}, bf16[6,3,192,128]{3,2,1,0:T(8,128)(2,1)S(1)}, u32[]{:S(2)}, u32[]{:S(2)}) collective-permute-start(bf16[6,3,192,128]{3,2,1,0:T(8,128)(2,1)S(1)} %get-tuple-element.16), channel_id=1, source_target_pairs={{0,384},{1,385},{2,386},{3,387},{4,388},{5,389},{6,390},{7,391},{8... | collective-permute-start | bytes 2654216 | tf_op jit(solution)/shard_map/ppermute | solution.py:44
  135.7 10.7 %collective-permute-start.19 = (bf16[2,3,192,128]{3,2,1,0:T(8,128)(2,1)S(1)}, bf16[2,3,192,128]{3,2,1,0:T(8,128)(2,1)S(1)}, u32[]{:S(2)}, u32[]{:S(2)}) collective-permute-start(bf16[2,3,192,128]{3,2,1,0:T(8,128)(2,1)S(1)} %broadcast_select_fusion.refs_4_.refs_0_), channel_id=1, source_target_pairs={{16,0},{17,1},{18,2},{19,3},{20,4},{21,5},{22,6},{23,7},{24,8},{25... | collective-permute-start | bytes 884744 | tf_op jit(solution)/shard_map/ppermute | solution.py:44
  146.4 9.3 %collective-permute-start.20 = (bf16[2,3,192,128]{3,2,1,0:T(8,128)(2,1)S(1)}, bf16[2,3,192,128]{3,2,1,0:T(8,128)(2,1)}, u32[]{:S(2)}, u32[]{:S(2)}) collective-permute-start(bf16[2,3,192,128]{3,2,1,0:T(8,128)(2,1)S(1)} %collective-permute-done.19.refs_1_), channel_id=1, source_target_pairs={{16,0},{17,1},{18,2},{19,3},{20,4},{21,5},{22,6},{23,7},{24,8},{25... | collective-permute-start | bytes 884744 | tf_op jit(solution)/shard_map/ppermute | solution.py:44
  155.7 1.0 copy-start.9
  159.2 19.0 %collective-permute-start.21 = (bf16[6,3,192,128]{3,2,1,0:T(8,128)(2,1)}, bf16[6,3,192,128]{3,2,1,0:T(8,128)(2,1)S(1)}, u32[]{:S(2)}, u32[]{:S(2)}) collective-permute-start(bf16[6,3,192,128]{3,2,1,0:T(8,128)(2,1)} %get-tuple-element.17.refs_9_), channel_id=1, source_target_pairs={{0,128},{1,129},{2,130},{3,131},{4,132},{5,133},{6,134},{7,135},{8... | collective-permute-start | bytes 2654216 | tf_op jit(solution)/shard_map/ppermute | solution.py:44
  164.5 18.9 %collective-permute-start.22 = (bf16[6,3,192,128]{3,2,1,0:T(8,128)(2,1)}, bf16[6,3,192,128]{3,2,1,0:T(8,128)(2,1)S(1)}, u32[]{:S(2)}, u32[]{:S(2)}) collective-permute-start(bf16[6,3,192,128]{3,2,1,0:T(8,128)(2,1)} %get-tuple-element.18), channel_id=1, source_target_pairs={{0,384},{1,385},{2,386},{3,387},{4,388},{5,389},{6,390},{7,391},{8... | collective-permute-start | bytes 2654216 | tf_op jit(solution)/shard_map/ppermute | solution.py:44
  166.4 8.9 %collective-permute-start.23 = (bf16[2,3,192,128]{3,2,1,0:T(8,128)(2,1)}, bf16[2,3,192,128]{3,2,1,0:T(8,128)(2,1)}, u32[]{:S(2)}, u32[]{:S(2)}) collective-permute-start(bf16[2,3,192,128]{3,2,1,0:T(8,128)(2,1)} %collective-permute-done.20.refs_2_.refs_1_), channel_id=1, source_target_pairs={{16,0},{17,1},{18,2},{19,3},{20,4},{21,5},{22,6},{23,7},{24,8},{25... | collective-permute-start | bytes 884744 | tf_op jit(solution)/shard_map/ppermute | solution.py:44
  183.4 1.0 copy-start.7
  184.3 1.0 copy-start.10
  187.5 13.7 %collective-permute-start.24 = (bf16[4,3,192,128]{3,2,1,0:T(8,128)(2,1)}, bf16[4,3,192,128]{3,2,1,0:T(8,128)(2,1)}, u32[]{:S(2)}, u32[]{:S(2)}) collective-permute-start(bf16[4,3,192,128]{3,2,1,0:T(8,128)(2,1)} %get-tuple-element.19.refs_0_), channel_id=1, source_target_pairs={{0,128},{1,129},{2,130},{3,131},{4,132},{5,133},{6,134},{7,135},{8... | collective-permute-start | bytes 1769480 | tf_op jit(solution)/shard_map/ppermute | solution.py:44
  189.4 15.2 %collective-permute-start.25 = (bf16[4,3,192,128]{3,2,1,0:T(8,128)(2,1)}, bf16[4,3,192,128]{3,2,1,0:T(8,128)(2,1)}, u32[]{:S(2)}, u32[]{:S(2)}) collective-permute-start(bf16[4,3,192,128]{3,2,1,0:T(8,128)(2,1)} %get-tuple-element.20), channel_id=1, source_target_pairs={{0,384},{1,385},{2,386},{3,387},{4,388},{5,389},{6,390},{7,391},{8... | collective-permute-start | bytes 1769480 | tf_op jit(solution)/shard_map/ppermute | solution.py:44
  202.7 28.1 %collective-permute-start.26 = (bf16[1,3,192,128]{3,2,1,0:T(8,128)(2,1)}, bf16[1,3,192,128]{3,2,1,0:T(8,128)(2,1)}, u32[]{:S(2)}, u32[]{:S(2)}) collective-permute-start(bf16[1,3,192,128]{3,2,1,0:T(8,128)(2,1)} %slice.36), channel_id=1, source_target_pairs={{0,128},{1,129},{2,130},{3,131},{4,132},{5,133},{6,134},{7,135},{8... | collective-permute-start | bytes 442376 | tf_op jit(solution)/shard_map/ppermute | solution.py:44
  206.2 24.6 %collective-permute-start.27 = (bf16[1,3,192,128]{3,2,1,0:T(8,128)(2,1)}, bf16[1,3,192,128]{3,2,1,0:T(8,128)(2,1)}, u32[]{:S(2)}, u32[]{:S(2)}) collective-permute-start(bf16[1,3,192,128]{3,2,1,0:T(8,128)(2,1)} %slice.37), channel_id=1, source_target_pairs={{0,384},{1,385},{2,386},{3,387},{4,388},{5,389},{6,390},{7,391},{8... | collective-permute-start | bytes 442376 | tf_op jit(solution)/shard_map/ppermute | solution.py:44
  210.4 1.9 copy-start
  212.3 1.9 copy-start.1
  214.2 0.7 copy-start.21
  214.9 6.5 %copy-start.3 = (bf16[5,3,192,128]{3,2,1,0:T(8,128)(2,1)S(1)}, bf16[5,3,192,128]{3,2,1,0:T(8,128)(2,1)}, u32[]{:S(2)}) copy-start(bf16[5,3,192,128]{3,2,1,0:T(8,128)(2,1)} %copy-done.2) | copy-start | bytes 2211844
  214.9 6.5 %copy-start.5 = (bf16[5,3,192,128]{3,2,1,0:T(8,128)(2,1)S(1)}, bf16[5,3,192,128]{3,2,1,0:T(8,128)(2,1)}, u32[]{:S(2)}) copy-start(bf16[5,3,192,128]{3,2,1,0:T(8,128)(2,1)} %copy-done.4) | copy-start | bytes 2211844
  214.9 6.5 %copy-start.12 = (bf16[2,3,192,128]{3,2,1,0:T(8,128)(2,1)S(1)}, bf16[2,3,192,128]{3,2,1,0:T(8,128)(2,1)}, u32[]{:S(2)}) copy-start(bf16[2,3,192,128]{3,2,1,0:T(8,128)(2,1)} %copy-done.11) | copy-start | bytes 884740
  214.9 6.5 %copy-start.14 = (bf16[2,3,192,128]{3,2,1,0:T(8,128)(2,1)S(1)}, bf16[2,3,192,128]{3,2,1,0:T(8,128)(2,1)}, u32[]{:S(2)}) copy-start(bf16[2,3,192,128]{3,2,1,0:T(8,128)(2,1)} %copy-done.13) | copy-start | bytes 884740
  214.9 6.5 %copy-start.16 = (bf16[2,3,192,128]{3,2,1,0:T(8,128)(2,1)S(1)}, bf16[2,3,192,128]{3,2,1,0:T(8,128)(2,1)}, u32[]{:S(2)}) copy-start(bf16[2,3,192,128]{3,2,1,0:T(8,128)(2,1)} %copy-done.15) | copy-start | bytes 884740
  214.9 6.5 %copy-start.18 = (bf16[6,3,192,128]{3,2,1,0:T(8,128)(2,1)S(1)}, bf16[6,3,192,128]{3,2,1,0:T(8,128)(2,1)}, u32[]{:S(2)}) copy-start(bf16[6,3,192,128]{3,2,1,0:T(8,128)(2,1)} %copy-done.17) | copy-start | bytes 2654212
  215.0 6.5 %copy-start.20 = (bf16[5,3,192,128]{3,2,1,0:T(8,128)(2,1)S(1)}, bf16[5,3,192,128]{3,2,1,0:T(8,128)(2,1)}, u32[]{:S(2)}) copy-start(bf16[5,3,192,128]{3,2,1,0:T(8,128)(2,1)} %copy-done.19) | copy-start | bytes 2211844
  228.2 2.7 %copy-start.22 = (f32[2,256]{1,0:T(2,128)S(1)}, f32[2,256]{1,0:T(2,128)}, u32[]{:S(2)}) copy-start(f32[2,256]{1,0:T(2,128)} %gain_ref.1) | copy-start | bytes 6148
Sparse Core Ops, SparseCore 0:
  31.0 36.5 all-gather.3
  73.9 38.7 all-gather.5

commit v4 on v3

--- a/solution.py
+++ b/solution.py
@@ -187,8 +187,10 @@
     )(index, normed, *extra, *pieces)
 
 
-def relay_kernel(slots, forward, zl_ref, *refs):
-    *sources, left_ref, right_ref, to_right, to_left = refs
+def relay_kernel(slots, forward, count, zl_ref, *refs):
+    sources, rest = refs[:count], refs[count:]
+    lefts, rest = rest[: len(forward)], rest[len(forward) :]
+    rights, (to_right, to_left) = rest[: len(forward)], rest[-2:]
     zl = zl_ref[0]
     for place, choices in enumerate(slots):
         for source, rows in choices:
@@ -200,90 +202,174 @@
                 to_right[2 * place : 2 * place + 2] = block
                 to_left[2 * place : 2 * place + 2] = block
 
-    for place in range(forward):
-        to_right[2 * len(slots) + place] = left_ref[2 * place]
-        to_left[2 * len(slots) + place] = right_ref[2 * place + 1]
-
-
-def relay(zl, slots, arrays, left, right, forward):
+    end = 2 * len(slots)
+    for left_ref, right_ref, blocks in zip(lefts, rights, forward):
+        for place in range(blocks):
+            to_right[end] = left_ref[2 * place]
+            to_left[end] = right_ref[2 * place + 1]
+            end += 1
+
+
+def relay(row, slots, arrays, lefts, rights, forward, after=()):
     whole = pl.BlockSpec(memory_space=pltpu.VMEM)
-    message = jax.ShapeDtypeStruct((2 * len(slots) + forward, 3, 192, HEAD), jnp.bfloat16)
-    return pl.pallas_call(
-        functools.partial(relay_kernel, slots, forward),
+    message = jax.ShapeDtypeStruct((2 * len(slots) + sum(forward), 3, 192, HEAD), jnp.bfloat16)
+    return pl.pallas_call(
+        functools.partial(relay_kernel, slots, forward, len(arrays)),
         out_shape=(message, message),
-        in_specs=[pl.BlockSpec(memory_space=pltpu.SMEM)] + [whole] * (len(arrays) + 2),
+        in_specs=[pl.BlockSpec(memory_space=pltpu.SMEM)]
+        + [whole] * (len(arrays) + 2 * len(forward))
+        + [pl.BlockSpec(memory_space=pl.ANY)] * len(after),
         out_specs=(whole, whole),
         compiler_params=pltpu.CompilerParams(vmem_limit_bytes=16 * 2**20),
         cost_estimate=pl.CostEstimate(flops=0, bytes_accessed=4 * 2**20, transcendentals=0),
-    )(zl, *arrays, left, right)
-
-
-def gather_weights(own, zl):
+    )(row, *arrays, *lefts, *rights, *after)
+
+
+def mix_kernel(weight_ref, offset_ref, tokens_ref, partner_ref, *refs):
+    mixed_ref = refs[-1]
+    for image in range(2):
+        lam = weight_ref[image].astype(jnp.float32) / 256.0
+        partner = partner_ref[lax.rem(image + offset_ref[image], 2)]
+        mixed = lam * tokens_ref[image].astype(jnp.float32) + (1.0 - lam) * partner.astype(
+            jnp.float32
+        )
+        mixed_ref[image] = mixed.astype(jnp.bfloat16)
+
+
+def mix(weight, offset, tokens, partner, after):
+    whole, scalars = pl.BlockSpec(memory_space=pltpu.VMEM), pl.BlockSpec(memory_space=pltpu.SMEM)
+    return pl.pallas_call(
+        mix_kernel,
+        out_shape=jax.ShapeDtypeStruct(tokens.shape, tokens.dtype),
+        in_specs=[scalars, scalars, whole, whole]
+        + [pl.BlockSpec(memory_space=pl.ANY)] * len(after),
+        out_specs=whole,
+        compiler_params=pltpu.CompilerParams(vmem_limit_bytes=8 * 2**20),
+    )(weight, offset, tokens, partner, *after)
+
+
+def copy_kernel(count, *refs):
+    for source, target in zip(refs[:count], refs[-count:]):
+        target[...] = source[...]
+
+
+def held_back(values, after):
+    whole = pl.BlockSpec(memory_space=pltpu.VMEM)
+    return pl.pallas_call(
+        functools.partial(copy_kernel, len(values)),
+        out_shape=[jax.ShapeDtypeStruct(value.shape, value.dtype) for value in values],
+        in_specs=[whole] * len(values) + [pl.BlockSpec(memory_space=pl.ANY)] * len(after),
+        out_specs=[whole] * len(values),
+        compiler_params=pltpu.CompilerParams(vmem_limit_bytes=8 * 2**20),
+    )(*values, *after)
+
+
+def other_kernel(zh_ref, first_ref, second_ref, *refs):
+    refs[-1][0:256] = first_ref[...]
+    refs[-1][256:512] = second_ref[1 - zh_ref[0]]
+
+
+def other_half(zh, first_image, second_images, after):
+    whole = pl.BlockSpec(memory_space=pltpu.VMEM)
+    return pl.pallas_call(
+        other_kernel,
+        out_shape=jax.ShapeDtypeStruct((512, 384), jnp.bfloat16),
+        in_specs=[pl.BlockSpec(memory_space=pltpu.SMEM), whole, whole]
+        + [pl.BlockSpec(memory_space=pl.ANY)] * len(after),
+        out_specs=whole,
+        compiler_params=pltpu.CompilerParams(vmem_limit_bytes=8 * 2**20),
+    )(zh, first_image, second_images, *after)
+
+
+def either_kernel(zl_ref, upper_ref, lower_ref, *refs):
+    @pl.when(zl_ref[0] >= 4)
+    def _():
+        refs[-1][...] = upper_ref[...]
+
+    @pl.when(zl_ref[0] < 4)
+    def _():
+        refs[-1][...] = lower_ref[...]
+
+
+def either(row, upper, lower, after):
+    whole = pl.BlockSpec(memory_space=pltpu.VMEM)
+    return pl.pallas_call(
+        either_kernel,
+        out_shape=jax.ShapeDtypeStruct(upper.shape, upper.dtype),
+        in_specs=[pl.BlockSpec(memory_space=pltpu.SMEM), whole, whole]
+        + [pl.BlockSpec(memory_space=pl.ANY)] * len(after),
+        out_specs=whole,
+        compiler_params=pltpu.CompilerParams(vmem_limit_bytes=8 * 2**20),
+    )(row, upper, lower, *after)
+
+
+def per_device(tokens, mix_weight, partner_offset, ln_gain, qkv_weight, qk_gain):
+    x, zl, zh = lax.axis_index("x"), lax.axis_index("zl"), lax.axis_index("zh")
+
+    halves = jnp.stack([qkv_weight[:, :, :HEAD], qkv_weight[:, :, HEAD:]])
+    partner_block = previous_images(tokens)
+    a1 = along_line(halves, up=range(0, 7))
+    b1 = along_line(halves, down=range(1, 8))
+    sent, left, right = [halves], [along_x(halves, 1)], [along_x(halves, -1)]
+
+    mixed = mix(
+        mix_weight, partner_offset, tokens, partner_block, [a1, b1, left[0], right[0]]
+    )
+    own_features = lax.all_gather(mixed.reshape(512, 384), ("y", "c"))
+    second_images = lax.all_gather(mixed[1], "zh")
+    first_image = along_z(mixed[0], 8)
+
     row = zl.reshape(1)
-    left, right, sent = [along_x(own, 1)], [along_x(own, -1)], [(own, own)]
-
-    def group(slots, arrays):
-        forward = left[-1].shape[0] // 2 if len(left) == 1 else 2
-        to_right, to_left = relay(row, slots, arrays, left[-1], right[-1], forward)
-        sent.append((to_right, to_left))
+
+    def send(slots, arrays, forward, after=()):
+        lefts = [left[group] for group, _ in forward]
+        rights = [right[group] for group, _ in forward]
+        to_right, to_left = relay(
+            row, slots, arrays, lefts, rights, tuple(blocks for _, blocks in forward), after
+        )
+        sent.append(to_right)
         left.append(along_x(to_right, 1))
         right.append(along_x(to_left, -1))
 
-    a1 = along_line(own, up=range(0, 7))
-    b1 = along_line(own, down=range(1, 8))
     a2 = along_line(a1, up=range(1, 7))
     b2 = along_line(b1, down=range(1, 7))
-    group(
+    send(
         [[(0, range(1, 8)), (3, (0,))], [(1, range(0, 7)), (2, (7,))]],
         [a1, b1, a2, b2],
+        [],
     )
     a3 = along_line(a2, up=range(2, 7))
     b3 = along_line(b2, down=range(1, 6))
     a4 = along_line(a3, up=range(3, 7))
     b4 = along_line(b3, down=range(1, 5))
-    m4 = jnp.where(zl >= 4, a4, b4)
-    group(
+    m4 = either(row, a4, b4, [left[1], right[1]])
+    send(
         [
             [(0, range(2, 7)), (3, (0, 1)), (4, (7,))],
             [(1, range(1, 6)), (2, (6, 7)), (4, (0,))],
         ],
         [a2, b2, a3, b3, m4],
+        [(0, 1)],
     )
     m5 = along_line(m4, up=range(4, 7), down=range(1, 4))
     m6 = along_line(m5, up=range(5, 7), down=range(1, 3))
-    group(
+    send(
         [
             [(0, range(1, 7)), (1, (0, 7))],
             [(1, (1, 2, 5, 6)), (2, (0, 7)), (3, (4,)), (4, (3,))],
         ],
         [m4, m5, m6, a3, b3],
-    )
-    m7 = along_line(m6, up=(6,), down=(1,))
-    group(
+        [(1, 2)],
+    )
+    other = other_half(zh.reshape(1), first_image, second_images, [m5])
+    other_features = lax.all_gather(other, ("y", "c"))
+    (held,) = held_back([m6], [left[2], right[2]])
+    m7 = along_line(held, up=(6,), down=(1,))
+    send(
         [[(0, (0, 7)), (1, (1, 6)), (2, (3, 5)), (3, (2, 4))]],
         [m7, m6, a3, b3],
-    )
-    last = along_x(left[-1][0:1], 1), along_x(right[-1][1:2], -1)
-    return sent, left, right, last
-
-
-def per_device(tokens, mix_weight, partner_offset, ln_gain, qkv_weight, qk_gain):
-    x, zl, zh = lax.axis_index("x"), lax.axis_index("zl"), lax.axis_index("zh")
-
-    partner_block = previous_images(tokens)
-    lam = (mix_weight.astype(jnp.float32) / 256.0)[:, None, None]
-    first = ((jnp.arange(2, dtype=jnp.int32) + partner_offset) % 2 == 0)[:, None, None]
-    partner = jnp.where(first, partner_block[0], partner_block[1])
-    mixed = lam * tokens.astype(jnp.float32) + (1.0 - lam) * partner.astype(jnp.float32)
-    mixed = mixed.astype(jnp.bfloat16)
-
-    ahead = along_z(along_z(mixed[0], 4), 4)
-    behind = along_z(along_z(mixed[1], -4), -4)
-    own_features = lax.all_gather(mixed.reshape(512, 384), ("y", "c"))
-    other_features = lax.all_gather(jnp.concatenate([ahead, behind]), ("y", "c"))
-
-    halves = jnp.stack([qkv_weight[:, :, :HEAD], qkv_weight[:, :, HEAD:]])
-    sent, left, right, (last_left, last_right) = gather_weights(halves, zl)
+        [(2, 2)],
+    )
 
     sources = jnp.asarray(SLOT_SOURCES)[zl]
     block_of = ((x + jnp.arange(4, dtype=jnp.int32)) % 4 * 8)[:, None] + sources[None, :]
@@ -307,31 +393,37 @@
             (which, ((a[0] + base, a[1]), (b[0] + base, b[1]))) for which, (a, b) in blocks
         ]
 
-    first_blocks, pieces = [], []
-    for group, (slots_in, opposite) in enumerate(
-        [((0,), ()), ((1, 2), (0,)), ((3, 4), (1, 2)), ((5, 6), (3, 4))]
-    ):
+    def group_blocks(slots_in, opposite):
         blocks = []
         for place, slot in enumerate(slots_in):
             blocks += three(slot, place)
         for place, slot in enumerate(opposite):
             tail = 2 * len(slots_in) + place
             blocks.append((16 + slot, ((1, tail), (2, tail))))
-        first_blocks += at(blocks, 3 * group)
-        pieces += [sent[group][0], left[group], right[group]]
+        return blocks
+
+    def arrays(group):
+        return [sent[group], left[group], right[group]]
+
+    first_blocks, pieces = [], []
+    for group, (slots_in, opposite) in enumerate(
+        [((0,), ()), ((1, 2), ()), ((3, 4), (0,)), ((5, 6), (1, 2))]
+    ):
+        first_blocks += at(group_blocks(slots_in, opposite), 3 * group)
+        pieces += arrays(group)
     acc_shape = jax.ShapeDtypeStruct((3, 512, 256), jnp.float32)
     acc = project(first_kernel, first_blocks, index, normed, [], pieces, acc_shape)
-    blocks = three(7, 0) + [(16 + 5, ((1, 2), (2, 2))), (16 + 6, ((1, 3), (2, 3)))]
+    send([], [], [(3, 2), (4, 1)], [acc])
     acc = project(
-        next_kernel, blocks, index, normed, [acc], [sent[4][0], left[4], right[4]], acc_shape
+        next_kernel, group_blocks((7,), (3, 4)), index, normed, [acc], arrays(4), acc_shape
     )
     out = project(
         last_kernel,
-        [(16 + 7, ((0, 0), (1, 0)))],
+        at(group_blocks((), (5, 6, 7)), -1),
         index,
         normed,
         [acc, qk_gain],
-        [last_left, last_right],
+        arrays(5)[1:],
         jax.ShapeDtypeStruct((512, 256), jnp.bfloat16),
         [pltpu.VMEM((3, 512, 256), jnp.float32)],
     )

time: 243 us -> 221 us (0.909)
  the two profiles are of different devices: /device:TPU:6 before, /device:TPU:486 now
where the time goes in v4:
time: 221 us; the launch traced here: 220 us
  waiting for transfers between devices  71.8 us (32%)
  starting transfers between devices  62 us (28%)
  Pallas kernels  32.1 us (15%)
  blocking collectives  22.6 us (10%)
  local copies, waits for them, and re-layouts  15.6 us (7%)
  between operations  13.9 us (6%)
    ppermute x25, waiting for transfers between devices, move(): return lax.ppermute(value, AXES, pairs)  71.8 us
    ppermute x25, starting transfers between devices, move(): return lax.ppermute(value, AXES, pairs)  62 us
    all_gather x1, blocking collectives, per_device(): second_images = lax.all_gather(mixed[1], 'zh')  22.6 us
    pallas_call x3, Pallas kernels, project(): pl.pallas_call(functools.partial(kernel, blocks), out_shape=out_shape, in...  13 us
    unnamed x42, local copies, waits for them, and re-layouts  10.7 us
    pallas_call x5, Pallas kernels, relay(): pl.pallas_call(functools.partial(relay_kernel, slots, forward, len(arrays...  7.72 us
    pallas_call x1, Pallas kernels, norm_tokens(): pl.pallas_call(norm_kernel, out_shape=jax.ShapeDtypeStruct((32, 512, 192)...  6.42 us
  transfers between devices with their start and end apart: 27, of which 11 were waited for; matrix products, arithmetic and copies ran while one was open for 3% of the time, Pallas kernels for 12%

profile of v4, /device:TPU:486, one launch (start us, length us, event | category | flops | bytes accessed | tf_op | source)
XLA Modules:
  0.0 219.6 jit_solution(1080543361427884352)
XLA Ops:
  6.5 2.9 %collective-permute-start = (bf16[2,256,384]{2,1,0:T(8,128)(2,1)}, bf16[2,256,384]{2,1,0:T(8,128)(2,1)S(1)}, u32[]{:S(2)}, u32[]{:S(2)}) collective-permute-start(bf16[2,256,384]{2,1,0:T(8,128)(2,1)} %tokens_ref.1), channel_id=1, source_target_pairs={{0,496},{1,497},{2,498},{3,499},{4,500},{5,501},{6,502},{7,503},{8... | collective-permute-start | bytes 1179656 | tf_op jit(solution)/shard_map/ppermute | solution.py:44
  9.5 1.0 slice_bitcast_fusion.2
  10.5 1.3 collective-permute-start.1
  11.8 4.6 %collective-permute-start.2 = (bf16[2,3,192,128]{3,2,1,0:T(8,128)(2,1)S(1)}, bf16[2,3,192,128]{3,2,1,0:T(8,128)(2,1)S(1)}, u32[]{:S(2)}, u32[]{:S(2)}) collective-permute-start(bf16[2,3,192,128]{3,2,1,0:T(8,128)(2,1)S(1)} %pad_maximum_fusion.refs_0_), channel_id=1, source_target_pairs={{16,0},{17,1},{18,2},{19,3},{20,4},{21,5},{22,6},{23,7},{24,8},{25... | collective-permute-start | bytes 884744 | tf_op jit(solution)/shard_map/ppermute | solution.py:44
  16.4 2.4 %collective-permute-start.3 = (bf16[2,3,192,128]{3,2,1,0:T(8,128)(2,1)S(1)}, bf16[2,3,192,128]{3,2,1,0:T(8,128)(2,1)S(1)}, u32[]{:S(2)}, u32[]{:S(2)}) collective-permute-start(bf16[2,3,192,128]{3,2,1,0:T(8,128)(2,1)S(1)} %pad_maximum_fusion.refs_0_), channel_id=1, source_target_pairs={{0,128},{1,129},{2,130},{3,131},{4,132},{5,133},{6,134},{7,135},{8... | collective-permute-start | bytes 884744 | tf_op jit(solution)/shard_map/ppermute | solution.py:44
  18.8 3.5 %collective-permute-start.4 = (bf16[2,3,192,128]{3,2,1,0:T(8,128)(2,1)S(1)}, bf16[2,3,192,128]{3,2,1,0:T(8,128)(2,1)S(1)}, u32[]{:S(2)}, u32[]{:S(2)}) collective-permute-start(bf16[2,3,192,128]{3,2,1,0:T(8,128)(2,1)S(1)} %pad_maximum_fusion.refs_0_), channel_id=1, source_target_pairs={{0,384},{1,385},{2,386},{3,387},{4,388},{5,389},{6,390},{7,391},{8... | collective-permute-start | bytes 884744 | tf_op jit(solution)/shard_map/ppermute | solution.py:44
  22.2 7.1 %collective-permute-done.1.refs_0_ = bf16[2,3,192,128]{3,2,1,0:T(8,128)(2,1)S(1)} collective-permute-done((bf16[2,3,192,128]{3,2,1,0:T(8,128)(2,1)S(1)}, bf16[2,3,192,128]{3,2,1,0:T(8,128)(2,1)S(1)}, u32[]{:S(2)}, u32[]{:S(2)}) %collective-permute-start.1) | collective-permute-done | bytes 294944 | tf_op jit(solution)/shard_map/ppermute | solution.py:44
  29.3 5.6 %collective-permute-done.4.refs_3_.refs_6_.refs_2_ = bf16[2,3,192,128]{3,2,1,0:T(8,128)(2,1)S(1)} collective-permute-done((bf16[2,3,192,128]{3,2,1,0:T(8,128)(2,1)S(1)}, bf16[2,3,192,128]{3,2,1,0:T(8,128)(2,1)S(1)}, u32[]{:S(2)}, u32[]{:S(2)}) %collective-permute-start.4) | collective-permute-done | bytes 294944 | tf_op jit(solution)/shard_map/ppermute | solution.py:44
  34.9 1.1 copy-done.16
  36.0 0.7 copy-done.19
  36.6 0.7 copy-done.20
  37.3 1.5 shard_map.73
  38.8 1.3 collective-permute-start.6
  40.1 0.7 collective-permute-start.9
  40.8 8.8 %collective-permute-done.6.refs_2_.refs_0_ = bf16[2,3,192,128]{3,2,1,0:T(8,128)(2,1)S(1)} collective-permute-done((bf16[2,3,192,128]{3,2,1,0:T(8,128)(2,1)S(1)}, bf16[2,3,192,128]{3,2,1,0:T(8,128)(2,1)S(1)}, u32[]{:S(2)}, u32[]{:S(2)}) %collective-permute-start.6) | collective-permute-done | bytes 294944 | tf_op jit(solution)/shard_map/ppermute | solution.py:44
  49.7 1.3 collective-permute-start.7
  51.0 0.7 collective-permute-start.10
  51.6 0.2 shard_map.74
  51.8 1.9 collective-permute-start.12
  53.8 0.8 copy-done.14
  54.6 3.9 %collective-permute-start.13 = (bf16[4,3,192,128]{3,2,1,0:T(8,128)(2,1)S(1)}, bf16[4,3,192,128]{3,2,1,0:T(8,128)(2,1)S(1)}, u32[]{:S(2)}, u32[]{:S(2)}) collective-permute-start(bf16[4,3,192,128]{3,2,1,0:T(8,128)(2,1)S(1)} %get-tuple-element.16), channel_id=1, source_target_pairs={{0,384},{1,385},{2,386},{3,387},{4,388},{5,389},{6,390},{7,391},{8... | collective-permute-start | bytes 1769480 | tf_op jit(solution)/shard_map/ppermute | solution.py:44
  58.5 1.1 collective-permute-done.7.refs_2_.refs_3_
  59.6 1.3 collective-permute-start.8
  60.9 0.7 collective-permute-start.11
  61.6 7.2 %collective-permute-done.8.upper_ref = bf16[2,3,192,128]{3,2,1,0:T(8,128)(2,1)S(1)} collective-permute-done((bf16[2,3,192,128]{3,2,1,0:T(8,128)(2,1)S(1)}, bf16[2,3,192,128]{3,2,1,0:T(8,128)(2,1)S(1)}, u32[]{:S(2)}, u32[]{:S(2)}) %collective-permute-start.8) | collective-permute-done | bytes 294944 | tf_op jit(solution)/shard_map/ppermute | solution.py:44
  68.8 3.3 %collective-permute-done.13.refs_1_.refs_6_.refs_5_ = bf16[4,3,192,128]{3,2,1,0:T(8,128)(2,1)S(1)} collective-permute-done((bf16[4,3,192,128]{3,2,1,0:T(8,128)(2,1)S(1)}, bf16[4,3,192,128]{3,2,1,0:T(8,128)(2,1)S(1)}, u32[]{:S(2)}, u32[]{:S(2)}) %collective-permute-start.13) | collective-permute-done | bytes 589856 | tf_op jit(solution)/shard_map/ppermute | solution.py:44
  72.1 1.3 collective-permute-start.14
  73.4 1.8 fusion.8
  75.2 6.1 %collective-permute-start.5 = (bf16[256,384]{1,0:T(8,128)(2,1)}, bf16[256,384]{1,0:T(8,128)(2,1)}, u32[]{:S(2)}, u32[]{:S(2)}) collective-permute-start(bf16[256,384]{1,0:T(8,128)(2,1)} %get-tuple-element.26), channel_id=1, source_target_pairs={{0,8},{1,9},{2,10},{3,11},{4,12},{5,13},{6,14},{7,15},{8,0},{9,1},... | collective-permute-start | bytes 589832 | tf_op jit(solution)/shard_map/ppermute | solution.py:44
  81.3 22.6 %all_gather.13.second_ref = bf16[2,256,384]{2,1,0:T(8,128)(2,1)S(1)} all-gather(bf16[1,256,384]{2,1,0:T(8,128)(2,1)} %get-tuple-element.25), channel_id=1, replica_groups=mesh['x'=4,'zl'=8,'zh'=2,'y'=4,'c'=2] {'zh'}, dimensions={0}, use_global_device_ids=true | all-gather | bytes 589824 | tf_op jit(solution)/shard_map/all_gather | solution.py:319
  103.9 5.7 %collective-permute-done.14.refs_0_.refs_1_ = bf16[2,3,192,128]{3,2,1,0:T(8,128)(2,1)S(1)} collective-permute-done((bf16[2,3,192,128]{3,2,1,0:T(8,128)(2,1)S(1)}, bf16[2,3,192,128]{3,2,1,0:T(8,128)(2,1)S(1)}, u32[]{:S(2)}, u32[]{:S(2)}) %collective-permute-start.14) | collective-permute-done | bytes 294944 | tf_op jit(solution)/shard_map/ppermute | solution.py:44
  109.6 1.8 shard_map.76
  111.5 1.3 shard_map.78
  112.8 1.9 collective-permute-start.15
  114.7 3.9 %collective-permute-start.16 = (bf16[5,3,192,128]{3,2,1,0:T(8,128)(2,1)}, bf16[5,3,192,128]{3,2,1,0:T(8,128)(2,1)S(1)}, u32[]{:S(2)}, u32[]{:S(2)}) collective-permute-start(bf16[5,3,192,128]{3,2,1,0:T(8,128)(2,1)} %get-tuple-element.18), channel_id=1, source_target_pairs={{0,384},{1,385},{2,386},{3,387},{4,388},{5,389},{6,390},{7,391},{8... | collective-permute-start | bytes 2211848 | tf_op jit(solution)/shard_map/ppermute | solution.py:44
  118.6 1.3 collective-permute-start.17
  119.9 18.6 %collective-permute-done.17.refs_2_.refs_0_.refs_1_ = bf16[2,3,192,128]{3,2,1,0:T(8,128)(2,1)} collective-permute-done((bf16[2,3,192,128]{3,2,1,0:T(8,128)(2,1)}, bf16[2,3,192,128]{3,2,1,0:T(8,128)(2,1)}, u32[]{:S(2)}, u32[]{:S(2)}) %collective-permute-start.17) | collective-permute-done | bytes 294944 | tf_op jit(solution)/shard_map/ppermute | solution.py:44
  138.5 1.0 copy-done.11
  139.5 2.4 %shard_map.79 = (bf16[6,3,192,128]{3,2,1,0:T(8,128)(2,1)}, bf16[6,3,192,128]{3,2,1,0:T(8,128)(2,1)}) custom-call(s32[1]{0:T(128)} %bitcast.6.zl_ref, bf16[2,3,192,128]{3,2,1,0:T(8,128)(2,1)S(1)} %shard_map.75.refs_4_.refs_0_, bf16[2,3,192,128]{3,2,1,0:T(8,128)(2,1)S(1)} %copy-done.11, ...), custom_call_target="tpu_custom_call" | custom-call | bytes 4194304 | tf_op jit(solution)/shard_map/pallas_call | solution.py:216
  141.9 3.4 %collective-permute-start.18 = (bf16[6,3,192,128]{3,2,1,0:T(8,128)(2,1)}, bf16[6,3,192,128]{3,2,1,0:T(8,128)(2,1)S(1)}, u32[]{:S(2)}, u32[]{:S(2)}) collective-permute-start(bf16[6,3,192,128]{3,2,1,0:T(8,128)(2,1)} %get-tuple-element.19.refs_9_), channel_id=1, source_target_pairs={{0,128},{1,129},{2,130},{3,131},{4,132},{5,133},{6,134},{7,135},{8... | collective-permute-start | bytes 2654216 | tf_op jit(solution)/shard_map/ppermute | solution.py:44
  145.3 2.4 %collective-permute-start.19 = (bf16[6,3,192,128]{3,2,1,0:T(8,128)(2,1)}, bf16[6,3,192,128]{3,2,1,0:T(8,128)(2,1)}, u32[]{:S(2)}, u32[]{:S(2)}) collective-permute-start(bf16[6,3,192,128]{3,2,1,0:T(8,128)(2,1)} %get-tuple-element.20), channel_id=1, source_target_pairs={{0,384},{1,385},{2,386},{3,387},{4,388},{5,389},{6,390},{7,391},{8... | collective-permute-start | bytes 2654216 | tf_op jit(solution)/shard_map/ppermute | solution.py:44
  147.8 1.7 shard_map.81
  149.5 1.3 collective-permute-start.20
  150.8 0.7 dynamic-slice_bitcast_fusion
  151.6 7.3 %collective-permute-done.20.refs_0_ = bf16[2,3,192,128]{3,2,1,0:T(8,128)(2,1)} collective-permute-done((bf16[2,3,192,128]{3,2,1,0:T(8,128)(2,1)}, bf16[2,3,192,128]{3,2,1,0:T(8,128)(2,1)}, u32[]{:S(2)}, u32[]{:S(2)}) %collective-permute-start.20) | collective-permute-done | bytes 294944 | tf_op jit(solution)/shard_map/ppermute | solution.py:44
  158.9 1.0 copy-done.3
  159.9 1.0 copy-done.5
  160.8 2.2 %shard_map.82 = (bf16[4,3,192,128]{3,2,1,0:T(8,128)(2,1)}, bf16[4,3,192,128]{3,2,1,0:T(8,128)(2,1)}) custom-call(s32[1]{0:T(128)} %bitcast.6.zl_ref, bf16[2,3,192,128]{3,2,1,0:T(8,128)(2,1)} %collective-permute-done.20.refs_0_, bf16[2,3,192,128]{3,2,1,0:T(8,128)(2,1)} %collective-permute-done.17.refs_2_.refs_0_.refs_1_, ...), custom_call_target="tpu_custom_call" | custom-call | bytes 4194304 | tf_op jit(solution)/shard_map/pallas_call | solution.py:216
  163.1 4.9 %collective-permute-start.21 = (bf16[4,3,192,128]{3,2,1,0:T(8,128)(2,1)}, bf16[4,3,192,128]{3,2,1,0:T(8,128)(2,1)}, u32[]{:S(2)}, u32[]{:S(2)}) collective-permute-start(bf16[4,3,192,128]{3,2,1,0:T(8,128)(2,1)} %get-tuple-element.21.refs_0_), channel_id=1, source_target_pairs={{0,128},{1,129},{2,130},{3,131},{4,132},{5,133},{6,134},{7,135},{8... | collective-permute-start | bytes 1769480 | tf_op jit(solution)/shard_map/ppermute | solution.py:44
  167.9 1.9 collective-permute-start.22
  169.9 1.4 reshape.37
  171.3 1.4 fusion.gain_ref
  172.7 1.9 copy-done
  174.6 1.9 copy-done.1
  176.5 0.7 copy-done.17
  177.2 6.4 %shard_map.77.normed_ref = bf16[32,512,192]{2,1,0:T(8,128)(2,1)S(1)} custom-call(bf16[8,512,384]{2,1,0:T(8,128)(2,1)S(1)} %copy-done, bf16[8,512,384]{2,1,0:T(8,128)(2,1)S(1)} %bitcast.15, f32[16,384]{1,0:T(8,128)S(1)} %copy-done.17), custom_call_target="tpu_custom_call" | custom-call | flops 25165824 | bytes 14680064 | tf_op jit(solution)/shard_map/pallas_call | solution.py:101
  183.7 6.7 %shard_map.80.held_ref.refs_4_ = f32[3,512,256]{2,1,0:T(8,128)S(1)} custom-call(s32[32]{0:T(128)S(1)} %fusion.1.index_ref, bf16[32,512,192]{2,1,0:T(8,128)(2,1)S(1)} %shard_map.77.normed_ref, bf16[2,3,192,128]{3,2,1,0:T(8,128)(2,1)S(1)} %copy-done.13, bf16[2,3,192,128]{3,2,1,0:T(8,128)(2,1)S(1)} %copy-done.7, bf16[2,3,192,128]{3,2,1,0:T(8,128)(2,1)S(1)} %copy-done.9, ...), custom_call_target="tpu_custom_call" | custom-call | flops 3623878656 | bytes 15466496 | tf_op jit(solution)/shard_map/pallas_call | solution.py:175
  190.5 1.6 shard_map.84
  192.1 5.1 %collective-permute-start.23 = (bf16[3,3,192,128]{3,2,1,0:T(8,128)(2,1)S(1)}, bf16[3,3,192,128]{3,2,1,0:T(8,128)(2,1)S(1)}, u32[]{:S(2)}, u32[]{:S(2)}) collective-permute-start(bf16[3,3,192,128]{3,2,1,0:T(8,128)(2,1)S(1)} %get-tuple-element.23), channel_id=1, source_target_pairs={{0,128},{1,129},{2,130},{3,131},{4,132},{5,133},{6,134},{7,135},{8... | collective-permute-start | bytes 1327112 | tf_op jit(solution)/shard_map/ppermute | solution.py:44
  197.2 2.1 collective-permute-start.24
  199.3 2.6 %shard_map.83.held_ref = f32[3,512,256]{2,1,0:T(8,128)S(1)} custom-call(s32[32]{0:T(128)S(1)} %fusion.1.index_ref, bf16[32,512,192]{2,1,0:T(8,128)(2,1)S(1)} %shard_map.77.normed_ref, f32[3,512,256]{2,1,0:T(8,128)S(1)} %shard_map.80.held_ref.refs_4_, bf16[4,3,192,128]{3,2,1,0:T(8,128)(2,1)} %get-tuple-element.21.refs_0_, ...), custom_call_target="tpu_custom_call" | custom-call | flops 754974720 | bytes 9863168 | tf_op jit(solution)/shard_map/pallas_call | solution.py:175
  202.0 1.9 collective-permute-done.23.refs_0_
  203.8 5.3 %collective-permute-done.24.refs_1_ = bf16[3,3,192,128]{3,2,1,0:T(8,128)(2,1)S(1)} collective-permute-done((bf16[3,3,192,128]{3,2,1,0:T(8,128)(2,1)S(1)}, bf16[3,3,192,128]{3,2,1,0:T(8,128)(2,1)S(1)}, u32[]{:S(2)}, u32[]{:S(2)}) %collective-permute-start.24) | collective-permute-done | bytes 442400 | tf_op jit(solution)/shard_map/ppermute | solution.py:44
  209.2 3.6 %shard_map.85 = bf16[512,256]{1,0:T(8,128)(2,1)} custom-call(s32[32]{0:T(128)S(1)} %fusion.1.index_ref, bf16[32,512,192]{2,1,0:T(8,128)(2,1)S(1)} %shard_map.77.normed_ref, f32[3,512,256]{2,1,0:T(8,128)S(1)} %shard_map.83.held_ref, f32[2,256]{1,0:T(2,128)S(1)} %copy-done.18, bf16[3,3,192,128]{3,2,1,0:T(8,128)(2,1)S(1)} %collective-permute-done.23.refs_0_, ...), custom_call_target="tpu_custom_call" | custom-call | flops 452984832 | bytes 9273344 | tf_op jit(solution)/shard_map/pallas_call | solution.py:175
  (58 shorter events, 0.4 us)
Async XLA Ops:
  6.5 166.1 %all-gather.4.cloned.1.call-start = ((), (), s32[]{:S(2)}) async-start(), calls=%async_computation | async-start | bytes 3538944 | tf_op jit(solution)/shard_map/all_gather | solution.py:318
  6.5 28.3 %collective-permute-start = (bf16[2,256,384]{2,1,0:T(8,128)(2,1)}, bf16[2,256,384]{2,1,0:T(8,128)(2,1)S(1)}, u32[]{:S(2)}, u32[]{:S(2)}) collective-permute-start(bf16[2,256,384]{2,1,0:T(8,128)(2,1)} %tokens_ref.1), channel_id=1, source_target_pairs={{0,496},{1,497},{2,498},{3,499},{4,500},{5,501},{6,502},{7,503},{8... | collective-permute-start | bytes 1179656 | tf_op jit(solution)/shard_map/ppermute | solution.py:44
  10.5 28.3 %copy-start.12 = (bf16[2,3,192,128]{3,2,1,0:T(8,128)(2,1)}, bf16[2,3,192,128]{3,2,1,0:T(8,128)(2,1)S(1)}, u32[]{:S(2)}) copy-start(bf16[2,3,192,128]{3,2,1,0:T(8,128)(2,1)S(1)} %pad_maximum_fusion.refs_0_) | copy-start | bytes 884740
  10.5 18.8 %collective-permute-start.1 = (bf16[2,3,192,128]{3,2,1,0:T(8,128)(2,1)S(1)}, bf16[2,3,192,128]{3,2,1,0:T(8,128)(2,1)S(1)}, u32[]{:S(2)}, u32[]{:S(2)}) collective-permute-start(bf16[2,3,192,128]{3,2,1,0:T(8,128)(2,1)S(1)} %pad_maximum_fusion.refs_0_), channel_id=1, source_target_pairs={{0,16},{1,17},{2,18},{3,19},{4,20},{5,21},{6,22},{7,23},{8,24},{9,... | collective-permute-start | bytes 884744 | tf_op jit(solution)/shard_map/ppermute | solution.py:44
  11.8 17.5 %collective-permute-start.2 = (bf16[2,3,192,128]{3,2,1,0:T(8,128)(2,1)S(1)}, bf16[2,3,192,128]{3,2,1,0:T(8,128)(2,1)S(1)}, u32[]{:S(2)}, u32[]{:S(2)}) collective-permute-start(bf16[2,3,192,128]{3,2,1,0:T(8,128)(2,1)S(1)} %pad_maximum_fusion.refs_0_), channel_id=1, source_target_pairs={{16,0},{17,1},{18,2},{19,3},{20,4},{21,5},{22,6},{23,7},{24,8},{25... | collective-permute-start | bytes 884744 | tf_op jit(solution)/shard_map/ppermute | solution.py:44
  16.4 12.9 %collective-permute-start.3 = (bf16[2,3,192,128]{3,2,1,0:T(8,128)(2,1)S(1)}, bf16[2,3,192,128]{3,2,1,0:T(8,128)(2,1)S(1)}, u32[]{:S(2)}, u32[]{:S(2)}) collective-permute-start(bf16[2,3,192,128]{3,2,1,0:T(8,128)(2,1)S(1)} %pad_maximum_fusion.refs_0_), channel_id=1, source_target_pairs={{0,128},{1,129},{2,130},{3,131},{4,132},{5,133},{6,134},{7,135},{8... | collective-permute-start | bytes 884744 | tf_op jit(solution)/shard_map/ppermute | solution.py:44
  18.8 16.1 %collective-permute-start.4 = (bf16[2,3,192,128]{3,2,1,0:T(8,128)(2,1)S(1)}, bf16[2,3,192,128]{3,2,1,0:T(8,128)(2,1)S(1)}, u32[]{:S(2)}, u32[]{:S(2)}) collective-permute-start(bf16[2,3,192,128]{3,2,1,0:T(8,128)(2,1)S(1)} %pad_maximum_fusion.refs_0_), channel_id=1, source_target_pairs={{0,384},{1,385},{2,386},{3,387},{4,388},{5,389},{6,390},{7,391},{8... | collective-permute-start | bytes 884744 | tf_op jit(solution)/shard_map/ppermute | solution.py:44
  29.3 82.1 %copy-start.6 = (bf16[2,3,192,128]{3,2,1,0:T(8,128)(2,1)}, bf16[2,3,192,128]{3,2,1,0:T(8,128)(2,1)S(1)}, u32[]{:S(2)}) copy-start(bf16[2,3,192,128]{3,2,1,0:T(8,128)(2,1)S(1)} %collective-permute-done.3.refs_2_.refs_5_.refs_1_) | copy-start | bytes 884740
  34.9 76.6 %copy-start.8 = (bf16[2,3,192,128]{3,2,1,0:T(8,128)(2,1)}, bf16[2,3,192,128]{3,2,1,0:T(8,128)(2,1)S(1)}, u32[]{:S(2)}) copy-start(bf16[2,3,192,128]{3,2,1,0:T(8,128)(2,1)S(1)} %collective-permute-done.4.refs_3_.refs_6_.refs_2_) | copy-start | bytes 884740
  34.9 1.1 copy-start.16
  36.0 0.7 copy-start.19
  36.6 0.7 copy-start.20
  38.8 133.9 %all-gather.6.cloned.1.call-start = ((), (), s32[]{:S(2)}) async-start(), calls=%async_computation.1 | async-start | bytes 3538944 | tf_op jit(solution)/shard_map/all_gather | solution.py:365
  38.8 10.8 %collective-permute-start.6 = (bf16[2,3,192,128]{3,2,1,0:T(8,128)(2,1)S(1)}, bf16[2,3,192,128]{3,2,1,0:T(8,128)(2,1)S(1)}, u32[]{:S(2)}, u32[]{:S(2)}) collective-permute-start(bf16[2,3,192,128]{3,2,1,0:T(8,128)(2,1)S(1)} %collective-permute-done.1.refs_0_), channel_id=1, source_target_pairs={{16,32},{17,33},{18,34},{19,35},{20,36},{21,37},{22,38},{23,39},{2... | collective-permute-start | bytes 884744 | tf_op jit(solution)/shard_map/ppermute | solution.py:44
  40.1 10.8 %collective-permute-start.9 = (bf16[2,3,192,128]{3,2,1,0:T(8,128)(2,1)S(1)}, bf16[2,3,192,128]{3,2,1,0:T(8,128)(2,1)S(1)}, u32[]{:S(2)}, u32[]{:S(2)}) collective-permute-start(bf16[2,3,192,128]{3,2,1,0:T(8,128)(2,1)S(1)} %collective-permute-done.2.refs_1_), channel_id=1, source_target_pairs={{16,0},{17,1},{18,2},{19,3},{20,4},{21,5},{22,6},{23,7},{24,8},{25... | collective-permute-start | bytes 884744 | tf_op jit(solution)/shard_map/ppermute | solution.py:44
  49.7 10.0 %collective-permute-start.7 = (bf16[2,3,192,128]{3,2,1,0:T(8,128)(2,1)S(1)}, bf16[2,3,192,128]{3,2,1,0:T(8,128)(2,1)S(1)}, u32[]{:S(2)}, u32[]{:S(2)}) collective-permute-start(bf16[2,3,192,128]{3,2,1,0:T(8,128)(2,1)S(1)} %collective-permute-done.6.refs_2_.refs_0_), channel_id=1, source_target_pairs={{32,48},{33,49},{34,50},{35,51},{36,52},{37,53},{38,54},{39,55},{4... | collective-permute-start | bytes 884744 | tf_op jit(solution)/shard_map/ppermute | solution.py:44
  51.0 10.0 %collective-permute-start.10 = (bf16[2,3,192,128]{3,2,1,0:T(8,128)(2,1)S(1)}, bf16[2,3,192,128]{3,2,1,0:T(8,128)(2,1)S(1)}, u32[]{:S(2)}, u32[]{:S(2)}) collective-permute-start(bf16[2,3,192,128]{3,2,1,0:T(8,128)(2,1)S(1)} %collective-permute-done.9.refs_3_.refs_1_), channel_id=1, source_target_pairs={{16,0},{17,1},{18,2},{19,3},{20,4},{21,5},{22,6},{23,7},{24,8},{25... | collective-permute-start | bytes 884744 | tf_op jit(solution)/shard_map/ppermute | solution.py:44
  51.8 17.0 %collective-permute-start.12 = (bf16[4,3,192,128]{3,2,1,0:T(8,128)(2,1)S(1)}, bf16[4,3,192,128]{3,2,1,0:T(8,128)(2,1)S(1)}, u32[]{:S(2)}, u32[]{:S(2)}) collective-permute-start(bf16[4,3,192,128]{3,2,1,0:T(8,128)(2,1)S(1)} %get-tuple-element.15.refs_3_), channel_id=1, source_target_pairs={{0,128},{1,129},{2,130},{3,131},{4,132},{5,133},{6,134},{7,135},{8... | collective-permute-start | bytes 1769480 | tf_op jit(solution)/shard_map/ppermute | solution.py:44
  53.8 0.8 copy-start.14
  54.6 17.5 %collective-permute-start.13 = (bf16[4,3,192,128]{3,2,1,0:T(8,128)(2,1)S(1)}, bf16[4,3,192,128]{3,2,1,0:T(8,128)(2,1)S(1)}, u32[]{:S(2)}, u32[]{:S(2)}) collective-permute-start(bf16[4,3,192,128]{3,2,1,0:T(8,128)(2,1)S(1)} %get-tuple-element.16), channel_id=1, source_target_pairs={{0,384},{1,385},{2,386},{3,387},{4,388},{5,389},{6,390},{7,391},{8... | collective-permute-start | bytes 1769480 | tf_op jit(solution)/shard_map/ppermute | solution.py:44
  59.6 78.9 %copy-start.2 = (bf16[2,3,192,128]{3,2,1,0:T(8,128)(2,1)}, bf16[2,3,192,128]{3,2,1,0:T(8,128)(2,1)S(1)}, u32[]{:S(2)}) copy-start(bf16[2,3,192,128]{3,2,1,0:T(8,128)(2,1)S(1)} %collective-permute-done.7.refs_2_.refs_3_) | copy-start | bytes 884740
  59.6 9.2 %collective-permute-start.8 = (bf16[2,3,192,128]{3,2,1,0:T(8,128)(2,1)S(1)}, bf16[2,3,192,128]{3,2,1,0:T(8,128)(2,1)S(1)}, u32[]{:S(2)}, u32[]{:S(2)}) collective-permute-start(bf16[2,3,192,128]{3,2,1,0:T(8,128)(2,1)S(1)} %collective-permute-done.7.refs_2_.refs_3_), channel_id=1, source_target_pairs={{48,64},{49,65},{50,66},{51,67},{52,68},{53,69},{54,70},{55,71},{5... | collective-permute-start | bytes 884744 | tf_op jit(solution)/shard_map/ppermute | solution.py:44
  60.9 77.6 %copy-start.4 = (bf16[2,3,192,128]{3,2,1,0:T(8,128)(2,1)}, bf16[2,3,192,128]{3,2,1,0:T(8,128)(2,1)S(1)}, u32[]{:S(2)}) copy-start(bf16[2,3,192,128]{3,2,1,0:T(8,128)(2,1)S(1)} %collective-permute-done.10.refs_3_.refs_4_) | copy-start | bytes 884740
  60.9 7.8 %collective-permute-start.11 = (bf16[2,3,192,128]{3,2,1,0:T(8,128)(2,1)S(1)}, bf16[2,3,192,128]{3,2,1,0:T(8,128)(2,1)S(1)}, u32[]{:S(2)}, u32[]{:S(2)}) collective-permute-start(bf16[2,3,192,128]{3,2,1,0:T(8,128)(2,1)S(1)} %collective-permute-done.10.refs_3_.refs_4_), channel_id=1, source_target_pairs={{16,0},{17,1},{18,2},{19,3},{20,4},{21,5},{22,6},{23,7},{24,8},{25... | collective-permute-start | bytes 884744 | tf_op jit(solution)/shard_map/ppermute | solution.py:44
  72.1 37.5 %collective-permute-start.14 = (bf16[2,3,192,128]{3,2,1,0:T(8,128)(2,1)S(1)}, bf16[2,3,192,128]{3,2,1,0:T(8,128)(2,1)S(1)}, u32[]{:S(2)}, u32[]{:S(2)}) collective-permute-start(bf16[2,3,192,128]{3,2,1,0:T(8,128)(2,1)S(1)} %shard_map.75.refs_4_.refs_0_), channel_id=1, source_target_pairs={{16,0},{17,1},{18,2},{19,3},{20,4},{21,5},{22,6},{23,7},{24,8},{25... | collective-permute-start | bytes 884744 | tf_op jit(solution)/shard_map/ppermute | solution.py:44
  75.2 28.7 %collective-permute-start.5 = (bf16[256,384]{1,0:T(8,128)(2,1)}, bf16[256,384]{1,0:T(8,128)(2,1)}, u32[]{:S(2)}, u32[]{:S(2)}) collective-permute-start(bf16[256,384]{1,0:T(8,128)(2,1)} %get-tuple-element.26), channel_id=1, source_target_pairs={{0,8},{1,9},{2,10},{3,11},{4,12},{5,13},{6,14},{7,15},{8,0},{9,1},... | collective-permute-start | bytes 589832 | tf_op jit(solution)/shard_map/ppermute | solution.py:44
  109.6 5.1 %copy-start.10 = (bf16[2,3,192,128]{3,2,1,0:T(8,128)(2,1)}, bf16[2,3,192,128]{3,2,1,0:T(8,128)(2,1)S(1)}, u32[]{:S(2)}) copy-start(bf16[2,3,192,128]{3,2,1,0:T(8,128)(2,1)S(1)} %collective-permute-done.14.refs_0_.refs_1_) | copy-start | bytes 884740
  112.8 35.0 %collective-permute-start.15 = (bf16[5,3,192,128]{3,2,1,0:T(8,128)(2,1)}, bf16[5,3,192,128]{3,2,1,0:T(8,128)(2,1)S(1)}, u32[]{:S(2)}, u32[]{:S(2)}) collective-permute-start(bf16[5,3,192,128]{3,2,1,0:T(8,128)(2,1)} %get-tuple-element.17.refs_6_), channel_id=1, source_target_pairs={{0,128},{1,129},{2,130},{3,131},{4,132},{5,133},{6,134},{7,135},{8... | collective-permute-start | bytes 2211848 | tf_op jit(solution)/shard_map/ppermute | solution.py:44
  114.7 33.1 %collective-permute-start.16 = (bf16[5,3,192,128]{3,2,1,0:T(8,128)(2,1)}, bf16[5,3,192,128]{3,2,1,0:T(8,128)(2,1)S(1)}, u32[]{:S(2)}, u32[]{:S(2)}) collective-permute-start(bf16[5,3,192,128]{3,2,1,0:T(8,128)(2,1)} %get-tuple-element.18), channel_id=1, source_target_pairs={{0,384},{1,385},{2,386},{3,387},{4,388},{5,389},{6,390},{7,391},{8... | collective-permute-start | bytes 2211848 | tf_op jit(solution)/shard_map/ppermute | solution.py:44
  118.6 19.9 %collective-permute-start.17 = (bf16[2,3,192,128]{3,2,1,0:T(8,128)(2,1)}, bf16[2,3,192,128]{3,2,1,0:T(8,128)(2,1)}, u32[]{:S(2)}, u32[]{:S(2)}) collective-permute-start(bf16[2,3,192,128]{3,2,1,0:T(8,128)(2,1)} %copy-done.10), channel_id=1, source_target_pairs={{16,0},{17,1},{18,2},{19,3},{20,4},{21,5},{22,6},{23,7},{24,8},{25... | collective-permute-start | bytes 884744 | tf_op jit(solution)/shard_map/ppermute | solution.py:44
  138.5 1.0 copy-start.11
  141.9 41.7 %collective-permute-start.18 = (bf16[6,3,192,128]{3,2,1,0:T(8,128)(2,1)}, bf16[6,3,192,128]{3,2,1,0:T(8,128)(2,1)S(1)}, u32[]{:S(2)}, u32[]{:S(2)}) collective-permute-start(bf16[6,3,192,128]{3,2,1,0:T(8,128)(2,1)} %get-tuple-element.19.refs_9_), channel_id=1, source_target_pairs={{0,128},{1,129},{2,130},{3,131},{4,132},{5,133},{6,134},{7,135},{8... | collective-permute-start | bytes 2654216 | tf_op jit(solution)/shard_map/ppermute | solution.py:44
  145.3 38.4 %collective-permute-start.19 = (bf16[6,3,192,128]{3,2,1,0:T(8,128)(2,1)}, bf16[6,3,192,128]{3,2,1,0:T(8,128)(2,1)}, u32[]{:S(2)}, u32[]{:S(2)}) collective-permute-start(bf16[6,3,192,128]{3,2,1,0:T(8,128)(2,1)} %get-tuple-element.20), channel_id=1, source_target_pairs={{0,384},{1,385},{2,386},{3,387},{4,388},{5,389},{6,390},{7,391},{8... | collective-permute-start | bytes 2654216 | tf_op jit(solution)/shard_map/ppermute | solution.py:44
  149.5 9.4 %collective-permute-start.20 = (bf16[2,3,192,128]{3,2,1,0:T(8,128)(2,1)}, bf16[2,3,192,128]{3,2,1,0:T(8,128)(2,1)}, u32[]{:S(2)}, u32[]{:S(2)}) collective-permute-start(bf16[2,3,192,128]{3,2,1,0:T(8,128)(2,1)} %shard_map.81), channel_id=1, source_target_pairs={{16,0},{17,1},{18,2},{19,3},{20,4},{21,5},{22,6},{23,7},{24,8},{25... | collective-permute-start | bytes 884744 | tf_op jit(solution)/shard_map/ppermute | solution.py:44
  158.9 1.0 copy-start.3
  159.8 1.0 copy-start.5
  163.1 27.4 %collective-permute-start.21 = (bf16[4,3,192,128]{3,2,1,0:T(8,128)(2,1)}, bf16[4,3,192,128]{3,2,1,0:T(8,128)(2,1)}, u32[]{:S(2)}, u32[]{:S(2)}) collective-permute-start(bf16[4,3,192,128]{3,2,1,0:T(8,128)(2,1)} %get-tuple-element.21.refs_0_), channel_id=1, source_target_pairs={{0,128},{1,129},{2,130},{3,131},{4,132},{5,133},{6,134},{7,135},{8... | collective-permute-start | bytes 1769480 | tf_op jit(solution)/shard_map/ppermute | solution.py:44
  167.9 22.5 %collective-permute-start.22 = (bf16[4,3,192,128]{3,2,1,0:T(8,128)(2,1)}, bf16[4,3,192,128]{3,2,1,0:T(8,128)(2,1)}, u32[]{:S(2)}, u32[]{:S(2)}) collective-permute-start(bf16[4,3,192,128]{3,2,1,0:T(8,128)(2,1)} %get-tuple-element.22), channel_id=1, source_target_pairs={{0,384},{1,385},{2,386},{3,387},{4,388},{5,389},{6,390},{7,391},{8... | collective-permute-start | bytes 1769480 | tf_op jit(solution)/shard_map/ppermute | solution.py:44
  172.7 1.9 copy-start
  174.6 1.9 copy-start.1
  176.5 0.7 copy-start.17
  177.2 6.5 %copy-start.7 = (bf16[2,3,192,128]{3,2,1,0:T(8,128)(2,1)S(1)}, bf16[2,3,192,128]{3,2,1,0:T(8,128)(2,1)}, u32[]{:S(2)}) copy-start(bf16[2,3,192,128]{3,2,1,0:T(8,128)(2,1)} %copy-done.6) | copy-start | bytes 884740
  177.2 6.5 %copy-start.9 = (bf16[2,3,192,128]{3,2,1,0:T(8,128)(2,1)S(1)}, bf16[2,3,192,128]{3,2,1,0:T(8,128)(2,1)}, u32[]{:S(2)}) copy-start(bf16[2,3,192,128]{3,2,1,0:T(8,128)(2,1)} %copy-done.8) | copy-start | bytes 884740
  177.2 6.5 %copy-start.13 = (bf16[2,3,192,128]{3,2,1,0:T(8,128)(2,1)S(1)}, bf16[2,3,192,128]{3,2,1,0:T(8,128)(2,1)}, u32[]{:S(2)}) copy-start(bf16[2,3,192,128]{3,2,1,0:T(8,128)(2,1)} %copy-done.12) | copy-start | bytes 884740
  177.2 6.5 %copy-start.15 = (bf16[4,3,192,128]{3,2,1,0:T(8,128)(2,1)S(1)}, bf16[4,3,192,128]{3,2,1,0:T(8,128)(2,1)}, u32[]{:S(2)}) copy-start(bf16[4,3,192,128]{3,2,1,0:T(8,128)(2,1)} %copy-done.14) | copy-start | bytes 1769476
  192.1 11.8 %collective-permute-start.23 = (bf16[3,3,192,128]{3,2,1,0:T(8,128)(2,1)S(1)}, bf16[3,3,192,128]{3,2,1,0:T(8,128)(2,1)S(1)}, u32[]{:S(2)}, u32[]{:S(2)}) collective-permute-start(bf16[3,3,192,128]{3,2,1,0:T(8,128)(2,1)S(1)} %get-tuple-element.23), channel_id=1, source_target_pairs={{0,128},{1,129},{2,130},{3,131},{4,132},{5,133},{6,134},{7,135},{8... | collective-permute-start | bytes 1327112 | tf_op jit(solution)/shard_map/ppermute | solution.py:44
  197.2 12.0 %copy-start.18 = (f32[2,256]{1,0:T(2,128)S(1)}, f32[2,256]{1,0:T(2,128)}, u32[]{:S(2)}) copy-start(f32[2,256]{1,0:T(2,128)} %gain_ref.1) | copy-start | bytes 6148
  197.2 11.9 %collective-permute-start.24 = (bf16[3,3,192,128]{3,2,1,0:T(8,128)(2,1)S(1)}, bf16[3,3,192,128]{3,2,1,0:T(8,128)(2,1)S(1)}, u32[]{:S(2)}, u32[]{:S(2)}) collective-permute-start(bf16[3,3,192,128]{3,2,1,0:T(8,128)(2,1)S(1)} %get-tuple-element.24), channel_id=1, source_target_pairs={{0,384},{1,385},{2,386},{3,387},{4,388},{5,389},{6,390},{7,391},{8... | collective-permute-start | bytes 1327112 | tf_op jit(solution)/shard_map/ppermute | solution.py:44
Sparse Core Ops, SparseCore 0:
  38.9 31.8 all-gather.3
  111.6 42.4 all-gather.5

commit v5 on v4

--- a/solution.py
+++ b/solution.py
@@ -48,9 +48,10 @@
     return move(value, lambda x, zl, zh, y, c: (x + by, zl, zh, y, c))
 
 
-def along_z(value, by):
+def along_z_both_ways(value):
     def target(x, zl, zh, y, c):
-        z = (zh * 8 + zl + by) % 16
+        z = zh * 8 + zl
+        z = (z + 4 if z % 2 == 0 else z - 4) % 16
         return x, z % 8, z // 8, y, c
 
     return move(value, target)
@@ -264,23 +265,6 @@
     )(*values, *after)
 
 
-def other_kernel(zh_ref, first_ref, second_ref, *refs):
-    refs[-1][0:256] = first_ref[...]
-    refs[-1][256:512] = second_ref[1 - zh_ref[0]]
-
-
-def other_half(zh, first_image, second_images, after):
-    whole = pl.BlockSpec(memory_space=pltpu.VMEM)
-    return pl.pallas_call(
-        other_kernel,
-        out_shape=jax.ShapeDtypeStruct((512, 384), jnp.bfloat16),
-        in_specs=[pl.BlockSpec(memory_space=pltpu.SMEM), whole, whole]
-        + [pl.BlockSpec(memory_space=pl.ANY)] * len(after),
-        out_specs=whole,
-        compiler_params=pltpu.CompilerParams(vmem_limit_bytes=8 * 2**20),
-    )(zh, first_image, second_images, *after)
-
-
 def either_kernel(zl_ref, upper_ref, lower_ref, *refs):
     @pl.when(zl_ref[0] >= 4)
     def _():
@@ -316,8 +300,7 @@
         mix_weight, partner_offset, tokens, partner_block, [a1, b1, left[0], right[0]]
     )
     own_features = lax.all_gather(mixed.reshape(512, 384), ("y", "c"))
-    second_images = lax.all_gather(mixed[1], "zh")
-    first_image = along_z(mixed[0], 8)
+    halfway = along_z_both_ways(mixed.reshape(512, 384))
 
     row = zl.reshape(1)
 
@@ -340,6 +323,8 @@
     )
     a3 = along_line(a2, up=range(2, 7))
     b3 = along_line(b2, down=range(1, 6))
+    (halfway,) = held_back([halfway], [a3, b3])
+    other = along_z_both_ways(halfway)
     a4 = along_line(a3, up=range(3, 7))
     b4 = along_line(b3, down=range(1, 5))
     m4 = either(row, a4, b4, [left[1], right[1]])
@@ -352,6 +337,8 @@
         [(0, 1)],
     )
     m5 = along_line(m4, up=range(4, 7), down=range(1, 4))
+    (other,) = held_back([other], [m5])
+    other_features = lax.all_gather(other, ("y", "c"))
     m6 = along_line(m5, up=range(5, 7), down=range(1, 3))
     send(
         [
@@ -361,10 +348,7 @@
         [m4, m5, m6, a3, b3],
         [(1, 2)],
     )
-    other = other_half(zh.reshape(1), first_image, second_images, [m5])
-    other_features = lax.all_gather(other, ("y", "c"))
-    (held,) = held_back([m6], [left[2], right[2]])
-    m7 = along_line(held, up=(6,), down=(1,))
+    m7 = along_line(m6, up=(6,), down=(1,))
     send(
         [[(0, (0, 7)), (1, (1, 6)), (2, (3, 5)), (3, (2, 4))]],
         [m7, m6, a3, b3],

time: 221 us -> 207 us (0.937)
  the two profiles are of different devices: /device:TPU:486 before, /device:TPU:6 now
where the time goes in v5:
time: 207 us; the launch traced here: 206 us
  waiting for transfers between devices  82 us (40%)
  starting transfers between devices  68.7 us (33%)
  Pallas kernels  28.7 us (14%)
  between operations  13.9 us (7%)
  local copies, waits for them, and re-layouts  12.1 us (6%)
    ppermute x26, waiting for transfers between devices, move(): return lax.ppermute(value, AXES, pairs)  81.9 us
    ppermute x26, starting transfers between devices, move(): return lax.ppermute(value, AXES, pairs)  68.6 us
    pallas_call x3, Pallas kernels, project(): pl.pallas_call(functools.partial(kernel, blocks), out_shape=out_shape, in...  13.1 us
    unnamed x36, local copies, waits for them, and re-layouts  9.58 us
    pallas_call x5, Pallas kernels, relay(): pl.pallas_call(functools.partial(relay_kernel, slots, forward, len(arrays...  6.96 us
    pallas_call x1, Pallas kernels, norm_tokens(): pl.pallas_call(norm_kernel, out_shape=jax.ShapeDtypeStruct((32, 512, 192)...  6.42 us
  transfers between devices with their start and end apart: 28, of which 13 were waited for; matrix products, arithmetic and copies ran while one was open for 1% of the time, Pallas kernels for 11%

profile of v5, /device:TPU:6, one launch (start us, length us, event | category | flops | bytes accessed | tf_op | source)
XLA Modules:
  0.0 205.5 jit_solution(1469389818256931683)
XLA Ops:
  6.5 13.4 %collective-permute-start = (bf16[2,256,384]{2,1,0:T(8,128)(2,1)}, bf16[2,256,384]{2,1,0:T(8,128)(2,1)S(1)}, u32[]{:S(2)}, u32[]{:S(2)}) collective-permute-start(bf16[2,256,384]{2,1,0:T(8,128)(2,1)} %tokens_ref.1), channel_id=1, source_target_pairs={{0,496},{1,497},{2,498},{3,499},{4,500},{5,501},{6,502},{7,503},{8... | collective-permute-start | bytes 1179656 | tf_op jit(solution)/shard_map/ppermute | solution.py:44
  20.0 1.0 slice_bitcast_fusion.1
  21.0 1.3 collective-permute-start.1
  22.3 1.3 collective-permute-start.2
  23.6 4.3 %collective-permute-start.3 = (bf16[2,3,192,128]{3,2,1,0:T(8,128)(2,1)S(1)}, bf16[2,3,192,128]{3,2,1,0:T(8,128)(2,1)S(1)}, u32[]{:S(2)}, u32[]{:S(2)}) collective-permute-start(bf16[2,3,192,128]{3,2,1,0:T(8,128)(2,1)S(1)} %pad_maximum_fusion.refs_0_), channel_id=1, source_target_pairs={{0,128},{1,129},{2,130},{3,131},{4,132},{5,133},{6,134},{7,135},{8... | collective-permute-start | bytes 884744 | tf_op jit(solution)/shard_map/ppermute | solution.py:44
  27.9 1.9 collective-permute-start.4
  29.9 0.7 copy-done.10
  30.6 4.3 %collective-permute-done.1.refs_0_ = bf16[2,3,192,128]{3,2,1,0:T(8,128)(2,1)S(1)} collective-permute-done((bf16[2,3,192,128]{3,2,1,0:T(8,128)(2,1)S(1)}, bf16[2,3,192,128]{3,2,1,0:T(8,128)(2,1)S(1)}, u32[]{:S(2)}, u32[]{:S(2)}) %collective-permute-start.1) | collective-permute-done | bytes 294944 | tf_op jit(solution)/shard_map/ppermute | solution.py:44
  34.8 4.4 %collective-permute-done.4.refs_3_.refs_6_.refs_2_ = bf16[2,3,192,128]{3,2,1,0:T(8,128)(2,1)S(1)} collective-permute-done((bf16[2,3,192,128]{3,2,1,0:T(8,128)(2,1)S(1)}, bf16[2,3,192,128]{3,2,1,0:T(8,128)(2,1)S(1)}, u32[]{:S(2)}, u32[]{:S(2)}) %collective-permute-start.4) | collective-permute-done | bytes 294944 | tf_op jit(solution)/shard_map/ppermute | solution.py:44
  39.2 1.1 copy-done.14
  40.3 0.7 copy-done.16
  41.0 0.7 copy-done.17
  41.7 1.4 shard_map.73
  43.2 0.7 collective-permute-start.6
  43.9 1.3 collective-permute-start.8
  45.2 0.7 collective-permute-start.7
  45.9 8.1 %collective-permute-done.8.refs_3_.refs_1_ = bf16[2,3,192,128]{3,2,1,0:T(8,128)(2,1)S(1)} collective-permute-done((bf16[2,3,192,128]{3,2,1,0:T(8,128)(2,1)S(1)}, bf16[2,3,192,128]{3,2,1,0:T(8,128)(2,1)S(1)}, u32[]{:S(2)}, u32[]{:S(2)}) %collective-permute-start.8) | collective-permute-done | bytes 294944 | tf_op jit(solution)/shard_map/ppermute | solution.py:44
  54.0 1.3 collective-permute-start.9
  55.3 0.2 shard_map.75
  55.5 1.9 collective-permute-start.13
  57.4 3.9 %collective-permute-start.14 = (bf16[4,3,192,128]{3,2,1,0:T(8,128)(2,1)S(1)}, bf16[4,3,192,128]{3,2,1,0:T(8,128)(2,1)S(1)}, u32[]{:S(2)}, u32[]{:S(2)}) collective-permute-start(bf16[4,3,192,128]{3,2,1,0:T(8,128)(2,1)S(1)} %get-tuple-element.16), channel_id=1, source_target_pairs={{0,384},{1,385},{2,386},{3,387},{4,388},{5,389},{6,390},{7,391},{8... | collective-permute-start | bytes 1769480 | tf_op jit(solution)/shard_map/ppermute | solution.py:44
  61.3 5.2 %collective-permute-start.5 = (bf16[512,384]{1,0:T(8,128)(2,1)}, bf16[512,384]{1,0:T(8,128)(2,1)S(1)}, u32[]{:S(2)}, u32[]{:S(2)}) collective-permute-start(bf16[512,384]{1,0:T(8,128)(2,1)} %bitcast.4), channel_id=1, source_target_pairs={{0,64},{1,65},{2,66},{3,67},{4,68},{5,69},{6,70},{7,71},{8,72},{9,... | collective-permute-start | bytes 1179656 | tf_op jit(solution)/shard_map/ppermute | solution.py:44
  66.6 0.7 collective-permute-start.11
  67.3 1.3 collective-permute-start.12
  68.6 23.5 %collective-permute-done.5.refs_0_ = bf16[512,384]{1,0:T(8,128)(2,1)S(1)} collective-permute-done((bf16[512,384]{1,0:T(8,128)(2,1)}, bf16[512,384]{1,0:T(8,128)(2,1)S(1)}, u32[]{:S(2)}, u32[]{:S(2)}) %collective-permute-start.5) | collective-permute-done | bytes 393248 | tf_op jit(solution)/shard_map/ppermute | solution.py:44
  92.1 1.9 collective-permute-start.10
  94.1 3.5 %collective-permute-done.12.lower_ref = bf16[2,3,192,128]{3,2,1,0:T(8,128)(2,1)S(1)} collective-permute-done((bf16[2,3,192,128]{3,2,1,0:T(8,128)(2,1)S(1)}, bf16[2,3,192,128]{3,2,1,0:T(8,128)(2,1)S(1)}, u32[]{:S(2)}, u32[]{:S(2)}) %collective-permute-start.12) | collective-permute-done | bytes 294944 | tf_op jit(solution)/shard_map/ppermute | solution.py:44
  97.6 1.3 collective-permute-start.15
  98.9 13.4 %collective-permute-done.10.refs_0_ = bf16[512,384]{1,0:T(8,128)(2,1)S(1)} collective-permute-done((bf16[512,384]{1,0:T(8,128)(2,1)S(1)}, bf16[512,384]{1,0:T(8,128)(2,1)S(1)}, u32[]{:S(2)}, u32[]{:S(2)}) %collective-permute-start.10) | collective-permute-done | bytes 393248 | tf_op jit(solution)/shard_map/ppermute | solution.py:44
  112.3 5.4 %collective-permute-done.15.refs_1_ = bf16[2,3,192,128]{3,2,1,0:T(8,128)(2,1)S(1)} collective-permute-done((bf16[2,3,192,128]{3,2,1,0:T(8,128)(2,1)S(1)}, bf16[2,3,192,128]{3,2,1,0:T(8,128)(2,1)S(1)}, u32[]{:S(2)}, u32[]{:S(2)}) %collective-permute-start.15) | collective-permute-done | bytes 294944 | tf_op jit(solution)/shard_map/ppermute | solution.py:44
  117.8 0.8 shard_map.77
  118.6 0.7 copy-done.8
  119.4 1.3 collective-permute-start.18
  120.7 1.4 shard_map.79
  122.0 3.4 %collective-permute-start.16 = (bf16[5,3,192,128]{3,2,1,0:T(8,128)(2,1)}, bf16[5,3,192,128]{3,2,1,0:T(8,128)(2,1)}, u32[]{:S(2)}, u32[]{:S(2)}) collective-permute-start(bf16[5,3,192,128]{3,2,1,0:T(8,128)(2,1)} %get-tuple-element.17.refs_6_), channel_id=1, source_target_pairs={{0,128},{1,129},{2,130},{3,131},{4,132},{5,133},{6,134},{7,135},{8... | collective-permute-start | bytes 2211848 | tf_op jit(solution)/shard_map/ppermute | solution.py:44
  125.4 2.4 %collective-permute-start.17 = (bf16[5,3,192,128]{3,2,1,0:T(8,128)(2,1)}, bf16[5,3,192,128]{3,2,1,0:T(8,128)(2,1)}, u32[]{:S(2)}, u32[]{:S(2)}) collective-permute-start(bf16[5,3,192,128]{3,2,1,0:T(8,128)(2,1)} %get-tuple-element.18), channel_id=1, source_target_pairs={{0,384},{1,385},{2,386},{3,387},{4,388},{5,389},{6,390},{7,391},{8... | collective-permute-start | bytes 2211848 | tf_op jit(solution)/shard_map/ppermute | solution.py:44
  127.9 2.2 %collective-permute-done.18.refs_2_.refs_1_ = bf16[2,3,192,128]{3,2,1,0:T(8,128)(2,1)S(1)} collective-permute-done((bf16[2,3,192,128]{3,2,1,0:T(8,128)(2,1)}, bf16[2,3,192,128]{3,2,1,0:T(8,128)(2,1)S(1)}, u32[]{:S(2)}, u32[]{:S(2)}) %collective-permute-start.18) | collective-permute-done | bytes 294944 | tf_op jit(solution)/shard_map/ppermute | solution.py:44
  130.0 1.0 copy-done.9
  131.0 1.5 shard_map.80
  132.5 3.4 %collective-permute-start.19 = (bf16[6,3,192,128]{3,2,1,0:T(8,128)(2,1)}, bf16[6,3,192,128]{3,2,1,0:T(8,128)(2,1)S(1)}, u32[]{:S(2)}, u32[]{:S(2)}) collective-permute-start(bf16[6,3,192,128]{3,2,1,0:T(8,128)(2,1)} %get-tuple-element.19.refs_9_), channel_id=1, source_target_pairs={{0,128},{1,129},{2,130},{3,131},{4,132},{5,133},{6,134},{7,135},{8... | collective-permute-start | bytes 2654216 | tf_op jit(solution)/shard_map/ppermute | solution.py:44
  135.9 2.4 %collective-permute-start.20 = (bf16[6,3,192,128]{3,2,1,0:T(8,128)(2,1)}, bf16[6,3,192,128]{3,2,1,0:T(8,128)(2,1)S(1)}, u32[]{:S(2)}, u32[]{:S(2)}) collective-permute-start(bf16[6,3,192,128]{3,2,1,0:T(8,128)(2,1)} %get-tuple-element.20), channel_id=1, source_target_pairs={{0,384},{1,385},{2,386},{3,387},{4,388},{5,389},{6,390},{7,391},{8... | collective-permute-start | bytes 2654216 | tf_op jit(solution)/shard_map/ppermute | solution.py:44
  138.3 1.3 collective-permute-start.21
  139.6 0.7 dynamic-slice_bitcast_fusion
  140.3 0.1 broadcast_add_fusion
  140.4 0.1 add.86
  140.5 3.1 %collective-permute-done.16.refs_7_.refs_4_ = bf16[5,3,192,128]{3,2,1,0:T(8,128)(2,1)} collective-permute-done((bf16[5,3,192,128]{3,2,1,0:T(8,128)(2,1)}, bf16[5,3,192,128]{3,2,1,0:T(8,128)(2,1)}, u32[]{:S(2)}, u32[]{:S(2)}) %collective-permute-start.16) | collective-permute-done | bytes 737312 | tf_op jit(solution)/shard_map/ppermute | solution.py:44
  143.6 4.7 %collective-permute-done.17.refs_8_.refs_5_ = bf16[5,3,192,128]{3,2,1,0:T(8,128)(2,1)} collective-permute-done((bf16[5,3,192,128]{3,2,1,0:T(8,128)(2,1)}, bf16[5,3,192,128]{3,2,1,0:T(8,128)(2,1)}, u32[]{:S(2)}, u32[]{:S(2)}) %collective-permute-start.17) | collective-permute-done | bytes 737312 | tf_op jit(solution)/shard_map/ppermute | solution.py:44
  148.3 1.0 copy-done.7
  149.3 2.7 %shard_map.82 = (bf16[4,3,192,128]{3,2,1,0:T(8,128)(2,1)}, bf16[4,3,192,128]{3,2,1,0:T(8,128)(2,1)}) custom-call(s32[1]{0:T(128)} %bitcast.5.zl_ref, bf16[2,3,192,128]{3,2,1,0:T(8,128)(2,1)} %collective-permute-done.21.refs_0_, bf16[2,3,192,128]{3,2,1,0:T(8,128)(2,1)S(1)} %copy-done.7, ...), custom_call_target="tpu_custom_call" | custom-call | bytes 4194304 | tf_op jit(solution)/shard_map/pallas_call | solution.py:217
  151.9 4.0 %collective-permute-start.22 = (bf16[4,3,192,128]{3,2,1,0:T(8,128)(2,1)}, bf16[4,3,192,128]{3,2,1,0:T(8,128)(2,1)}, u32[]{:S(2)}, u32[]{:S(2)}) collective-permute-start(bf16[4,3,192,128]{3,2,1,0:T(8,128)(2,1)} %get-tuple-element.21.refs_0_), channel_id=1, source_target_pairs={{0,128},{1,129},{2,130},{3,131},{4,132},{5,133},{6,134},{7,135},{8... | collective-permute-start | bytes 1769480 | tf_op jit(solution)/shard_map/ppermute | solution.py:44
  155.9 1.9 collective-permute-start.23
  157.9 0.7 reshape.37
  158.7 1.9 copy-done
  160.6 1.9 copy-done.1
  162.5 6.4 %shard_map.78.normed_ref = bf16[32,512,192]{2,1,0:T(8,128)(2,1)S(1)} custom-call(bf16[8,512,384]{2,1,0:T(8,128)(2,1)S(1)} %copy-done, bf16[8,512,384]{2,1,0:T(8,128)(2,1)S(1)} %bitcast.13, f32[16,384]{1,0:T(8,128)S(1)} %fusion.gain_ref), custom_call_target="tpu_custom_call" | custom-call | flops 25165824 | bytes 14680064 | tf_op jit(solution)/shard_map/pallas_call | solution.py:102
  169.0 6.9 %shard_map.81.held_ref.refs_4_ = f32[3,512,256]{2,1,0:T(8,128)S(1)} custom-call(s32[32]{0:T(128)S(1)} %fusion.1.index_ref, bf16[32,512,192]{2,1,0:T(8,128)(2,1)S(1)} %shard_map.78.normed_ref, bf16[2,3,192,128]{3,2,1,0:T(8,128)(2,1)S(1)} %copy-done.11, bf16[2,3,192,128]{3,2,1,0:T(8,128)(2,1)S(1)} %copy-done.3, bf16[2,3,192,128]{3,2,1,0:T(8,128)(2,1)S(1)} %copy-done.5, ...), custom_call_target="tpu_custom_call" | custom-call | flops 3623878656 | bytes 15466496 | tf_op jit(solution)/shard_map/pallas_call | solution.py:176
  175.9 2.4 %collective-permute-done.23.refs_2_.refs_3_ = bf16[4,3,192,128]{3,2,1,0:T(8,128)(2,1)} collective-permute-done((bf16[4,3,192,128]{3,2,1,0:T(8,128)(2,1)}, bf16[4,3,192,128]{3,2,1,0:T(8,128)(2,1)}, u32[]{:S(2)}, u32[]{:S(2)}) %collective-permute-start.23) | collective-permute-done | bytes 589856 | tf_op jit(solution)/shard_map/ppermute | solution.py:44
  178.2 1.3 shard_map.84
  179.5 2.8 %collective-permute-start.24 = (bf16[3,3,192,128]{3,2,1,0:T(8,128)(2,1)S(1)}, bf16[3,3,192,128]{3,2,1,0:T(8,128)(2,1)S(1)}, u32[]{:S(2)}, u32[]{:S(2)}) collective-permute-start(bf16[3,3,192,128]{3,2,1,0:T(8,128)(2,1)S(1)} %get-tuple-element.23), channel_id=1, source_target_pairs={{0,128},{1,129},{2,130},{3,131},{4,132},{5,133},{6,134},{7,135},{8... | collective-permute-start | bytes 1327112 | tf_op jit(solution)/shard_map/ppermute | solution.py:44
  182.4 3.2 %collective-permute-start.25 = (bf16[3,3,192,128]{3,2,1,0:T(8,128)(2,1)S(1)}, bf16[3,3,192,128]{3,2,1,0:T(8,128)(2,1)S(1)}, u32[]{:S(2)}, u32[]{:S(2)}) collective-permute-start(bf16[3,3,192,128]{3,2,1,0:T(8,128)(2,1)S(1)} %get-tuple-element.24), channel_id=1, source_target_pairs={{0,384},{1,385},{2,386},{3,387},{4,388},{5,389},{6,390},{7,391},{8... | collective-permute-start | bytes 1327112 | tf_op jit(solution)/shard_map/ppermute | solution.py:44
  185.6 2.6 %shard_map.83.held_ref = f32[3,512,256]{2,1,0:T(8,128)S(1)} custom-call(s32[32]{0:T(128)S(1)} %fusion.1.index_ref, bf16[32,512,192]{2,1,0:T(8,128)(2,1)S(1)} %shard_map.78.normed_ref, f32[3,512,256]{2,1,0:T(8,128)S(1)} %shard_map.81.held_ref.refs_4_, bf16[4,3,192,128]{3,2,1,0:T(8,128)(2,1)} %get-tuple-element.21.refs_0_, ...), custom_call_target="tpu_custom_call" | custom-call | flops 754974720 | bytes 9863168 | tf_op jit(solution)/shard_map/pallas_call | solution.py:176
  188.2 3.8 %collective-permute-done.24.refs_0_ = bf16[3,3,192,128]{3,2,1,0:T(8,128)(2,1)S(1)} collective-permute-done((bf16[3,3,192,128]{3,2,1,0:T(8,128)(2,1)S(1)}, bf16[3,3,192,128]{3,2,1,0:T(8,128)(2,1)S(1)}, u32[]{:S(2)}, u32[]{:S(2)}) %collective-permute-start.24) | collective-permute-done | bytes 442400 | tf_op jit(solution)/shard_map/ppermute | solution.py:44
  192.0 3.2 %collective-permute-done.25.refs_1_ = bf16[3,3,192,128]{3,2,1,0:T(8,128)(2,1)S(1)} collective-permute-done((bf16[3,3,192,128]{3,2,1,0:T(8,128)(2,1)S(1)}, bf16[3,3,192,128]{3,2,1,0:T(8,128)(2,1)S(1)}, u32[]{:S(2)}, u32[]{:S(2)}) %collective-permute-start.25) | collective-permute-done | bytes 442400 | tf_op jit(solution)/shard_map/ppermute | solution.py:44
  195.1 3.6 %shard_map.85 = bf16[512,256]{1,0:T(8,128)(2,1)} custom-call(s32[32]{0:T(128)S(1)} %fusion.1.index_ref, bf16[32,512,192]{2,1,0:T(8,128)(2,1)S(1)} %shard_map.78.normed_ref, f32[3,512,256]{2,1,0:T(8,128)S(1)} %shard_map.83.held_ref, f32[2,256]{1,0:T(2,128)S(1)} %copy-done.15, bf16[3,3,192,128]{3,2,1,0:T(8,128)(2,1)S(1)} %collective-permute-done.24.refs_0_, ...), custom_call_target="tpu_custom_call" | custom-call | flops 452984832 | bytes 9273344 | tf_op jit(solution)/shard_map/pallas_call | solution.py:176
  (52 shorter events, 0.3 us)
Async XLA Ops:
  6.5 152.1 %all-gather.4.cloned.1.call-start = ((), (), s32[]{:S(2)}) async-start(), calls=%async_computation | async-start | bytes 3538944 | tf_op jit(solution)/shard_map/all_gather | solution.py:302
  6.5 32.7 %collective-permute-start = (bf16[2,256,384]{2,1,0:T(8,128)(2,1)}, bf16[2,256,384]{2,1,0:T(8,128)(2,1)S(1)}, u32[]{:S(2)}, u32[]{:S(2)}) collective-permute-start(bf16[2,256,384]{2,1,0:T(8,128)(2,1)} %tokens_ref.1), channel_id=1, source_target_pairs={{0,496},{1,497},{2,498},{3,499},{4,500},{5,501},{6,502},{7,503},{8... | collective-permute-start | bytes 1179656 | tf_op jit(solution)/shard_map/ppermute | solution.py:44
  21.0 13.8 %collective-permute-start.1 = (bf16[2,3,192,128]{3,2,1,0:T(8,128)(2,1)S(1)}, bf16[2,3,192,128]{3,2,1,0:T(8,128)(2,1)S(1)}, u32[]{:S(2)}, u32[]{:S(2)}) collective-permute-start(bf16[2,3,192,128]{3,2,1,0:T(8,128)(2,1)S(1)} %pad_maximum_fusion.refs_0_), channel_id=1, source_target_pairs={{0,16},{1,17},{2,18},{3,19},{4,20},{5,21},{6,22},{7,23},{8,24},{9,... | collective-permute-start | bytes 884744 | tf_op jit(solution)/shard_map/ppermute | solution.py:44
  22.3 12.5 %collective-permute-start.2 = (bf16[2,3,192,128]{3,2,1,0:T(8,128)(2,1)S(1)}, bf16[2,3,192,128]{3,2,1,0:T(8,128)(2,1)S(1)}, u32[]{:S(2)}, u32[]{:S(2)}) collective-permute-start(bf16[2,3,192,128]{3,2,1,0:T(8,128)(2,1)S(1)} %pad_maximum_fusion.refs_0_), channel_id=1, source_target_pairs={{16,0},{17,1},{18,2},{19,3},{20,4},{21,5},{22,6},{23,7},{24,8},{25... | collective-permute-start | bytes 884744 | tf_op jit(solution)/shard_map/ppermute | solution.py:44
  23.6 11.2 %collective-permute-start.3 = (bf16[2,3,192,128]{3,2,1,0:T(8,128)(2,1)S(1)}, bf16[2,3,192,128]{3,2,1,0:T(8,128)(2,1)S(1)}, u32[]{:S(2)}, u32[]{:S(2)}) collective-permute-start(bf16[2,3,192,128]{3,2,1,0:T(8,128)(2,1)S(1)} %pad_maximum_fusion.refs_0_), channel_id=1, source_target_pairs={{0,128},{1,129},{2,130},{3,131},{4,132},{5,133},{6,134},{7,135},{8... | collective-permute-start | bytes 884744 | tf_op jit(solution)/shard_map/ppermute | solution.py:44
  27.9 11.3 %collective-permute-start.4 = (bf16[2,3,192,128]{3,2,1,0:T(8,128)(2,1)S(1)}, bf16[2,3,192,128]{3,2,1,0:T(8,128)(2,1)S(1)}, u32[]{:S(2)}, u32[]{:S(2)}) collective-permute-start(bf16[2,3,192,128]{3,2,1,0:T(8,128)(2,1)S(1)} %pad_maximum_fusion.refs_0_), channel_id=1, source_target_pairs={{0,384},{1,385},{2,386},{3,387},{4,388},{5,389},{6,390},{7,391},{8... | collective-permute-start | bytes 884744 | tf_op jit(solution)/shard_map/ppermute | solution.py:44
  29.9 0.7 copy-start.10
  34.8 85.8 %copy-start.2 = (bf16[2,3,192,128]{3,2,1,0:T(8,128)(2,1)}, bf16[2,3,192,128]{3,2,1,0:T(8,128)(2,1)S(1)}, u32[]{:S(2)}) copy-start(bf16[2,3,192,128]{3,2,1,0:T(8,128)(2,1)S(1)} %collective-permute-done.3.refs_2_.refs_5_.refs_1_) | copy-start | bytes 884740
  39.2 81.4 %copy-start.4 = (bf16[2,3,192,128]{3,2,1,0:T(8,128)(2,1)}, bf16[2,3,192,128]{3,2,1,0:T(8,128)(2,1)S(1)}, u32[]{:S(2)}) copy-start(bf16[2,3,192,128]{3,2,1,0:T(8,128)(2,1)S(1)} %collective-permute-done.4.refs_3_.refs_6_.refs_2_) | copy-start | bytes 884740
  39.2 1.1 copy-start.14
  40.3 0.7 copy-start.16
  41.0 0.7 copy-start.17
  43.1 115.6 %all-gather.6.cloned.1.call-start = ((), (), s32[]{:S(2)}) async-start(), calls=%async_computation.1 | async-start | bytes 3538944 | tf_op jit(solution)/shard_map/all_gather | solution.py:341
  43.2 2.0 collective-permute-start.6
  43.9 10.1 %collective-permute-start.8 = (bf16[2,3,192,128]{3,2,1,0:T(8,128)(2,1)S(1)}, bf16[2,3,192,128]{3,2,1,0:T(8,128)(2,1)S(1)}, u32[]{:S(2)}, u32[]{:S(2)}) collective-permute-start(bf16[2,3,192,128]{3,2,1,0:T(8,128)(2,1)S(1)} %collective-permute-done.2.refs_1_), channel_id=1, source_target_pairs={{16,0},{17,1},{18,2},{19,3},{20,4},{21,5},{22,6},{23,7},{24,8},{25... | collective-permute-start | bytes 884744 | tf_op jit(solution)/shard_map/ppermute | solution.py:44
  45.2 21.4 %collective-permute-start.7 = (bf16[2,3,192,128]{3,2,1,0:T(8,128)(2,1)S(1)}, bf16[2,3,192,128]{3,2,1,0:T(8,128)(2,1)S(1)}, u32[]{:S(2)}, u32[]{:S(2)}) collective-permute-start(bf16[2,3,192,128]{3,2,1,0:T(8,128)(2,1)S(1)} %collective-permute-done.6.refs_2_.refs_0_), channel_id=1, source_target_pairs={{32,48},{33,49},{34,50},{35,51},{36,52},{37,53},{38,54},{39,55},{4... | collective-permute-start | bytes 884744 | tf_op jit(solution)/shard_map/ppermute | solution.py:44
  54.0 13.3 %collective-permute-start.9 = (bf16[2,3,192,128]{3,2,1,0:T(8,128)(2,1)S(1)}, bf16[2,3,192,128]{3,2,1,0:T(8,128)(2,1)S(1)}, u32[]{:S(2)}, u32[]{:S(2)}) collective-permute-start(bf16[2,3,192,128]{3,2,1,0:T(8,128)(2,1)S(1)} %collective-permute-done.8.refs_3_.refs_1_), channel_id=1, source_target_pairs={{16,0},{17,1},{18,2},{19,3},{20,4},{21,5},{22,6},{23,7},{24,8},{25... | collective-permute-start | bytes 884744 | tf_op jit(solution)/shard_map/ppermute | solution.py:44
  55.5 62.3 %copy-start.12 = (bf16[4,3,192,128]{3,2,1,0:T(8,128)(2,1)}, bf16[4,3,192,128]{3,2,1,0:T(8,128)(2,1)S(1)}, u32[]{:S(2)}) copy-start(bf16[4,3,192,128]{3,2,1,0:T(8,128)(2,1)S(1)} %get-tuple-element.15.refs_3_) | copy-start | bytes 1769476
  55.5 42.1 %collective-permute-start.13 = (bf16[4,3,192,128]{3,2,1,0:T(8,128)(2,1)S(1)}, bf16[4,3,192,128]{3,2,1,0:T(8,128)(2,1)S(1)}, u32[]{:S(2)}, u32[]{:S(2)}) collective-permute-start(bf16[4,3,192,128]{3,2,1,0:T(8,128)(2,1)S(1)} %get-tuple-element.15.refs_3_), channel_id=1, source_target_pairs={{0,128},{1,129},{2,130},{3,131},{4,132},{5,133},{6,134},{7,135},{8... | collective-permute-start | bytes 1769480 | tf_op jit(solution)/shard_map/ppermute | solution.py:44
  57.4 40.2 %collective-permute-start.14 = (bf16[4,3,192,128]{3,2,1,0:T(8,128)(2,1)S(1)}, bf16[4,3,192,128]{3,2,1,0:T(8,128)(2,1)S(1)}, u32[]{:S(2)}, u32[]{:S(2)}) collective-permute-start(bf16[4,3,192,128]{3,2,1,0:T(8,128)(2,1)S(1)} %get-tuple-element.16), channel_id=1, source_target_pairs={{0,384},{1,385},{2,386},{3,387},{4,388},{5,389},{6,390},{7,391},{8... | collective-permute-start | bytes 1769480 | tf_op jit(solution)/shard_map/ppermute | solution.py:44
  61.3 30.7 %collective-permute-start.5 = (bf16[512,384]{1,0:T(8,128)(2,1)}, bf16[512,384]{1,0:T(8,128)(2,1)S(1)}, u32[]{:S(2)}, u32[]{:S(2)}) collective-permute-start(bf16[512,384]{1,0:T(8,128)(2,1)} %bitcast.4), channel_id=1, source_target_pairs={{0,64},{1,65},{2,66},{3,67},{4,68},{5,69},{6,70},{7,71},{8,72},{9,... | collective-permute-start | bytes 1179656 | tf_op jit(solution)/shard_map/ppermute | solution.py:44
  66.6 27.5 %collective-permute-start.11 = (bf16[2,3,192,128]{3,2,1,0:T(8,128)(2,1)S(1)}, bf16[2,3,192,128]{3,2,1,0:T(8,128)(2,1)S(1)}, u32[]{:S(2)}, u32[]{:S(2)}) collective-permute-start(bf16[2,3,192,128]{3,2,1,0:T(8,128)(2,1)S(1)} %collective-permute-done.7.refs_1_.refs_2_.refs_3_), channel_id=1, source_target_pairs={{48,64},{49,65},{50,66},{51,67},{52,68},{53,69},{54,70},{55,71},{5... | collective-permute-start | bytes 884744 | tf_op jit(solution)/shard_map/ppermute | solution.py:44
  67.3 30.3 %collective-permute-start.12 = (bf16[2,3,192,128]{3,2,1,0:T(8,128)(2,1)S(1)}, bf16[2,3,192,128]{3,2,1,0:T(8,128)(2,1)S(1)}, u32[]{:S(2)}, u32[]{:S(2)}) collective-permute-start(bf16[2,3,192,128]{3,2,1,0:T(8,128)(2,1)S(1)} %collective-permute-done.9.refs_2_.refs_3_.refs_4_), channel_id=1, source_target_pairs={{16,0},{17,1},{18,2},{19,3},{20,4},{21,5},{22,6},{23,7},{24,8},{25... | collective-permute-start | bytes 884744 | tf_op jit(solution)/shard_map/ppermute | solution.py:44
  92.1 20.2 %collective-permute-start.10 = (bf16[512,384]{1,0:T(8,128)(2,1)S(1)}, bf16[512,384]{1,0:T(8,128)(2,1)S(1)}, u32[]{:S(2)}, u32[]{:S(2)}) collective-permute-start(bf16[512,384]{1,0:T(8,128)(2,1)S(1)} %shard_map.74), channel_id=1, source_target_pairs={{0,64},{1,65},{2,66},{3,67},{4,68},{5,69},{6,70},{7,71},{8,72},{9,... | collective-permute-start | bytes 1179656 | tf_op jit(solution)/shard_map/ppermute | solution.py:44
  97.6 20.2 %collective-permute-start.15 = (bf16[2,3,192,128]{3,2,1,0:T(8,128)(2,1)S(1)}, bf16[2,3,192,128]{3,2,1,0:T(8,128)(2,1)S(1)}, u32[]{:S(2)}, u32[]{:S(2)}) collective-permute-start(bf16[2,3,192,128]{3,2,1,0:T(8,128)(2,1)S(1)} %shard_map.76.refs_4_.refs_0_), channel_id=1, source_target_pairs={{16,0},{17,1},{18,2},{19,3},{20,4},{21,5},{22,6},{23,7},{24,8},{25... | collective-permute-start | bytes 884744 | tf_op jit(solution)/shard_map/ppermute | solution.py:44
  118.6 0.7 copy-start.8
  119.4 10.7 %collective-permute-start.18 = (bf16[2,3,192,128]{3,2,1,0:T(8,128)(2,1)}, bf16[2,3,192,128]{3,2,1,0:T(8,128)(2,1)S(1)}, u32[]{:S(2)}, u32[]{:S(2)}) collective-permute-start(bf16[2,3,192,128]{3,2,1,0:T(8,128)(2,1)} %copy-done.8), channel_id=1, source_target_pairs={{16,0},{17,1},{18,2},{19,3},{20,4},{21,5},{22,6},{23,7},{24,8},{25... | collective-permute-start | bytes 884744 | tf_op jit(solution)/shard_map/ppermute | solution.py:44
  122.0 21.6 %collective-permute-start.16 = (bf16[5,3,192,128]{3,2,1,0:T(8,128)(2,1)}, bf16[5,3,192,128]{3,2,1,0:T(8,128)(2,1)}, u32[]{:S(2)}, u32[]{:S(2)}) collective-permute-start(bf16[5,3,192,128]{3,2,1,0:T(8,128)(2,1)} %get-tuple-element.17.refs_6_), channel_id=1, source_target_pairs={{0,128},{1,129},{2,130},{3,131},{4,132},{5,133},{6,134},{7,135},{8... | collective-permute-start | bytes 2211848 | tf_op jit(solution)/shard_map/ppermute | solution.py:44
  125.4 22.8 %collective-permute-start.17 = (bf16[5,3,192,128]{3,2,1,0:T(8,128)(2,1)}, bf16[5,3,192,128]{3,2,1,0:T(8,128)(2,1)}, u32[]{:S(2)}, u32[]{:S(2)}) collective-permute-start(bf16[5,3,192,128]{3,2,1,0:T(8,128)(2,1)} %get-tuple-element.18), channel_id=1, source_target_pairs={{0,384},{1,385},{2,386},{3,387},{4,388},{5,389},{6,390},{7,391},{8... | collective-permute-start | bytes 2211848 | tf_op jit(solution)/shard_map/ppermute | solution.py:44
  130.0 1.0 copy-start.9
  131.0 4.9 %copy-start.6 = (bf16[2,3,192,128]{3,2,1,0:T(8,128)(2,1)}, bf16[2,3,192,128]{3,2,1,0:T(8,128)(2,1)S(1)}, u32[]{:S(2)}) copy-start(bf16[2,3,192,128]{3,2,1,0:T(8,128)(2,1)S(1)} %collective-permute-done.18.refs_2_.refs_1_) | copy-start | bytes 884740
  132.5 36.5 %collective-permute-start.19 = (bf16[6,3,192,128]{3,2,1,0:T(8,128)(2,1)}, bf16[6,3,192,128]{3,2,1,0:T(8,128)(2,1)S(1)}, u32[]{:S(2)}, u32[]{:S(2)}) collective-permute-start(bf16[6,3,192,128]{3,2,1,0:T(8,128)(2,1)} %get-tuple-element.19.refs_9_), channel_id=1, source_target_pairs={{0,128},{1,129},{2,130},{3,131},{4,132},{5,133},{6,134},{7,135},{8... | collective-permute-start | bytes 2654216 | tf_op jit(solution)/shard_map/ppermute | solution.py:44
  135.9 33.0 %collective-permute-start.20 = (bf16[6,3,192,128]{3,2,1,0:T(8,128)(2,1)}, bf16[6,3,192,128]{3,2,1,0:T(8,128)(2,1)S(1)}, u32[]{:S(2)}, u32[]{:S(2)}) collective-permute-start(bf16[6,3,192,128]{3,2,1,0:T(8,128)(2,1)} %get-tuple-element.20), channel_id=1, source_target_pairs={{0,384},{1,385},{2,386},{3,387},{4,388},{5,389},{6,390},{7,391},{8... | collective-permute-start | bytes 2654216 | tf_op jit(solution)/shard_map/ppermute | solution.py:44
  138.3 9.9 %collective-permute-start.21 = (bf16[2,3,192,128]{3,2,1,0:T(8,128)(2,1)}, bf16[2,3,192,128]{3,2,1,0:T(8,128)(2,1)}, u32[]{:S(2)}, u32[]{:S(2)}) collective-permute-start(bf16[2,3,192,128]{3,2,1,0:T(8,128)(2,1)} %copy-done.6), channel_id=1, source_target_pairs={{16,0},{17,1},{18,2},{19,3},{20,4},{21,5},{22,6},{23,7},{24,8},{25... | collective-permute-start | bytes 884744 | tf_op jit(solution)/shard_map/ppermute | solution.py:44
  148.3 1.0 copy-start.7
  151.9 23.9 %collective-permute-start.22 = (bf16[4,3,192,128]{3,2,1,0:T(8,128)(2,1)}, bf16[4,3,192,128]{3,2,1,0:T(8,128)(2,1)}, u32[]{:S(2)}, u32[]{:S(2)}) collective-permute-start(bf16[4,3,192,128]{3,2,1,0:T(8,128)(2,1)} %get-tuple-element.21.refs_0_), channel_id=1, source_target_pairs={{0,128},{1,129},{2,130},{3,131},{4,132},{5,133},{6,134},{7,135},{8... | collective-permute-start | bytes 1769480 | tf_op jit(solution)/shard_map/ppermute | solution.py:44
  155.9 22.3 %collective-permute-start.23 = (bf16[4,3,192,128]{3,2,1,0:T(8,128)(2,1)}, bf16[4,3,192,128]{3,2,1,0:T(8,128)(2,1)}, u32[]{:S(2)}, u32[]{:S(2)}) collective-permute-start(bf16[4,3,192,128]{3,2,1,0:T(8,128)(2,1)} %get-tuple-element.22), channel_id=1, source_target_pairs={{0,384},{1,385},{2,386},{3,387},{4,388},{5,389},{6,390},{7,391},{8... | collective-permute-start | bytes 1769480 | tf_op jit(solution)/shard_map/ppermute | solution.py:44
  158.7 1.9 copy-start
  160.6 1.9 copy-start.1
  162.5 6.5 %copy-start.3 = (bf16[2,3,192,128]{3,2,1,0:T(8,128)(2,1)S(1)}, bf16[2,3,192,128]{3,2,1,0:T(8,128)(2,1)}, u32[]{:S(2)}) copy-start(bf16[2,3,192,128]{3,2,1,0:T(8,128)(2,1)} %copy-done.2) | copy-start | bytes 884740
  162.5 6.5 %copy-start.5 = (bf16[2,3,192,128]{3,2,1,0:T(8,128)(2,1)S(1)}, bf16[2,3,192,128]{3,2,1,0:T(8,128)(2,1)}, u32[]{:S(2)}) copy-start(bf16[2,3,192,128]{3,2,1,0:T(8,128)(2,1)} %copy-done.4) | copy-start | bytes 884740
  162.5 6.5 %copy-start.11 = (bf16[2,3,192,128]{3,2,1,0:T(8,128)(2,1)S(1)}, bf16[2,3,192,128]{3,2,1,0:T(8,128)(2,1)}, u32[]{:S(2)}) copy-start(bf16[2,3,192,128]{3,2,1,0:T(8,128)(2,1)} %copy-done.10) | copy-start | bytes 884740
  162.5 6.5 %copy-start.13 = (bf16[4,3,192,128]{3,2,1,0:T(8,128)(2,1)S(1)}, bf16[4,3,192,128]{3,2,1,0:T(8,128)(2,1)}, u32[]{:S(2)}) copy-start(bf16[4,3,192,128]{3,2,1,0:T(8,128)(2,1)} %copy-done.12) | copy-start | bytes 1769476
  179.5 12.4 %collective-permute-start.24 = (bf16[3,3,192,128]{3,2,1,0:T(8,128)(2,1)S(1)}, bf16[3,3,192,128]{3,2,1,0:T(8,128)(2,1)S(1)}, u32[]{:S(2)}, u32[]{:S(2)}) collective-permute-start(bf16[3,3,192,128]{3,2,1,0:T(8,128)(2,1)S(1)} %get-tuple-element.23), channel_id=1, source_target_pairs={{0,128},{1,129},{2,130},{3,131},{4,132},{5,133},{6,134},{7,135},{8... | collective-permute-start | bytes 1327112 | tf_op jit(solution)/shard_map/ppermute | solution.py:44
  182.3 12.8 %copy-start.15 = (f32[2,256]{1,0:T(2,128)S(1)}, f32[2,256]{1,0:T(2,128)}, u32[]{:S(2)}) copy-start(f32[2,256]{1,0:T(2,128)} %gain_ref.1) | copy-start | bytes 6148
  182.4 12.8 %collective-permute-start.25 = (bf16[3,3,192,128]{3,2,1,0:T(8,128)(2,1)S(1)}, bf16[3,3,192,128]{3,2,1,0:T(8,128)(2,1)S(1)}, u32[]{:S(2)}, u32[]{:S(2)}) collective-permute-start(bf16[3,3,192,128]{3,2,1,0:T(8,128)(2,1)S(1)} %get-tuple-element.24), channel_id=1, source_target_pairs={{0,384},{1,385},{2,386},{3,387},{4,388},{5,389},{6,390},{7,391},{8... | collective-permute-start | bytes 1327112 | tf_op jit(solution)/shard_map/ppermute | solution.py:44
Sparse Core Ops, SparseCore 0:
  43.2 32.9 all-gather.3
  119.5 33.2 all-gather.5

commit v6 on v5

--- a/solution.py
+++ b/solution.py
@@ -337,7 +337,7 @@
         [(0, 1)],
     )
     m5 = along_line(m4, up=range(4, 7), down=range(1, 4))
-    (other,) = held_back([other], [m5])
+    (other,) = held_back([other], [m5, sent[2]])
     other_features = lax.all_gather(other, ("y", "c"))
     m6 = along_line(m5, up=range(5, 7), down=range(1, 3))
     send(

time: 207 us -> 205 us (level)
  waiting for transfers between devices: 82 us -> 79.5 us
    ppermute x26, waiting for transfers between devices: 81.9 us -> 79.4 us  [move(): return lax.ppermute(value, AXES, pairs)]
  transfers between devices with their start and end apart: 28 -> 28, of which waited for: 13 -> 14; matrix products, arithmetic and copies ran while one was open for 1% -> 1% of each run, Pallas kernels for 11% -> 11%
where the time goes in v6:
time: 205 us; the launch traced here: 204 us
  waiting for transfers between devices  79.5 us (39%)
  starting transfers between devices  70.1 us (34%)
  Pallas kernels  28.4 us (14%)
  between operations  13.9 us (7%)
  local copies, waits for them, and re-layouts  12.3 us (6%)
    ppermute x26, waiting for transfers between devices, move(): return lax.ppermute(value, AXES, pairs)  79.4 us
    ppermute x26, starting transfers between devices, move(): return lax.ppermute(value, AXES, pairs)  70.1 us
    pallas_call x3, Pallas kernels, project(): pl.pallas_call(functools.partial(kernel, blocks), out_shape=out_shape, in...  13.1 us
    unnamed x36, local copies, waits for them, and re-layouts  9.75 us
    pallas_call x5, Pallas kernels, relay(): pl.pallas_call(functools.partial(relay_kernel, slots, forward, len(arrays...  6.57 us
    pallas_call x1, Pallas kernels, norm_tokens(): pl.pallas_call(norm_kernel, out_shape=jax.ShapeDtypeStruct((32, 512, 192)...  6.42 us
  transfers between devices with their start and end apart: 28, of which 14 were waited for; matrix products, arithmetic and copies ran while one was open for 1% of the time, Pallas kernels for 11%

profile of v6, /device:TPU:6, one launch (start us, length us, event | category | flops | bytes accessed | tf_op | source)
XLA Modules:
  0.0 204.3 jit_solution(15149019423280689459)
XLA Ops:
  6.5 13.4 %collective-permute-start = (bf16[2,256,384]{2,1,0:T(8,128)(2,1)}, bf16[2,256,384]{2,1,0:T(8,128)(2,1)S(1)}, u32[]{:S(2)}, u32[]{:S(2)}) collective-permute-start(bf16[2,256,384]{2,1,0:T(8,128)(2,1)} %tokens_ref.1), channel_id=1, source_target_pairs={{0,496},{1,497},{2,498},{3,499},{4,500},{5,501},{6,502},{7,503},{8... | collective-permute-start | bytes 1179656 | tf_op jit(solution)/shard_map/ppermute | solution.py:44
  20.0 1.0 slice_bitcast_fusion.1
  21.0 1.3 collective-permute-start.1
  22.3 1.3 collective-permute-start.2
  23.6 4.3 %collective-permute-start.3 = (bf16[2,3,192,128]{3,2,1,0:T(8,128)(2,1)S(1)}, bf16[2,3,192,128]{3,2,1,0:T(8,128)(2,1)S(1)}, u32[]{:S(2)}, u32[]{:S(2)}) collective-permute-start(bf16[2,3,192,128]{3,2,1,0:T(8,128)(2,1)S(1)} %pad_maximum_fusion.refs_0_), channel_id=1, source_target_pairs={{0,128},{1,129},{2,130},{3,131},{4,132},{5,133},{6,134},{7,135},{8... | collective-permute-start | bytes 884744 | tf_op jit(solution)/shard_map/ppermute | solution.py:44
  28.0 1.9 collective-permute-start.4
  29.9 5.0 %collective-permute-done.1.refs_0_ = bf16[2,3,192,128]{3,2,1,0:T(8,128)(2,1)S(1)} collective-permute-done((bf16[2,3,192,128]{3,2,1,0:T(8,128)(2,1)S(1)}, bf16[2,3,192,128]{3,2,1,0:T(8,128)(2,1)S(1)}, u32[]{:S(2)}, u32[]{:S(2)}) %collective-permute-start.1) | collective-permute-done | bytes 294944 | tf_op jit(solution)/shard_map/ppermute | solution.py:44
  34.8 4.4 %collective-permute-done.4.refs_3_.refs_6_.refs_2_ = bf16[2,3,192,128]{3,2,1,0:T(8,128)(2,1)S(1)} collective-permute-done((bf16[2,3,192,128]{3,2,1,0:T(8,128)(2,1)S(1)}, bf16[2,3,192,128]{3,2,1,0:T(8,128)(2,1)S(1)}, u32[]{:S(2)}, u32[]{:S(2)}) %collective-permute-start.4) | collective-permute-done | bytes 294944 | tf_op jit(solution)/shard_map/ppermute | solution.py:44
  39.3 1.1 copy-done.13
  40.4 0.7 copy-done.15
  41.0 0.7 copy-done.16
  41.7 1.5 shard_map.73
  43.2 0.7 collective-permute-start.6
  43.9 1.3 collective-permute-start.8
  45.2 0.7 collective-permute-start.7
  45.9 8.1 %collective-permute-done.8.refs_3_.refs_1_ = bf16[2,3,192,128]{3,2,1,0:T(8,128)(2,1)S(1)} collective-permute-done((bf16[2,3,192,128]{3,2,1,0:T(8,128)(2,1)S(1)}, bf16[2,3,192,128]{3,2,1,0:T(8,128)(2,1)S(1)}, u32[]{:S(2)}, u32[]{:S(2)}) %collective-permute-start.8) | collective-permute-done | bytes 294944 | tf_op jit(solution)/shard_map/ppermute | solution.py:44
  54.0 1.3 collective-permute-start.9
  55.3 0.2 shard_map.75
  55.5 1.9 collective-permute-start.13
  57.4 3.9 %collective-permute-start.14 = (bf16[4,3,192,128]{3,2,1,0:T(8,128)(2,1)S(1)}, bf16[4,3,192,128]{3,2,1,0:T(8,128)(2,1)S(1)}, u32[]{:S(2)}, u32[]{:S(2)}) collective-permute-start(bf16[4,3,192,128]{3,2,1,0:T(8,128)(2,1)S(1)} %get-tuple-element.16), channel_id=1, source_target_pairs={{0,384},{1,385},{2,386},{3,387},{4,388},{5,389},{6,390},{7,391},{8... | collective-permute-start | bytes 1769480 | tf_op jit(solution)/shard_map/ppermute | solution.py:44
  61.4 5.3 %collective-permute-start.5 = (bf16[512,384]{1,0:T(8,128)(2,1)}, bf16[512,384]{1,0:T(8,128)(2,1)S(1)}, u32[]{:S(2)}, u32[]{:S(2)}) collective-permute-start(bf16[512,384]{1,0:T(8,128)(2,1)} %bitcast.4), channel_id=1, source_target_pairs={{0,64},{1,65},{2,66},{3,67},{4,68},{5,69},{6,70},{7,71},{8,72},{9,... | collective-permute-start | bytes 1179656 | tf_op jit(solution)/shard_map/ppermute | solution.py:44
  66.6 0.7 collective-permute-start.11
  67.3 1.3 collective-permute-start.12
  68.6 23.5 %collective-permute-done.5.refs_0_ = bf16[512,384]{1,0:T(8,128)(2,1)S(1)} collective-permute-done((bf16[512,384]{1,0:T(8,128)(2,1)}, bf16[512,384]{1,0:T(8,128)(2,1)S(1)}, u32[]{:S(2)}, u32[]{:S(2)}) %collective-permute-start.5) | collective-permute-done | bytes 393248 | tf_op jit(solution)/shard_map/ppermute | solution.py:44
  92.1 1.9 collective-permute-start.10
  94.1 3.5 %collective-permute-done.12.lower_ref = bf16[2,3,192,128]{3,2,1,0:T(8,128)(2,1)S(1)} collective-permute-done((bf16[2,3,192,128]{3,2,1,0:T(8,128)(2,1)S(1)}, bf16[2,3,192,128]{3,2,1,0:T(8,128)(2,1)S(1)}, u32[]{:S(2)}, u32[]{:S(2)}) %collective-permute-start.12) | collective-permute-done | bytes 294944 | tf_op jit(solution)/shard_map/ppermute | solution.py:44
  97.6 1.3 collective-permute-start.15
  99.0 1.1 shard_map.77
  100.0 0.9 copy-done.17
  100.9 11.4 %collective-permute-done.10.refs_0_ = bf16[512,384]{1,0:T(8,128)(2,1)S(1)} collective-permute-done((bf16[512,384]{1,0:T(8,128)(2,1)S(1)}, bf16[512,384]{1,0:T(8,128)(2,1)S(1)}, u32[]{:S(2)}, u32[]{:S(2)}) %collective-permute-start.10) | collective-permute-done | bytes 393248 | tf_op jit(solution)/shard_map/ppermute | solution.py:44
  112.4 5.5 %collective-permute-done.15.refs_1_ = bf16[2,3,192,128]{3,2,1,0:T(8,128)(2,1)S(1)} collective-permute-done((bf16[2,3,192,128]{3,2,1,0:T(8,128)(2,1)S(1)}, bf16[2,3,192,128]{3,2,1,0:T(8,128)(2,1)S(1)}, u32[]{:S(2)}, u32[]{:S(2)}) %collective-permute-start.15) | collective-permute-done | bytes 294944 | tf_op jit(solution)/shard_map/ppermute | solution.py:44
  117.8 0.8 shard_map.78
  118.6 1.3 collective-permute-start.18
  119.9 3.4 %collective-permute-start.16 = (bf16[5,3,192,128]{3,2,1,0:T(8,128)(2,1)}, bf16[5,3,192,128]{3,2,1,0:T(8,128)(2,1)}, u32[]{:S(2)}, u32[]{:S(2)}) collective-permute-start(bf16[5,3,192,128]{3,2,1,0:T(8,128)(2,1)} %get-tuple-element.17.refs_2_.refs_6_), channel_id=1, source_target_pairs={{0,128},{1,129},{2,130},{3,131},{4,132},{5,133},{6,134},{7,135},{8... | collective-permute-start | bytes 2211848 | tf_op jit(solution)/shard_map/ppermute | solution.py:44
  123.3 2.4 %collective-permute-start.17 = (bf16[5,3,192,128]{3,2,1,0:T(8,128)(2,1)}, bf16[5,3,192,128]{3,2,1,0:T(8,128)(2,1)}, u32[]{:S(2)}, u32[]{:S(2)}) collective-permute-start(bf16[5,3,192,128]{3,2,1,0:T(8,128)(2,1)} %copy-done.17), channel_id=1, source_target_pairs={{0,384},{1,385},{2,386},{3,387},{4,388},{5,389},{6,390},{7,391},{8... | collective-permute-start | bytes 2211848 | tf_op jit(solution)/shard_map/ppermute | solution.py:44
  125.8 3.3 %collective-permute-done.18.refs_2_.refs_1_ = bf16[2,3,192,128]{3,2,1,0:T(8,128)(2,1)S(1)} collective-permute-done((bf16[2,3,192,128]{3,2,1,0:T(8,128)(2,1)S(1)}, bf16[2,3,192,128]{3,2,1,0:T(8,128)(2,1)S(1)}, u32[]{:S(2)}, u32[]{:S(2)}) %collective-permute-start.18) | collective-permute-done | bytes 294944 | tf_op jit(solution)/shard_map/ppermute | solution.py:44
  129.1 0.7 copy-done.6
  129.8 1.0 copy-done.7
  130.8 1.4 shard_map.80
  132.2 3.4 %collective-permute-start.19 = (bf16[6,3,192,128]{3,2,1,0:T(8,128)(2,1)}, bf16[6,3,192,128]{3,2,1,0:T(8,128)(2,1)S(1)}, u32[]{:S(2)}, u32[]{:S(2)}) collective-permute-start(bf16[6,3,192,128]{3,2,1,0:T(8,128)(2,1)} %get-tuple-element.19.refs_9_), channel_id=1, source_target_pairs={{0,128},{1,129},{2,130},{3,131},{4,132},{5,133},{6,134},{7,135},{8... | collective-permute-start | bytes 2654216 | tf_op jit(solution)/shard_map/ppermute | solution.py:44
  135.6 2.4 %collective-permute-start.20 = (bf16[6,3,192,128]{3,2,1,0:T(8,128)(2,1)}, bf16[6,3,192,128]{3,2,1,0:T(8,128)(2,1)S(1)}, u32[]{:S(2)}, u32[]{:S(2)}) collective-permute-start(bf16[6,3,192,128]{3,2,1,0:T(8,128)(2,1)} %get-tuple-element.20), channel_id=1, source_target_pairs={{0,384},{1,385},{2,386},{3,387},{4,388},{5,389},{6,390},{7,391},{8... | collective-permute-start | bytes 2654216 | tf_op jit(solution)/shard_map/ppermute | solution.py:44
  138.1 1.3 collective-permute-start.21
  139.4 0.7 dynamic-slice_bitcast_fusion
  140.2 0.1 add.86
  140.2 1.3 collective-permute-done.16.refs_7_.refs_4_
  141.5 4.7 %collective-permute-done.17.refs_8_.refs_5_ = bf16[5,3,192,128]{3,2,1,0:T(8,128)(2,1)} collective-permute-done((bf16[5,3,192,128]{3,2,1,0:T(8,128)(2,1)}, bf16[5,3,192,128]{3,2,1,0:T(8,128)(2,1)}, u32[]{:S(2)}, u32[]{:S(2)}) %collective-permute-start.17) | collective-permute-done | bytes 737312 | tf_op jit(solution)/shard_map/ppermute | solution.py:44
  146.2 1.3 collective-permute-done.21.refs_0_
  147.5 1.0 copy-done.8
  148.5 2.6 %shard_map.82 = (bf16[4,3,192,128]{3,2,1,0:T(8,128)(2,1)}, bf16[4,3,192,128]{3,2,1,0:T(8,128)(2,1)}) custom-call(s32[1]{0:T(128)} %bitcast.5.zl_ref, bf16[2,3,192,128]{3,2,1,0:T(8,128)(2,1)} %collective-permute-done.21.refs_0_, bf16[2,3,192,128]{3,2,1,0:T(8,128)(2,1)S(1)} %copy-done.8, ...), custom_call_target="tpu_custom_call" | custom-call | bytes 4194304 | tf_op jit(solution)/shard_map/pallas_call | solution.py:217
  151.1 4.6 %collective-permute-start.22 = (bf16[4,3,192,128]{3,2,1,0:T(8,128)(2,1)}, bf16[4,3,192,128]{3,2,1,0:T(8,128)(2,1)}, u32[]{:S(2)}, u32[]{:S(2)}) collective-permute-start(bf16[4,3,192,128]{3,2,1,0:T(8,128)(2,1)} %get-tuple-element.21.refs_0_), channel_id=1, source_target_pairs={{0,128},{1,129},{2,130},{3,131},{4,132},{5,133},{6,134},{7,135},{8... | collective-permute-start | bytes 1769480 | tf_op jit(solution)/shard_map/ppermute | solution.py:44
  155.7 1.9 collective-permute-start.23
  157.7 0.7 reshape.37
  158.5 1.9 copy-done
  160.4 1.9 copy-done.1
  162.3 6.4 %shard_map.79.normed_ref = bf16[32,512,192]{2,1,0:T(8,128)(2,1)S(1)} custom-call(bf16[8,512,384]{2,1,0:T(8,128)(2,1)S(1)} %copy-done, bf16[8,512,384]{2,1,0:T(8,128)(2,1)S(1)} %bitcast.13, f32[16,384]{1,0:T(8,128)S(1)} %fusion.gain_ref), custom_call_target="tpu_custom_call" | custom-call | flops 25165824 | bytes 14680064 | tf_op jit(solution)/shard_map/pallas_call | solution.py:102
  168.8 6.9 %shard_map.81.held_ref.refs_4_ = f32[3,512,256]{2,1,0:T(8,128)S(1)} custom-call(s32[32]{0:T(128)S(1)} %fusion.1.index_ref, bf16[32,512,192]{2,1,0:T(8,128)(2,1)S(1)} %shard_map.79.normed_ref, bf16[2,3,192,128]{3,2,1,0:T(8,128)(2,1)S(1)} %copy-done.10, bf16[2,3,192,128]{3,2,1,0:T(8,128)(2,1)S(1)} %copy-done.3, bf16[2,3,192,128]{3,2,1,0:T(8,128)(2,1)S(1)} %copy-done.5, ...), custom_call_target="tpu_custom_call" | custom-call | flops 3623878656 | bytes 15466496 | tf_op jit(solution)/shard_map/pallas_call | solution.py:176
  175.7 0.5 collective-permute-done.23.refs_2_.refs_3_
  176.2 1.3 shard_map.84
  177.5 4.7 %collective-permute-start.24 = (bf16[3,3,192,128]{3,2,1,0:T(8,128)(2,1)S(1)}, bf16[3,3,192,128]{3,2,1,0:T(8,128)(2,1)S(1)}, u32[]{:S(2)}, u32[]{:S(2)}) collective-permute-start(bf16[3,3,192,128]{3,2,1,0:T(8,128)(2,1)S(1)} %get-tuple-element.23), channel_id=1, source_target_pairs={{0,128},{1,129},{2,130},{3,131},{4,132},{5,133},{6,134},{7,135},{8... | collective-permute-start | bytes 1327112 | tf_op jit(solution)/shard_map/ppermute | solution.py:44
  182.2 2.1 %collective-permute-start.25 = (bf16[3,3,192,128]{3,2,1,0:T(8,128)(2,1)S(1)}, bf16[3,3,192,128]{3,2,1,0:T(8,128)(2,1)S(1)}, u32[]{:S(2)}, u32[]{:S(2)}) collective-permute-start(bf16[3,3,192,128]{3,2,1,0:T(8,128)(2,1)S(1)} %get-tuple-element.24), channel_id=1, source_target_pairs={{0,384},{1,385},{2,386},{3,387},{4,388},{5,389},{6,390},{7,391},{8... | collective-permute-start | bytes 1327112 | tf_op jit(solution)/shard_map/ppermute | solution.py:44
  184.3 2.6 %shard_map.83.held_ref = f32[3,512,256]{2,1,0:T(8,128)S(1)} custom-call(s32[32]{0:T(128)S(1)} %fusion.1.index_ref, bf16[32,512,192]{2,1,0:T(8,128)(2,1)S(1)} %shard_map.79.normed_ref, f32[3,512,256]{2,1,0:T(8,128)S(1)} %shard_map.81.held_ref.refs_4_, bf16[4,3,192,128]{3,2,1,0:T(8,128)(2,1)} %get-tuple-element.21.refs_0_, ...), custom_call_target="tpu_custom_call" | custom-call | flops 754974720 | bytes 9863168 | tf_op jit(solution)/shard_map/pallas_call | solution.py:176
  186.9 3.0 %collective-permute-done.24.refs_0_ = bf16[3,3,192,128]{3,2,1,0:T(8,128)(2,1)S(1)} collective-permute-done((bf16[3,3,192,128]{3,2,1,0:T(8,128)(2,1)S(1)}, bf16[3,3,192,128]{3,2,1,0:T(8,128)(2,1)S(1)}, u32[]{:S(2)}, u32[]{:S(2)}) %collective-permute-start.24) | collective-permute-done | bytes 442400 | tf_op jit(solution)/shard_map/ppermute | solution.py:44
  189.9 4.0 %collective-permute-done.25.refs_1_ = bf16[3,3,192,128]{3,2,1,0:T(8,128)(2,1)S(1)} collective-permute-done((bf16[3,3,192,128]{3,2,1,0:T(8,128)(2,1)S(1)}, bf16[3,3,192,128]{3,2,1,0:T(8,128)(2,1)S(1)}, u32[]{:S(2)}, u32[]{:S(2)}) %collective-permute-start.25) | collective-permute-done | bytes 442400 | tf_op jit(solution)/shard_map/ppermute | solution.py:44
  193.9 3.6 %shard_map.85 = bf16[512,256]{1,0:T(8,128)(2,1)} custom-call(s32[32]{0:T(128)S(1)} %fusion.1.index_ref, bf16[32,512,192]{2,1,0:T(8,128)(2,1)S(1)} %shard_map.79.normed_ref, f32[3,512,256]{2,1,0:T(8,128)S(1)} %shard_map.83.held_ref, f32[2,256]{1,0:T(2,128)S(1)} %copy-done.14, bf16[3,3,192,128]{3,2,1,0:T(8,128)(2,1)S(1)} %collective-permute-done.24.refs_0_, ...), custom_call_target="tpu_custom_call" | custom-call | flops 452984832 | bytes 9273344 | tf_op jit(solution)/shard_map/pallas_call | solution.py:176
  (52 shorter events, 0.4 us)
Async XLA Ops:
  6.5 151.9 %all-gather.4.cloned.1.call-start = ((), (), s32[]{:S(2)}) async-start(), calls=%async_computation | async-start | bytes 3538944 | tf_op jit(solution)/shard_map/all_gather | solution.py:302
  6.5 32.7 %collective-permute-start = (bf16[2,256,384]{2,1,0:T(8,128)(2,1)}, bf16[2,256,384]{2,1,0:T(8,128)(2,1)S(1)}, u32[]{:S(2)}, u32[]{:S(2)}) collective-permute-start(bf16[2,256,384]{2,1,0:T(8,128)(2,1)} %tokens_ref.1), channel_id=1, source_target_pairs={{0,496},{1,497},{2,498},{3,499},{4,500},{5,501},{6,502},{7,503},{8... | collective-permute-start | bytes 1179656 | tf_op jit(solution)/shard_map/ppermute | solution.py:44
  21.0 22.1 %copy-start.9 = (bf16[2,3,192,128]{3,2,1,0:T(8,128)(2,1)}, bf16[2,3,192,128]{3,2,1,0:T(8,128)(2,1)S(1)}, u32[]{:S(2)}) copy-start(bf16[2,3,192,128]{3,2,1,0:T(8,128)(2,1)S(1)} %pad_maximum_fusion.refs_0_) | copy-start | bytes 884740
  21.0 13.8 %collective-permute-start.1 = (bf16[2,3,192,128]{3,2,1,0:T(8,128)(2,1)S(1)}, bf16[2,3,192,128]{3,2,1,0:T(8,128)(2,1)S(1)}, u32[]{:S(2)}, u32[]{:S(2)}) collective-permute-start(bf16[2,3,192,128]{3,2,1,0:T(8,128)(2,1)S(1)} %pad_maximum_fusion.refs_0_), channel_id=1, source_target_pairs={{0,16},{1,17},{2,18},{3,19},{4,20},{5,21},{6,22},{7,23},{8,24},{9,... | collective-permute-start | bytes 884744 | tf_op jit(solution)/shard_map/ppermute | solution.py:44
  22.3 12.5 %collective-permute-start.2 = (bf16[2,3,192,128]{3,2,1,0:T(8,128)(2,1)S(1)}, bf16[2,3,192,128]{3,2,1,0:T(8,128)(2,1)S(1)}, u32[]{:S(2)}, u32[]{:S(2)}) collective-permute-start(bf16[2,3,192,128]{3,2,1,0:T(8,128)(2,1)S(1)} %pad_maximum_fusion.refs_0_), channel_id=1, source_target_pairs={{16,0},{17,1},{18,2},{19,3},{20,4},{21,5},{22,6},{23,7},{24,8},{25... | collective-permute-start | bytes 884744 | tf_op jit(solution)/shard_map/ppermute | solution.py:44
  23.6 11.2 %collective-permute-start.3 = (bf16[2,3,192,128]{3,2,1,0:T(8,128)(2,1)S(1)}, bf16[2,3,192,128]{3,2,1,0:T(8,128)(2,1)S(1)}, u32[]{:S(2)}, u32[]{:S(2)}) collective-permute-start(bf16[2,3,192,128]{3,2,1,0:T(8,128)(2,1)S(1)} %pad_maximum_fusion.refs_0_), channel_id=1, source_target_pairs={{0,128},{1,129},{2,130},{3,131},{4,132},{5,133},{6,134},{7,135},{8... | collective-permute-start | bytes 884744 | tf_op jit(solution)/shard_map/ppermute | solution.py:44
  28.0 11.3 %collective-permute-start.4 = (bf16[2,3,192,128]{3,2,1,0:T(8,128)(2,1)S(1)}, bf16[2,3,192,128]{3,2,1,0:T(8,128)(2,1)S(1)}, u32[]{:S(2)}, u32[]{:S(2)}) collective-permute-start(bf16[2,3,192,128]{3,2,1,0:T(8,128)(2,1)S(1)} %pad_maximum_fusion.refs_0_), channel_id=1, source_target_pairs={{0,384},{1,385},{2,386},{3,387},{4,388},{5,389},{6,390},{7,391},{8... | collective-permute-start | bytes 884744 | tf_op jit(solution)/shard_map/ppermute | solution.py:44
  34.8 64.1 %copy-start.2 = (bf16[2,3,192,128]{3,2,1,0:T(8,128)(2,1)}, bf16[2,3,192,128]{3,2,1,0:T(8,128)(2,1)S(1)}, u32[]{:S(2)}) copy-start(bf16[2,3,192,128]{3,2,1,0:T(8,128)(2,1)S(1)} %collective-permute-done.3.refs_2_.refs_5_.refs_1_) | copy-start | bytes 884740
  39.2 59.7 %copy-start.4 = (bf16[2,3,192,128]{3,2,1,0:T(8,128)(2,1)}, bf16[2,3,192,128]{3,2,1,0:T(8,128)(2,1)S(1)}, u32[]{:S(2)}) copy-start(bf16[2,3,192,128]{3,2,1,0:T(8,128)(2,1)S(1)} %collective-permute-done.4.refs_3_.refs_6_.refs_2_) | copy-start | bytes 884740
  39.3 1.1 copy-start.13
  40.4 0.7 copy-start.15
  41.0 0.7 copy-start.16
  43.2 115.3 %all-gather.6.cloned.1.call-start = ((), (), s32[]{:S(2)}) async-start(), calls=%async_computation.1 | async-start | bytes 3538944 | tf_op jit(solution)/shard_map/all_gather | solution.py:341
  43.2 2.0 collective-permute-start.6
  43.9 10.1 %collective-permute-start.8 = (bf16[2,3,192,128]{3,2,1,0:T(8,128)(2,1)S(1)}, bf16[2,3,192,128]{3,2,1,0:T(8,128)(2,1)S(1)}, u32[]{:S(2)}, u32[]{:S(2)}) collective-permute-start(bf16[2,3,192,128]{3,2,1,0:T(8,128)(2,1)S(1)} %collective-permute-done.2.refs_1_), channel_id=1, source_target_pairs={{16,0},{17,1},{18,2},{19,3},{20,4},{21,5},{22,6},{23,7},{24,8},{25... | collective-permute-start | bytes 884744 | tf_op jit(solution)/shard_map/ppermute | solution.py:44
  45.2 21.4 %collective-permute-start.7 = (bf16[2,3,192,128]{3,2,1,0:T(8,128)(2,1)S(1)}, bf16[2,3,192,128]{3,2,1,0:T(8,128)(2,1)S(1)}, u32[]{:S(2)}, u32[]{:S(2)}) collective-permute-start(bf16[2,3,192,128]{3,2,1,0:T(8,128)(2,1)S(1)} %collective-permute-done.6.refs_2_.refs_0_), channel_id=1, source_target_pairs={{32,48},{33,49},{34,50},{35,51},{36,52},{37,53},{38,54},{39,55},{4... | collective-permute-start | bytes 884744 | tf_op jit(solution)/shard_map/ppermute | solution.py:44
  54.0 13.3 %collective-permute-start.9 = (bf16[2,3,192,128]{3,2,1,0:T(8,128)(2,1)S(1)}, bf16[2,3,192,128]{3,2,1,0:T(8,128)(2,1)S(1)}, u32[]{:S(2)}, u32[]{:S(2)}) collective-permute-start(bf16[2,3,192,128]{3,2,1,0:T(8,128)(2,1)S(1)} %collective-permute-done.8.refs_3_.refs_1_), channel_id=1, source_target_pairs={{16,0},{17,1},{18,2},{19,3},{20,4},{21,5},{22,6},{23,7},{24,8},{25... | collective-permute-start | bytes 884744 | tf_op jit(solution)/shard_map/ppermute | solution.py:44
  55.5 42.1 %copy-start.11 = (bf16[4,3,192,128]{3,2,1,0:T(8,128)(2,1)}, bf16[4,3,192,128]{3,2,1,0:T(8,128)(2,1)S(1)}, u32[]{:S(2)}) copy-start(bf16[4,3,192,128]{3,2,1,0:T(8,128)(2,1)S(1)} %get-tuple-element.15.refs_3_) | copy-start | bytes 1769476
  55.5 42.1 %collective-permute-start.13 = (bf16[4,3,192,128]{3,2,1,0:T(8,128)(2,1)S(1)}, bf16[4,3,192,128]{3,2,1,0:T(8,128)(2,1)S(1)}, u32[]{:S(2)}, u32[]{:S(2)}) collective-permute-start(bf16[4,3,192,128]{3,2,1,0:T(8,128)(2,1)S(1)} %get-tuple-element.15.refs_3_), channel_id=1, source_target_pairs={{0,128},{1,129},{2,130},{3,131},{4,132},{5,133},{6,134},{7,135},{8... | collective-permute-start | bytes 1769480 | tf_op jit(solution)/shard_map/ppermute | solution.py:44
  57.4 40.2 %collective-permute-start.14 = (bf16[4,3,192,128]{3,2,1,0:T(8,128)(2,1)S(1)}, bf16[4,3,192,128]{3,2,1,0:T(8,128)(2,1)S(1)}, u32[]{:S(2)}, u32[]{:S(2)}) collective-permute-start(bf16[4,3,192,128]{3,2,1,0:T(8,128)(2,1)S(1)} %get-tuple-element.16), channel_id=1, source_target_pairs={{0,384},{1,385},{2,386},{3,387},{4,388},{5,389},{6,390},{7,391},{8... | collective-permute-start | bytes 1769480 | tf_op jit(solution)/shard_map/ppermute | solution.py:44
  61.4 30.7 %collective-permute-start.5 = (bf16[512,384]{1,0:T(8,128)(2,1)}, bf16[512,384]{1,0:T(8,128)(2,1)S(1)}, u32[]{:S(2)}, u32[]{:S(2)}) collective-permute-start(bf16[512,384]{1,0:T(8,128)(2,1)} %bitcast.4), channel_id=1, source_target_pairs={{0,64},{1,65},{2,66},{3,67},{4,68},{5,69},{6,70},{7,71},{8,72},{9,... | collective-permute-start | bytes 1179656 | tf_op jit(solution)/shard_map/ppermute | solution.py:44
  66.6 27.4 %collective-permute-start.11 = (bf16[2,3,192,128]{3,2,1,0:T(8,128)(2,1)S(1)}, bf16[2,3,192,128]{3,2,1,0:T(8,128)(2,1)S(1)}, u32[]{:S(2)}, u32[]{:S(2)}) collective-permute-start(bf16[2,3,192,128]{3,2,1,0:T(8,128)(2,1)S(1)} %collective-permute-done.7.refs_1_.refs_2_.refs_3_), channel_id=1, source_target_pairs={{48,64},{49,65},{50,66},{51,67},{52,68},{53,69},{54,70},{55,71},{5... | collective-permute-start | bytes 884744 | tf_op jit(solution)/shard_map/ppermute | solution.py:44
  67.3 30.3 %collective-permute-start.12 = (bf16[2,3,192,128]{3,2,1,0:T(8,128)(2,1)S(1)}, bf16[2,3,192,128]{3,2,1,0:T(8,128)(2,1)S(1)}, u32[]{:S(2)}, u32[]{:S(2)}) collective-permute-start(bf16[2,3,192,128]{3,2,1,0:T(8,128)(2,1)S(1)} %collective-permute-done.9.refs_2_.refs_3_.refs_4_), channel_id=1, source_target_pairs={{16,0},{17,1},{18,2},{19,3},{20,4},{21,5},{22,6},{23,7},{24,8},{25... | collective-permute-start | bytes 884744 | tf_op jit(solution)/shard_map/ppermute | solution.py:44
  92.1 20.2 %collective-permute-start.10 = (bf16[512,384]{1,0:T(8,128)(2,1)S(1)}, bf16[512,384]{1,0:T(8,128)(2,1)S(1)}, u32[]{:S(2)}, u32[]{:S(2)}) collective-permute-start(bf16[512,384]{1,0:T(8,128)(2,1)S(1)} %shard_map.74), channel_id=1, source_target_pairs={{0,64},{1,65},{2,66},{3,67},{4,68},{5,69},{6,70},{7,71},{8,72},{9,... | collective-permute-start | bytes 1179656 | tf_op jit(solution)/shard_map/ppermute | solution.py:44
  97.6 20.2 %collective-permute-start.15 = (bf16[2,3,192,128]{3,2,1,0:T(8,128)(2,1)S(1)}, bf16[2,3,192,128]{3,2,1,0:T(8,128)(2,1)S(1)}, u32[]{:S(2)}, u32[]{:S(2)}) collective-permute-start(bf16[2,3,192,128]{3,2,1,0:T(8,128)(2,1)S(1)} %shard_map.76.refs_4_.refs_0_), channel_id=1, source_target_pairs={{16,0},{17,1},{18,2},{19,3},{20,4},{21,5},{22,6},{23,7},{24,8},{25... | collective-permute-start | bytes 884744 | tf_op jit(solution)/shard_map/ppermute | solution.py:44
  100.0 0.9 copy-start.17
  118.6 10.5 %collective-permute-start.18 = (bf16[2,3,192,128]{3,2,1,0:T(8,128)(2,1)S(1)}, bf16[2,3,192,128]{3,2,1,0:T(8,128)(2,1)S(1)}, u32[]{:S(2)}, u32[]{:S(2)}) collective-permute-start(bf16[2,3,192,128]{3,2,1,0:T(8,128)(2,1)S(1)} %collective-permute-done.15.refs_1_), channel_id=1, source_target_pairs={{16,0},{17,1},{18,2},{19,3},{20,4},{21,5},{22,6},{23,7},{24,8},{25... | collective-permute-start | bytes 884744 | tf_op jit(solution)/shard_map/ppermute | solution.py:44
  119.9 21.6 %collective-permute-start.16 = (bf16[5,3,192,128]{3,2,1,0:T(8,128)(2,1)}, bf16[5,3,192,128]{3,2,1,0:T(8,128)(2,1)}, u32[]{:S(2)}, u32[]{:S(2)}) collective-permute-start(bf16[5,3,192,128]{3,2,1,0:T(8,128)(2,1)} %get-tuple-element.17.refs_2_.refs_6_), channel_id=1, source_target_pairs={{0,128},{1,129},{2,130},{3,131},{4,132},{5,133},{6,134},{7,135},{8... | collective-permute-start | bytes 2211848 | tf_op jit(solution)/shard_map/ppermute | solution.py:44
  123.3 22.8 %collective-permute-start.17 = (bf16[5,3,192,128]{3,2,1,0:T(8,128)(2,1)}, bf16[5,3,192,128]{3,2,1,0:T(8,128)(2,1)}, u32[]{:S(2)}, u32[]{:S(2)}) collective-permute-start(bf16[5,3,192,128]{3,2,1,0:T(8,128)(2,1)} %copy-done.17), channel_id=1, source_target_pairs={{0,384},{1,385},{2,386},{3,387},{4,388},{5,389},{6,390},{7,391},{8... | collective-permute-start | bytes 2211848 | tf_op jit(solution)/shard_map/ppermute | solution.py:44
  129.1 0.7 copy-start.6
  129.8 1.0 copy-start.7
  132.2 36.5 %collective-permute-start.19 = (bf16[6,3,192,128]{3,2,1,0:T(8,128)(2,1)}, bf16[6,3,192,128]{3,2,1,0:T(8,128)(2,1)S(1)}, u32[]{:S(2)}, u32[]{:S(2)}) collective-permute-start(bf16[6,3,192,128]{3,2,1,0:T(8,128)(2,1)} %get-tuple-element.19.refs_9_), channel_id=1, source_target_pairs={{0,128},{1,129},{2,130},{3,131},{4,132},{5,133},{6,134},{7,135},{8... | collective-permute-start | bytes 2654216 | tf_op jit(solution)/shard_map/ppermute | solution.py:44
  135.6 33.1 %collective-permute-start.20 = (bf16[6,3,192,128]{3,2,1,0:T(8,128)(2,1)}, bf16[6,3,192,128]{3,2,1,0:T(8,128)(2,1)S(1)}, u32[]{:S(2)}, u32[]{:S(2)}) collective-permute-start(bf16[6,3,192,128]{3,2,1,0:T(8,128)(2,1)} %get-tuple-element.20), channel_id=1, source_target_pairs={{0,384},{1,385},{2,386},{3,387},{4,388},{5,389},{6,390},{7,391},{8... | collective-permute-start | bytes 2654216 | tf_op jit(solution)/shard_map/ppermute | solution.py:44
  138.1 9.4 %collective-permute-start.21 = (bf16[2,3,192,128]{3,2,1,0:T(8,128)(2,1)}, bf16[2,3,192,128]{3,2,1,0:T(8,128)(2,1)}, u32[]{:S(2)}, u32[]{:S(2)}) collective-permute-start(bf16[2,3,192,128]{3,2,1,0:T(8,128)(2,1)} %copy-done.6), channel_id=1, source_target_pairs={{16,0},{17,1},{18,2},{19,3},{20,4},{21,5},{22,6},{23,7},{24,8},{25... | collective-permute-start | bytes 884744 | tf_op jit(solution)/shard_map/ppermute | solution.py:44
  147.5 1.0 copy-start.8
  151.1 24.6 %collective-permute-start.22 = (bf16[4,3,192,128]{3,2,1,0:T(8,128)(2,1)}, bf16[4,3,192,128]{3,2,1,0:T(8,128)(2,1)}, u32[]{:S(2)}, u32[]{:S(2)}) collective-permute-start(bf16[4,3,192,128]{3,2,1,0:T(8,128)(2,1)} %get-tuple-element.21.refs_0_), channel_id=1, source_target_pairs={{0,128},{1,129},{2,130},{3,131},{4,132},{5,133},{6,134},{7,135},{8... | collective-permute-start | bytes 1769480 | tf_op jit(solution)/shard_map/ppermute | solution.py:44
  155.7 20.4 %collective-permute-start.23 = (bf16[4,3,192,128]{3,2,1,0:T(8,128)(2,1)}, bf16[4,3,192,128]{3,2,1,0:T(8,128)(2,1)}, u32[]{:S(2)}, u32[]{:S(2)}) collective-permute-start(bf16[4,3,192,128]{3,2,1,0:T(8,128)(2,1)} %get-tuple-element.22), channel_id=1, source_target_pairs={{0,384},{1,385},{2,386},{3,387},{4,388},{5,389},{6,390},{7,391},{8... | collective-permute-start | bytes 1769480 | tf_op jit(solution)/shard_map/ppermute | solution.py:44
  158.5 1.9 copy-start
  160.4 1.9 copy-start.1
  162.3 6.5 %copy-start.3 = (bf16[2,3,192,128]{3,2,1,0:T(8,128)(2,1)S(1)}, bf16[2,3,192,128]{3,2,1,0:T(8,128)(2,1)}, u32[]{:S(2)}) copy-start(bf16[2,3,192,128]{3,2,1,0:T(8,128)(2,1)} %copy-done.2) | copy-start | bytes 884740
  162.3 6.5 %copy-start.5 = (bf16[2,3,192,128]{3,2,1,0:T(8,128)(2,1)S(1)}, bf16[2,3,192,128]{3,2,1,0:T(8,128)(2,1)}, u32[]{:S(2)}) copy-start(bf16[2,3,192,128]{3,2,1,0:T(8,128)(2,1)} %copy-done.4) | copy-start | bytes 884740
  162.3 6.5 %copy-start.10 = (bf16[2,3,192,128]{3,2,1,0:T(8,128)(2,1)S(1)}, bf16[2,3,192,128]{3,2,1,0:T(8,128)(2,1)}, u32[]{:S(2)}) copy-start(bf16[2,3,192,128]{3,2,1,0:T(8,128)(2,1)} %copy-done.9) | copy-start | bytes 884740
  162.3 6.5 %copy-start.12 = (bf16[4,3,192,128]{3,2,1,0:T(8,128)(2,1)S(1)}, bf16[4,3,192,128]{3,2,1,0:T(8,128)(2,1)}, u32[]{:S(2)}) copy-start(bf16[4,3,192,128]{3,2,1,0:T(8,128)(2,1)} %copy-done.11) | copy-start | bytes 1769476
  177.5 12.4 %collective-permute-start.24 = (bf16[3,3,192,128]{3,2,1,0:T(8,128)(2,1)S(1)}, bf16[3,3,192,128]{3,2,1,0:T(8,128)(2,1)S(1)}, u32[]{:S(2)}, u32[]{:S(2)}) collective-permute-start(bf16[3,3,192,128]{3,2,1,0:T(8,128)(2,1)S(1)} %get-tuple-element.23), channel_id=1, source_target_pairs={{0,128},{1,129},{2,130},{3,131},{4,132},{5,133},{6,134},{7,135},{8... | collective-permute-start | bytes 1327112 | tf_op jit(solution)/shard_map/ppermute | solution.py:44
  182.1 11.7 %copy-start.14 = (f32[2,256]{1,0:T(2,128)S(1)}, f32[2,256]{1,0:T(2,128)}, u32[]{:S(2)}) copy-start(f32[2,256]{1,0:T(2,128)} %gain_ref.1) | copy-start | bytes 6148
  182.2 11.7 %collective-permute-start.25 = (bf16[3,3,192,128]{3,2,1,0:T(8,128)(2,1)S(1)}, bf16[3,3,192,128]{3,2,1,0:T(8,128)(2,1)S(1)}, u32[]{:S(2)}, u32[]{:S(2)}) collective-permute-start(bf16[3,3,192,128]{3,2,1,0:T(8,128)(2,1)S(1)} %get-tuple-element.24), channel_id=1, source_target_pairs={{0,384},{1,385},{2,386},{3,387},{4,388},{5,389},{6,390},{7,391},{8... | collective-permute-start | bytes 1327112 | tf_op jit(solution)/shard_map/ppermute | solution.py:44
Sparse Core Ops, SparseCore 0:
  43.3 32.9 all-gather.3
  118.7 33.2 all-gather.5

commit v7 on v6

--- a/solution.py
+++ b/solution.py
@@ -219,7 +219,7 @@
         out_shape=(message, message),
         in_specs=[pl.BlockSpec(memory_space=pltpu.SMEM)]
         + [whole] * (len(arrays) + 2 * len(forward))
-        + [pl.BlockSpec(memory_space=pl.ANY)] * len(after),
+        + [pl.BlockSpec(memory_space=pltpu.VMEM)] * len(after),
         out_specs=(whole, whole),
         compiler_params=pltpu.CompilerParams(vmem_limit_bytes=16 * 2**20),
         cost_estimate=pl.CostEstimate(flops=0, bytes_accessed=4 * 2**20, transcendentals=0),
@@ -243,7 +243,7 @@
         mix_kernel,
         out_shape=jax.ShapeDtypeStruct(tokens.shape, tokens.dtype),
         in_specs=[scalars, scalars, whole, whole]
-        + [pl.BlockSpec(memory_space=pl.ANY)] * len(after),
+        + [pl.BlockSpec(memory_space=pltpu.VMEM)] * len(after),
         out_specs=whole,
         compiler_params=pltpu.CompilerParams(vmem_limit_bytes=8 * 2**20),
     )(weight, offset, tokens, partner, *after)
@@ -259,7 +259,7 @@
     return pl.pallas_call(
         functools.partial(copy_kernel, len(values)),
         out_shape=[jax.ShapeDtypeStruct(value.shape, value.dtype) for value in values],
-        in_specs=[whole] * len(values) + [pl.BlockSpec(memory_space=pl.ANY)] * len(after),
+        in_specs=[whole] * len(values) + [pl.BlockSpec(memory_space=pltpu.VMEM)] * len(after),
         out_specs=[whole] * len(values),
         compiler_params=pltpu.CompilerParams(vmem_limit_bytes=8 * 2**20),
     )(*values, *after)
@@ -281,7 +281,7 @@
         either_kernel,
         out_shape=jax.ShapeDtypeStruct(upper.shape, upper.dtype),
         in_specs=[pl.BlockSpec(memory_space=pltpu.SMEM), whole, whole]
-        + [pl.BlockSpec(memory_space=pl.ANY)] * len(after),
+        + [pl.BlockSpec(memory_space=pltpu.VMEM)] * len(after),
         out_specs=whole,
         compiler_params=pltpu.CompilerParams(vmem_limit_bytes=8 * 2**20),
     )(row, upper, lower, *after)

time: 205 us -> 207 us (level)
  no operation moved by 1% of the time
where the time goes in v7:
time: 207 us; the launch traced here: 205 us
  waiting for transfers between devices  79.5 us (38%)
  starting transfers between devices  70.1 us (34%)
  Pallas kernels  29.5 us (14%)
  between operations  13.9 us (7%)
  local copies, waits for them, and re-layouts  12.3 us (6%)
    ppermute x26, waiting for transfers between devices, move(): return lax.ppermute(value, AXES, pairs)  79.4 us
    ppermute x26, starting transfers between devices, move(): return lax.ppermute(value, AXES, pairs)  70.1 us
    pallas_call x3, Pallas kernels, project(): pl.pallas_call(functools.partial(kernel, blocks), out_shape=out_shape, in...  13.1 us
    unnamed x36, local copies, waits for them, and re-layouts  9.75 us
    pallas_call x5, Pallas kernels, relay(): pl.pallas_call(functools.partial(relay_kernel, slots, forward, len(arrays...  6.57 us
    pallas_call x1, Pallas kernels, norm_tokens(): pl.pallas_call(norm_kernel, out_shape=jax.ShapeDtypeStruct((32, 512, 192)...  6.42 us
  transfers between devices with their start and end apart: 28, of which 14 were waited for; matrix products, arithmetic and copies ran while one was open for 1% of the time, Pallas kernels for 11%

profile of v7, /device:TPU:6, one launch (start us, length us, event | category | flops | bytes accessed | tf_op | source)
XLA Modules:
  0.0 205.4 jit_solution(7831407143274448163)
XLA Ops:
  6.5 13.4 %collective-permute-start = (bf16[2,256,384]{2,1,0:T(8,128)(2,1)}, bf16[2,256,384]{2,1,0:T(8,128)(2,1)S(1)}, u32[]{:S(2)}, u32[]{:S(2)}) collective-permute-start(bf16[2,256,384]{2,1,0:T(8,128)(2,1)} %tokens_ref.1), channel_id=1, source_target_pairs={{0,496},{1,497},{2,498},{3,499},{4,500},{5,501},{6,502},{7,503},{8... | collective-permute-start | bytes 1179656 | tf_op jit(solution)/shard_map/ppermute | solution.py:44
  20.0 1.0 slice_bitcast_fusion.1
  21.0 1.3 collective-permute-start.1
  22.3 1.3 collective-permute-start.2
  23.6 4.3 %collective-permute-start.3 = (bf16[2,3,192,128]{3,2,1,0:T(8,128)(2,1)S(1)}, bf16[2,3,192,128]{3,2,1,0:T(8,128)(2,1)S(1)}, u32[]{:S(2)}, u32[]{:S(2)}) collective-permute-start(bf16[2,3,192,128]{3,2,1,0:T(8,128)(2,1)S(1)} %pad_maximum_fusion.refs_0_), channel_id=1, source_target_pairs={{0,128},{1,129},{2,130},{3,131},{4,132},{5,133},{6,134},{7,135},{8... | collective-permute-start | bytes 884744 | tf_op jit(solution)/shard_map/ppermute | solution.py:44
  28.0 1.9 collective-permute-start.4
  29.9 5.0 %collective-permute-done.1.refs_0_ = bf16[2,3,192,128]{3,2,1,0:T(8,128)(2,1)S(1)} collective-permute-done((bf16[2,3,192,128]{3,2,1,0:T(8,128)(2,1)S(1)}, bf16[2,3,192,128]{3,2,1,0:T(8,128)(2,1)S(1)}, u32[]{:S(2)}, u32[]{:S(2)}) %collective-permute-start.1) | collective-permute-done | bytes 294944 | tf_op jit(solution)/shard_map/ppermute | solution.py:44
  34.8 4.4 %collective-permute-done.4.refs_3_.refs_6_.refs_2_ = bf16[2,3,192,128]{3,2,1,0:T(8,128)(2,1)S(1)} collective-permute-done((bf16[2,3,192,128]{3,2,1,0:T(8,128)(2,1)S(1)}, bf16[2,3,192,128]{3,2,1,0:T(8,128)(2,1)S(1)}, u32[]{:S(2)}, u32[]{:S(2)}) %collective-permute-start.4) | collective-permute-done | bytes 294944 | tf_op jit(solution)/shard_map/ppermute | solution.py:44
  39.3 1.1 copy-done.13
  40.4 0.7 copy-done.15
  41.0 0.7 copy-done.16
  41.7 1.5 shard_map.73
  43.2 0.7 collective-permute-start.6
  43.9 1.3 collective-permute-start.8
  45.2 0.7 collective-permute-start.7
  45.9 8.1 %collective-permute-done.8.refs_3_.refs_1_ = bf16[2,3,192,128]{3,2,1,0:T(8,128)(2,1)S(1)} collective-permute-done((bf16[2,3,192,128]{3,2,1,0:T(8,128)(2,1)S(1)}, bf16[2,3,192,128]{3,2,1,0:T(8,128)(2,1)S(1)}, u32[]{:S(2)}, u32[]{:S(2)}) %collective-permute-start.8) | collective-permute-done | bytes 294944 | tf_op jit(solution)/shard_map/ppermute | solution.py:44
  54.0 1.3 collective-permute-start.9
  55.3 0.2 shard_map.75
  55.5 1.9 collective-permute-start.13
  57.4 3.9 %collective-permute-start.14 = (bf16[4,3,192,128]{3,2,1,0:T(8,128)(2,1)S(1)}, bf16[4,3,192,128]{3,2,1,0:T(8,128)(2,1)S(1)}, u32[]{:S(2)}, u32[]{:S(2)}) collective-permute-start(bf16[4,3,192,128]{3,2,1,0:T(8,128)(2,1)S(1)} %get-tuple-element.16), channel_id=1, source_target_pairs={{0,384},{1,385},{2,386},{3,387},{4,388},{5,389},{6,390},{7,391},{8... | collective-permute-start | bytes 1769480 | tf_op jit(solution)/shard_map/ppermute | solution.py:44
  61.4 5.3 %collective-permute-start.5 = (bf16[512,384]{1,0:T(8,128)(2,1)}, bf16[512,384]{1,0:T(8,128)(2,1)S(1)}, u32[]{:S(2)}, u32[]{:S(2)}) collective-permute-start(bf16[512,384]{1,0:T(8,128)(2,1)} %bitcast.4), channel_id=1, source_target_pairs={{0,64},{1,65},{2,66},{3,67},{4,68},{5,69},{6,70},{7,71},{8,72},{9,... | collective-permute-start | bytes 1179656 | tf_op jit(solution)/shard_map/ppermute | solution.py:44
  66.6 0.7 collective-permute-start.11
  67.3 1.3 collective-permute-start.12
  68.6 23.5 %collective-permute-done.5.refs_0_ = bf16[512,384]{1,0:T(8,128)(2,1)S(1)} collective-permute-done((bf16[512,384]{1,0:T(8,128)(2,1)}, bf16[512,384]{1,0:T(8,128)(2,1)S(1)}, u32[]{:S(2)}, u32[]{:S(2)}) %collective-permute-start.5) | collective-permute-done | bytes 393248 | tf_op jit(solution)/shard_map/ppermute | solution.py:44
  92.1 1.9 collective-permute-start.10
  94.1 3.5 %collective-permute-done.12.lower_ref = bf16[2,3,192,128]{3,2,1,0:T(8,128)(2,1)S(1)} collective-permute-done((bf16[2,3,192,128]{3,2,1,0:T(8,128)(2,1)S(1)}, bf16[2,3,192,128]{3,2,1,0:T(8,128)(2,1)S(1)}, u32[]{:S(2)}, u32[]{:S(2)}) %collective-permute-start.12) | collective-permute-done | bytes 294944 | tf_op jit(solution)/shard_map/ppermute | solution.py:44
  97.6 1.3 collective-permute-start.15
  99.0 1.1 shard_map.77
  100.0 0.9 copy-done.17
  100.9 11.4 %collective-permute-done.10.refs_0_ = bf16[512,384]{1,0:T(8,128)(2,1)S(1)} collective-permute-done((bf16[512,384]{1,0:T(8,128)(2,1)S(1)}, bf16[512,384]{1,0:T(8,128)(2,1)S(1)}, u32[]{:S(2)}, u32[]{:S(2)}) %collective-permute-start.10) | collective-permute-done | bytes 393248 | tf_op jit(solution)/shard_map/ppermute | solution.py:44
  112.4 5.5 %collective-permute-done.15.refs_1_ = bf16[2,3,192,128]{3,2,1,0:T(8,128)(2,1)S(1)} collective-permute-done((bf16[2,3,192,128]{3,2,1,0:T(8,128)(2,1)S(1)}, bf16[2,3,192,128]{3,2,1,0:T(8,128)(2,1)S(1)}, u32[]{:S(2)}, u32[]{:S(2)}) %collective-permute-start.15) | collective-permute-done | bytes 294944 | tf_op jit(solution)/shard_map/ppermute | solution.py:44
  117.8 1.9 shard_map.78
  119.7 1.3 collective-permute-start.18
  121.0 3.4 %collective-permute-start.16 = (bf16[5,3,192,128]{3,2,1,0:T(8,128)(2,1)}, bf16[5,3,192,128]{3,2,1,0:T(8,128)(2,1)}, u32[]{:S(2)}, u32[]{:S(2)}) collective-permute-start(bf16[5,3,192,128]{3,2,1,0:T(8,128)(2,1)} %get-tuple-element.17.refs_2_.refs_6_), channel_id=1, source_target_pairs={{0,128},{1,129},{2,130},{3,131},{4,132},{5,133},{6,134},{7,135},{8... | collective-permute-start | bytes 2211848 | tf_op jit(solution)/shard_map/ppermute | solution.py:44
  124.5 2.4 %collective-permute-start.17 = (bf16[5,3,192,128]{3,2,1,0:T(8,128)(2,1)}, bf16[5,3,192,128]{3,2,1,0:T(8,128)(2,1)}, u32[]{:S(2)}, u32[]{:S(2)}) collective-permute-start(bf16[5,3,192,128]{3,2,1,0:T(8,128)(2,1)} %copy-done.17), channel_id=1, source_target_pairs={{0,384},{1,385},{2,386},{3,387},{4,388},{5,389},{6,390},{7,391},{8... | collective-permute-start | bytes 2211848 | tf_op jit(solution)/shard_map/ppermute | solution.py:44
  126.9 3.3 %collective-permute-done.18.refs_2_.refs_1_ = bf16[2,3,192,128]{3,2,1,0:T(8,128)(2,1)S(1)} collective-permute-done((bf16[2,3,192,128]{3,2,1,0:T(8,128)(2,1)S(1)}, bf16[2,3,192,128]{3,2,1,0:T(8,128)(2,1)S(1)}, u32[]{:S(2)}, u32[]{:S(2)}) %collective-permute-start.18) | collective-permute-done | bytes 294944 | tf_op jit(solution)/shard_map/ppermute | solution.py:44
  130.2 0.7 copy-done.6
  130.9 1.0 copy-done.7
  131.9 1.4 shard_map.80
  133.3 3.4 %collective-permute-start.19 = (bf16[6,3,192,128]{3,2,1,0:T(8,128)(2,1)}, bf16[6,3,192,128]{3,2,1,0:T(8,128)(2,1)S(1)}, u32[]{:S(2)}, u32[]{:S(2)}) collective-permute-start(bf16[6,3,192,128]{3,2,1,0:T(8,128)(2,1)} %get-tuple-element.19.refs_9_), channel_id=1, source_target_pairs={{0,128},{1,129},{2,130},{3,131},{4,132},{5,133},{6,134},{7,135},{8... | collective-permute-start | bytes 2654216 | tf_op jit(solution)/shard_map/ppermute | solution.py:44
  136.7 2.4 %collective-permute-start.20 = (bf16[6,3,192,128]{3,2,1,0:T(8,128)(2,1)}, bf16[6,3,192,128]{3,2,1,0:T(8,128)(2,1)S(1)}, u32[]{:S(2)}, u32[]{:S(2)}) collective-permute-start(bf16[6,3,192,128]{3,2,1,0:T(8,128)(2,1)} %get-tuple-element.20), channel_id=1, source_target_pairs={{0,384},{1,385},{2,386},{3,387},{4,388},{5,389},{6,390},{7,391},{8... | collective-permute-start | bytes 2654216 | tf_op jit(solution)/shard_map/ppermute | solution.py:44
  139.2 1.3 collective-permute-start.21
  140.5 0.7 dynamic-slice_bitcast_fusion
  141.3 0.1 add.86
  141.4 1.3 collective-permute-done.16.refs_7_.refs_4_
  142.7 4.7 %collective-permute-done.17.refs_8_.refs_5_ = bf16[5,3,192,128]{3,2,1,0:T(8,128)(2,1)} collective-permute-done((bf16[5,3,192,128]{3,2,1,0:T(8,128)(2,1)}, bf16[5,3,192,128]{3,2,1,0:T(8,128)(2,1)}, u32[]{:S(2)}, u32[]{:S(2)}) %collective-permute-start.17) | collective-permute-done | bytes 737312 | tf_op jit(solution)/shard_map/ppermute | solution.py:44
  147.3 1.3 collective-permute-done.21.refs_0_
  148.6 1.0 copy-done.8
  149.6 2.6 %shard_map.82 = (bf16[4,3,192,128]{3,2,1,0:T(8,128)(2,1)}, bf16[4,3,192,128]{3,2,1,0:T(8,128)(2,1)}) custom-call(s32[1]{0:T(128)} %bitcast.5.zl_ref, bf16[2,3,192,128]{3,2,1,0:T(8,128)(2,1)} %collective-permute-done.21.refs_0_, bf16[2,3,192,128]{3,2,1,0:T(8,128)(2,1)S(1)} %copy-done.8, ...), custom_call_target="tpu_custom_call" | custom-call | bytes 4194304 | tf_op jit(solution)/shard_map/pallas_call | solution.py:217
  152.2 4.6 %collective-permute-start.22 = (bf16[4,3,192,128]{3,2,1,0:T(8,128)(2,1)}, bf16[4,3,192,128]{3,2,1,0:T(8,128)(2,1)}, u32[]{:S(2)}, u32[]{:S(2)}) collective-permute-start(bf16[4,3,192,128]{3,2,1,0:T(8,128)(2,1)} %get-tuple-element.21.refs_0_), channel_id=1, source_target_pairs={{0,128},{1,129},{2,130},{3,131},{4,132},{5,133},{6,134},{7,135},{8... | collective-permute-start | bytes 1769480 | tf_op jit(solution)/shard_map/ppermute | solution.py:44
  156.8 1.9 collective-permute-start.23
  158.8 0.7 reshape.37
  159.6 1.9 copy-done
  161.5 1.9 copy-done.1
  163.4 6.4 %shard_map.79.normed_ref = bf16[32,512,192]{2,1,0:T(8,128)(2,1)S(1)} custom-call(bf16[8,512,384]{2,1,0:T(8,128)(2,1)S(1)} %copy-done, bf16[8,512,384]{2,1,0:T(8,128)(2,1)S(1)} %bitcast.13, f32[16,384]{1,0:T(8,128)S(1)} %fusion.gain_ref), custom_call_target="tpu_custom_call" | custom-call | flops 25165824 | bytes 14680064 | tf_op jit(solution)/shard_map/pallas_call | solution.py:102
  169.9 6.9 %shard_map.81.held_ref.refs_4_ = f32[3,512,256]{2,1,0:T(8,128)S(1)} custom-call(s32[32]{0:T(128)S(1)} %fusion.1.index_ref, bf16[32,512,192]{2,1,0:T(8,128)(2,1)S(1)} %shard_map.79.normed_ref, bf16[2,3,192,128]{3,2,1,0:T(8,128)(2,1)S(1)} %copy-done.10, bf16[2,3,192,128]{3,2,1,0:T(8,128)(2,1)S(1)} %copy-done.3, bf16[2,3,192,128]{3,2,1,0:T(8,128)(2,1)S(1)} %copy-done.5, ...), custom_call_target="tpu_custom_call" | custom-call | flops 3623878656 | bytes 15466496 | tf_op jit(solution)/shard_map/pallas_call | solution.py:176
  176.8 0.5 collective-permute-done.23.refs_2_.refs_3_
  177.3 1.3 shard_map.84
  178.6 4.7 %collective-permute-start.24 = (bf16[3,3,192,128]{3,2,1,0:T(8,128)(2,1)S(1)}, bf16[3,3,192,128]{3,2,1,0:T(8,128)(2,1)S(1)}, u32[]{:S(2)}, u32[]{:S(2)}) collective-permute-start(bf16[3,3,192,128]{3,2,1,0:T(8,128)(2,1)S(1)} %get-tuple-element.23), channel_id=1, source_target_pairs={{0,128},{1,129},{2,130},{3,131},{4,132},{5,133},{6,134},{7,135},{8... | collective-permute-start | bytes 1327112 | tf_op jit(solution)/shard_map/ppermute | solution.py:44
  183.3 2.1 %collective-permute-start.25 = (bf16[3,3,192,128]{3,2,1,0:T(8,128)(2,1)S(1)}, bf16[3,3,192,128]{3,2,1,0:T(8,128)(2,1)S(1)}, u32[]{:S(2)}, u32[]{:S(2)}) collective-permute-start(bf16[3,3,192,128]{3,2,1,0:T(8,128)(2,1)S(1)} %get-tuple-element.24), channel_id=1, source_target_pairs={{0,384},{1,385},{2,386},{3,387},{4,388},{5,389},{6,390},{7,391},{8... | collective-permute-start | bytes 1327112 | tf_op jit(solution)/shard_map/ppermute | solution.py:44
  185.4 2.6 %shard_map.83.held_ref = f32[3,512,256]{2,1,0:T(8,128)S(1)} custom-call(s32[32]{0:T(128)S(1)} %fusion.1.index_ref, bf16[32,512,192]{2,1,0:T(8,128)(2,1)S(1)} %shard_map.79.normed_ref, f32[3,512,256]{2,1,0:T(8,128)S(1)} %shard_map.81.held_ref.refs_4_, bf16[4,3,192,128]{3,2,1,0:T(8,128)(2,1)} %get-tuple-element.21.refs_0_, ...), custom_call_target="tpu_custom_call" | custom-call | flops 754974720 | bytes 9863168 | tf_op jit(solution)/shard_map/pallas_call | solution.py:176
  188.0 3.0 %collective-permute-done.24.refs_0_ = bf16[3,3,192,128]{3,2,1,0:T(8,128)(2,1)S(1)} collective-permute-done((bf16[3,3,192,128]{3,2,1,0:T(8,128)(2,1)S(1)}, bf16[3,3,192,128]{3,2,1,0:T(8,128)(2,1)S(1)}, u32[]{:S(2)}, u32[]{:S(2)}) %collective-permute-start.24) | collective-permute-done | bytes 442400 | tf_op jit(solution)/shard_map/ppermute | solution.py:44
  191.0 4.0 %collective-permute-done.25.refs_1_ = bf16[3,3,192,128]{3,2,1,0:T(8,128)(2,1)S(1)} collective-permute-done((bf16[3,3,192,128]{3,2,1,0:T(8,128)(2,1)S(1)}, bf16[3,3,192,128]{3,2,1,0:T(8,128)(2,1)S(1)}, u32[]{:S(2)}, u32[]{:S(2)}) %collective-permute-start.25) | collective-permute-done | bytes 442400 | tf_op jit(solution)/shard_map/ppermute | solution.py:44
  195.0 3.6 %shard_map.85 = bf16[512,256]{1,0:T(8,128)(2,1)} custom-call(s32[32]{0:T(128)S(1)} %fusion.1.index_ref, bf16[32,512,192]{2,1,0:T(8,128)(2,1)S(1)} %shard_map.79.normed_ref, f32[3,512,256]{2,1,0:T(8,128)S(1)} %shard_map.83.held_ref, f32[2,256]{1,0:T(2,128)S(1)} %copy-done.14, bf16[3,3,192,128]{3,2,1,0:T(8,128)(2,1)S(1)} %collective-permute-done.24.refs_0_, ...), custom_call_target="tpu_custom_call" | custom-call | flops 452984832 | bytes 9273344 | tf_op jit(solution)/shard_map/pallas_call | solution.py:176
  (52 shorter events, 0.4 us)
Async XLA Ops:
  6.5 153.0 %all-gather.4.cloned.1.call-start = ((), (), s32[]{:S(2)}) async-start(), calls=%async_computation | async-start | bytes 3538944 | tf_op jit(solution)/shard_map/all_gather | solution.py:302
  6.5 32.7 %collective-permute-start = (bf16[2,256,384]{2,1,0:T(8,128)(2,1)}, bf16[2,256,384]{2,1,0:T(8,128)(2,1)S(1)}, u32[]{:S(2)}, u32[]{:S(2)}) collective-permute-start(bf16[2,256,384]{2,1,0:T(8,128)(2,1)} %tokens_ref.1), channel_id=1, source_target_pairs={{0,496},{1,497},{2,498},{3,499},{4,500},{5,501},{6,502},{7,503},{8... | collective-permute-start | bytes 1179656 | tf_op jit(solution)/shard_map/ppermute | solution.py:44
  21.0 22.1 %copy-start.9 = (bf16[2,3,192,128]{3,2,1,0:T(8,128)(2,1)}, bf16[2,3,192,128]{3,2,1,0:T(8,128)(2,1)S(1)}, u32[]{:S(2)}) copy-start(bf16[2,3,192,128]{3,2,1,0:T(8,128)(2,1)S(1)} %pad_maximum_fusion.refs_0_) | copy-start | bytes 884740
  21.0 13.8 %collective-permute-start.1 = (bf16[2,3,192,128]{3,2,1,0:T(8,128)(2,1)S(1)}, bf16[2,3,192,128]{3,2,1,0:T(8,128)(2,1)S(1)}, u32[]{:S(2)}, u32[]{:S(2)}) collective-permute-start(bf16[2,3,192,128]{3,2,1,0:T(8,128)(2,1)S(1)} %pad_maximum_fusion.refs_0_), channel_id=1, source_target_pairs={{0,16},{1,17},{2,18},{3,19},{4,20},{5,21},{6,22},{7,23},{8,24},{9,... | collective-permute-start | bytes 884744 | tf_op jit(solution)/shard_map/ppermute | solution.py:44
  22.3 12.5 %collective-permute-start.2 = (bf16[2,3,192,128]{3,2,1,0:T(8,128)(2,1)S(1)}, bf16[2,3,192,128]{3,2,1,0:T(8,128)(2,1)S(1)}, u32[]{:S(2)}, u32[]{:S(2)}) collective-permute-start(bf16[2,3,192,128]{3,2,1,0:T(8,128)(2,1)S(1)} %pad_maximum_fusion.refs_0_), channel_id=1, source_target_pairs={{16,0},{17,1},{18,2},{19,3},{20,4},{21,5},{22,6},{23,7},{24,8},{25... | collective-permute-start | bytes 884744 | tf_op jit(solution)/shard_map/ppermute | solution.py:44
  23.6 11.2 %collective-permute-start.3 = (bf16[2,3,192,128]{3,2,1,0:T(8,128)(2,1)S(1)}, bf16[2,3,192,128]{3,2,1,0:T(8,128)(2,1)S(1)}, u32[]{:S(2)}, u32[]{:S(2)}) collective-permute-start(bf16[2,3,192,128]{3,2,1,0:T(8,128)(2,1)S(1)} %pad_maximum_fusion.refs_0_), channel_id=1, source_target_pairs={{0,128},{1,129},{2,130},{3,131},{4,132},{5,133},{6,134},{7,135},{8... | collective-permute-start | bytes 884744 | tf_op jit(solution)/shard_map/ppermute | solution.py:44
  28.0 11.3 %collective-permute-start.4 = (bf16[2,3,192,128]{3,2,1,0:T(8,128)(2,1)S(1)}, bf16[2,3,192,128]{3,2,1,0:T(8,128)(2,1)S(1)}, u32[]{:S(2)}, u32[]{:S(2)}) collective-permute-start(bf16[2,3,192,128]{3,2,1,0:T(8,128)(2,1)S(1)} %pad_maximum_fusion.refs_0_), channel_id=1, source_target_pairs={{0,384},{1,385},{2,386},{3,387},{4,388},{5,389},{6,390},{7,391},{8... | collective-permute-start | bytes 884744 | tf_op jit(solution)/shard_map/ppermute | solution.py:44
  34.8 64.1 %copy-start.2 = (bf16[2,3,192,128]{3,2,1,0:T(8,128)(2,1)}, bf16[2,3,192,128]{3,2,1,0:T(8,128)(2,1)S(1)}, u32[]{:S(2)}) copy-start(bf16[2,3,192,128]{3,2,1,0:T(8,128)(2,1)S(1)} %collective-permute-done.3.refs_2_.refs_5_.refs_1_) | copy-start | bytes 884740
  39.2 59.7 %copy-start.4 = (bf16[2,3,192,128]{3,2,1,0:T(8,128)(2,1)}, bf16[2,3,192,128]{3,2,1,0:T(8,128)(2,1)S(1)}, u32[]{:S(2)}) copy-start(bf16[2,3,192,128]{3,2,1,0:T(8,128)(2,1)S(1)} %collective-permute-done.4.refs_3_.refs_6_.refs_2_) | copy-start | bytes 884740
  39.3 1.1 copy-start.13
  40.4 0.7 copy-start.15
  41.0 0.7 copy-start.16
  43.2 116.4 %all-gather.6.cloned.1.call-start = ((), (), s32[]{:S(2)}) async-start(), calls=%async_computation.1 | async-start | bytes 3538944 | tf_op jit(solution)/shard_map/all_gather | solution.py:341
  43.2 2.0 collective-permute-start.6
  43.9 10.1 %collective-permute-start.8 = (bf16[2,3,192,128]{3,2,1,0:T(8,128)(2,1)S(1)}, bf16[2,3,192,128]{3,2,1,0:T(8,128)(2,1)S(1)}, u32[]{:S(2)}, u32[]{:S(2)}) collective-permute-start(bf16[2,3,192,128]{3,2,1,0:T(8,128)(2,1)S(1)} %collective-permute-done.2.refs_1_), channel_id=1, source_target_pairs={{16,0},{17,1},{18,2},{19,3},{20,4},{21,5},{22,6},{23,7},{24,8},{25... | collective-permute-start | bytes 884744 | tf_op jit(solution)/shard_map/ppermute | solution.py:44
  45.2 21.4 %collective-permute-start.7 = (bf16[2,3,192,128]{3,2,1,0:T(8,128)(2,1)S(1)}, bf16[2,3,192,128]{3,2,1,0:T(8,128)(2,1)S(1)}, u32[]{:S(2)}, u32[]{:S(2)}) collective-permute-start(bf16[2,3,192,128]{3,2,1,0:T(8,128)(2,1)S(1)} %collective-permute-done.6.refs_2_.refs_0_), channel_id=1, source_target_pairs={{32,48},{33,49},{34,50},{35,51},{36,52},{37,53},{38,54},{39,55},{4... | collective-permute-start | bytes 884744 | tf_op jit(solution)/shard_map/ppermute | solution.py:44
  54.0 13.3 %collective-permute-start.9 = (bf16[2,3,192,128]{3,2,1,0:T(8,128)(2,1)S(1)}, bf16[2,3,192,128]{3,2,1,0:T(8,128)(2,1)S(1)}, u32[]{:S(2)}, u32[]{:S(2)}) collective-permute-start(bf16[2,3,192,128]{3,2,1,0:T(8,128)(2,1)S(1)} %collective-permute-done.8.refs_3_.refs_1_), channel_id=1, source_target_pairs={{16,0},{17,1},{18,2},{19,3},{20,4},{21,5},{22,6},{23,7},{24,8},{25... | collective-permute-start | bytes 884744 | tf_op jit(solution)/shard_map/ppermute | solution.py:44
  55.5 42.1 %copy-start.11 = (bf16[4,3,192,128]{3,2,1,0:T(8,128)(2,1)}, bf16[4,3,192,128]{3,2,1,0:T(8,128)(2,1)S(1)}, u32[]{:S(2)}) copy-start(bf16[4,3,192,128]{3,2,1,0:T(8,128)(2,1)S(1)} %get-tuple-element.15.refs_3_) | copy-start | bytes 1769476
  55.5 42.1 %collective-permute-start.13 = (bf16[4,3,192,128]{3,2,1,0:T(8,128)(2,1)S(1)}, bf16[4,3,192,128]{3,2,1,0:T(8,128)(2,1)S(1)}, u32[]{:S(2)}, u32[]{:S(2)}) collective-permute-start(bf16[4,3,192,128]{3,2,1,0:T(8,128)(2,1)S(1)} %get-tuple-element.15.refs_3_), channel_id=1, source_target_pairs={{0,128},{1,129},{2,130},{3,131},{4,132},{5,133},{6,134},{7,135},{8... | collective-permute-start | bytes 1769480 | tf_op jit(solution)/shard_map/ppermute | solution.py:44
  57.4 40.2 %collective-permute-start.14 = (bf16[4,3,192,128]{3,2,1,0:T(8,128)(2,1)S(1)}, bf16[4,3,192,128]{3,2,1,0:T(8,128)(2,1)S(1)}, u32[]{:S(2)}, u32[]{:S(2)}) collective-permute-start(bf16[4,3,192,128]{3,2,1,0:T(8,128)(2,1)S(1)} %get-tuple-element.16), channel_id=1, source_target_pairs={{0,384},{1,385},{2,386},{3,387},{4,388},{5,389},{6,390},{7,391},{8... | collective-permute-start | bytes 1769480 | tf_op jit(solution)/shard_map/ppermute | solution.py:44
  61.4 30.7 %collective-permute-start.5 = (bf16[512,384]{1,0:T(8,128)(2,1)}, bf16[512,384]{1,0:T(8,128)(2,1)S(1)}, u32[]{:S(2)}, u32[]{:S(2)}) collective-permute-start(bf16[512,384]{1,0:T(8,128)(2,1)} %bitcast.4), channel_id=1, source_target_pairs={{0,64},{1,65},{2,66},{3,67},{4,68},{5,69},{6,70},{7,71},{8,72},{9,... | collective-permute-start | bytes 1179656 | tf_op jit(solution)/shard_map/ppermute | solution.py:44
  66.6 27.4 %collective-permute-start.11 = (bf16[2,3,192,128]{3,2,1,0:T(8,128)(2,1)S(1)}, bf16[2,3,192,128]{3,2,1,0:T(8,128)(2,1)S(1)}, u32[]{:S(2)}, u32[]{:S(2)}) collective-permute-start(bf16[2,3,192,128]{3,2,1,0:T(8,128)(2,1)S(1)} %collective-permute-done.7.refs_1_.refs_2_.refs_3_), channel_id=1, source_target_pairs={{48,64},{49,65},{50,66},{51,67},{52,68},{53,69},{54,70},{55,71},{5... | collective-permute-start | bytes 884744 | tf_op jit(solution)/shard_map/ppermute | solution.py:44
  67.3 30.3 %collective-permute-start.12 = (bf16[2,3,192,128]{3,2,1,0:T(8,128)(2,1)S(1)}, bf16[2,3,192,128]{3,2,1,0:T(8,128)(2,1)S(1)}, u32[]{:S(2)}, u32[]{:S(2)}) collective-permute-start(bf16[2,3,192,128]{3,2,1,0:T(8,128)(2,1)S(1)} %collective-permute-done.9.refs_2_.refs_3_.refs_4_), channel_id=1, source_target_pairs={{16,0},{17,1},{18,2},{19,3},{20,4},{21,5},{22,6},{23,7},{24,8},{25... | collective-permute-start | bytes 884744 | tf_op jit(solution)/shard_map/ppermute | solution.py:44
  92.1 20.2 %collective-permute-start.10 = (bf16[512,384]{1,0:T(8,128)(2,1)S(1)}, bf16[512,384]{1,0:T(8,128)(2,1)S(1)}, u32[]{:S(2)}, u32[]{:S(2)}) collective-permute-start(bf16[512,384]{1,0:T(8,128)(2,1)S(1)} %shard_map.74), channel_id=1, source_target_pairs={{0,64},{1,65},{2,66},{3,67},{4,68},{5,69},{6,70},{7,71},{8,72},{9,... | collective-permute-start | bytes 1179656 | tf_op jit(solution)/shard_map/ppermute | solution.py:44
  97.6 20.2 %collective-permute-start.15 = (bf16[2,3,192,128]{3,2,1,0:T(8,128)(2,1)S(1)}, bf16[2,3,192,128]{3,2,1,0:T(8,128)(2,1)S(1)}, u32[]{:S(2)}, u32[]{:S(2)}) collective-permute-start(bf16[2,3,192,128]{3,2,1,0:T(8,128)(2,1)S(1)} %shard_map.76.refs_4_.refs_0_), channel_id=1, source_target_pairs={{16,0},{17,1},{18,2},{19,3},{20,4},{21,5},{22,6},{23,7},{24,8},{25... | collective-permute-start | bytes 884744 | tf_op jit(solution)/shard_map/ppermute | solution.py:44
  100.0 0.9 copy-start.17
  119.7 10.5 %collective-permute-start.18 = (bf16[2,3,192,128]{3,2,1,0:T(8,128)(2,1)S(1)}, bf16[2,3,192,128]{3,2,1,0:T(8,128)(2,1)S(1)}, u32[]{:S(2)}, u32[]{:S(2)}) collective-permute-start(bf16[2,3,192,128]{3,2,1,0:T(8,128)(2,1)S(1)} %collective-permute-done.15.refs_1_), channel_id=1, source_target_pairs={{16,0},{17,1},{18,2},{19,3},{20,4},{21,5},{22,6},{23,7},{24,8},{25... | collective-permute-start | bytes 884744 | tf_op jit(solution)/shard_map/ppermute | solution.py:44
  121.0 21.6 %collective-permute-start.16 = (bf16[5,3,192,128]{3,2,1,0:T(8,128)(2,1)}, bf16[5,3,192,128]{3,2,1,0:T(8,128)(2,1)}, u32[]{:S(2)}, u32[]{:S(2)}) collective-permute-start(bf16[5,3,192,128]{3,2,1,0:T(8,128)(2,1)} %get-tuple-element.17.refs_2_.refs_6_), channel_id=1, source_target_pairs={{0,128},{1,129},{2,130},{3,131},{4,132},{5,133},{6,134},{7,135},{8... | collective-permute-start | bytes 2211848 | tf_op jit(solution)/shard_map/ppermute | solution.py:44
  124.5 22.8 %collective-permute-start.17 = (bf16[5,3,192,128]{3,2,1,0:T(8,128)(2,1)}, bf16[5,3,192,128]{3,2,1,0:T(8,128)(2,1)}, u32[]{:S(2)}, u32[]{:S(2)}) collective-permute-start(bf16[5,3,192,128]{3,2,1,0:T(8,128)(2,1)} %copy-done.17), channel_id=1, source_target_pairs={{0,384},{1,385},{2,386},{3,387},{4,388},{5,389},{6,390},{7,391},{8... | collective-permute-start | bytes 2211848 | tf_op jit(solution)/shard_map/ppermute | solution.py:44
  130.2 0.7 copy-start.6
  130.9 1.0 copy-start.7
  133.3 36.5 %collective-permute-start.19 = (bf16[6,3,192,128]{3,2,1,0:T(8,128)(2,1)}, bf16[6,3,192,128]{3,2,1,0:T(8,128)(2,1)S(1)}, u32[]{:S(2)}, u32[]{:S(2)}) collective-permute-start(bf16[6,3,192,128]{3,2,1,0:T(8,128)(2,1)} %get-tuple-element.19.refs_9_), channel_id=1, source_target_pairs={{0,128},{1,129},{2,130},{3,131},{4,132},{5,133},{6,134},{7,135},{8... | collective-permute-start | bytes 2654216 | tf_op jit(solution)/shard_map/ppermute | solution.py:44
  136.7 33.1 %collective-permute-start.20 = (bf16[6,3,192,128]{3,2,1,0:T(8,128)(2,1)}, bf16[6,3,192,128]{3,2,1,0:T(8,128)(2,1)S(1)}, u32[]{:S(2)}, u32[]{:S(2)}) collective-permute-start(bf16[6,3,192,128]{3,2,1,0:T(8,128)(2,1)} %get-tuple-element.20), channel_id=1, source_target_pairs={{0,384},{1,385},{2,386},{3,387},{4,388},{5,389},{6,390},{7,391},{8... | collective-permute-start | bytes 2654216 | tf_op jit(solution)/shard_map/ppermute | solution.py:44
  139.2 9.4 %collective-permute-start.21 = (bf16[2,3,192,128]{3,2,1,0:T(8,128)(2,1)}, bf16[2,3,192,128]{3,2,1,0:T(8,128)(2,1)}, u32[]{:S(2)}, u32[]{:S(2)}) collective-permute-start(bf16[2,3,192,128]{3,2,1,0:T(8,128)(2,1)} %copy-done.6), channel_id=1, source_target_pairs={{16,0},{17,1},{18,2},{19,3},{20,4},{21,5},{22,6},{23,7},{24,8},{25... | collective-permute-start | bytes 884744 | tf_op jit(solution)/shard_map/ppermute | solution.py:44
  148.6 1.0 copy-start.8
  152.2 24.6 %collective-permute-start.22 = (bf16[4,3,192,128]{3,2,1,0:T(8,128)(2,1)}, bf16[4,3,192,128]{3,2,1,0:T(8,128)(2,1)}, u32[]{:S(2)}, u32[]{:S(2)}) collective-permute-start(bf16[4,3,192,128]{3,2,1,0:T(8,128)(2,1)} %get-tuple-element.21.refs_0_), channel_id=1, source_target_pairs={{0,128},{1,129},{2,130},{3,131},{4,132},{5,133},{6,134},{7,135},{8... | collective-permute-start | bytes 1769480 | tf_op jit(solution)/shard_map/ppermute | solution.py:44
  156.8 20.4 %collective-permute-start.23 = (bf16[4,3,192,128]{3,2,1,0:T(8,128)(2,1)}, bf16[4,3,192,128]{3,2,1,0:T(8,128)(2,1)}, u32[]{:S(2)}, u32[]{:S(2)}) collective-permute-start(bf16[4,3,192,128]{3,2,1,0:T(8,128)(2,1)} %get-tuple-element.22), channel_id=1, source_target_pairs={{0,384},{1,385},{2,386},{3,387},{4,388},{5,389},{6,390},{7,391},{8... | collective-permute-start | bytes 1769480 | tf_op jit(solution)/shard_map/ppermute | solution.py:44
  159.6 1.9 copy-start
  161.5 1.9 copy-start.1
  163.4 6.5 %copy-start.3 = (bf16[2,3,192,128]{3,2,1,0:T(8,128)(2,1)S(1)}, bf16[2,3,192,128]{3,2,1,0:T(8,128)(2,1)}, u32[]{:S(2)}) copy-start(bf16[2,3,192,128]{3,2,1,0:T(8,128)(2,1)} %copy-done.2) | copy-start | bytes 884740
  163.4 6.5 %copy-start.5 = (bf16[2,3,192,128]{3,2,1,0:T(8,128)(2,1)S(1)}, bf16[2,3,192,128]{3,2,1,0:T(8,128)(2,1)}, u32[]{:S(2)}) copy-start(bf16[2,3,192,128]{3,2,1,0:T(8,128)(2,1)} %copy-done.4) | copy-start | bytes 884740
  163.4 6.5 %copy-start.10 = (bf16[2,3,192,128]{3,2,1,0:T(8,128)(2,1)S(1)}, bf16[2,3,192,128]{3,2,1,0:T(8,128)(2,1)}, u32[]{:S(2)}) copy-start(bf16[2,3,192,128]{3,2,1,0:T(8,128)(2,1)} %copy-done.9) | copy-start | bytes 884740
  163.4 6.5 %copy-start.12 = (bf16[4,3,192,128]{3,2,1,0:T(8,128)(2,1)S(1)}, bf16[4,3,192,128]{3,2,1,0:T(8,128)(2,1)}, u32[]{:S(2)}) copy-start(bf16[4,3,192,128]{3,2,1,0:T(8,128)(2,1)} %copy-done.11) | copy-start | bytes 1769476
  178.6 12.4 %collective-permute-start.24 = (bf16[3,3,192,128]{3,2,1,0:T(8,128)(2,1)S(1)}, bf16[3,3,192,128]{3,2,1,0:T(8,128)(2,1)S(1)}, u32[]{:S(2)}, u32[]{:S(2)}) collective-permute-start(bf16[3,3,192,128]{3,2,1,0:T(8,128)(2,1)S(1)} %get-tuple-element.23), channel_id=1, source_target_pairs={{0,128},{1,129},{2,130},{3,131},{4,132},{5,133},{6,134},{7,135},{8... | collective-permute-start | bytes 1327112 | tf_op jit(solution)/shard_map/ppermute | solution.py:44
  183.3 11.7 %copy-start.14 = (f32[2,256]{1,0:T(2,128)S(1)}, f32[2,256]{1,0:T(2,128)}, u32[]{:S(2)}) copy-start(f32[2,256]{1,0:T(2,128)} %gain_ref.1) | copy-start | bytes 6148
  183.3 11.7 %collective-permute-start.25 = (bf16[3,3,192,128]{3,2,1,0:T(8,128)(2,1)S(1)}, bf16[3,3,192,128]{3,2,1,0:T(8,128)(2,1)S(1)}, u32[]{:S(2)}, u32[]{:S(2)}) collective-permute-start(bf16[3,3,192,128]{3,2,1,0:T(8,128)(2,1)S(1)} %get-tuple-element.24), channel_id=1, source_target_pairs={{0,384},{1,385},{2,386},{3,387},{4,388},{5,389},{6,390},{7,391},{8... | collective-permute-start | bytes 1327112 | tf_op jit(solution)/shard_map/ppermute | solution.py:44
Sparse Core Ops, SparseCore 0:
  43.3 32.9 all-gather.3
  119.9 33.2 all-gather.5
